TPU v7x, 32 devices: a whole 2x2x4 slice. The times are simulated.
32 devices in a mesh: gx: 8 (over z, y), gy: 4 (over x, core).
Axes of the slice: x: 2, y: 2, z: 4, core: 2. Of those that a mesh axis runs over, the one named last changes fastest.
Arguments:
- tokens: bfloat16 [65536, 768], P(('gx', 'gy'))
- seg_lengths: int32 [128, 4], P(('gx', 'gy')), may hold values from 1 to 256, 512 in all within a row
- cotangent: bfloat16 [65536, 768], P(('gx', 'gy')), may hold values from -6 to 6
- w_qkv: float32 [3, 768, 768], P(None, ('gx', 'gy')), may hold values from -0.21875 to 0.21875
- w_out: float32 [768, 768], P(('gx', 'gy')), may hold values from -0.875 to 0.875
- w_up: float32 [768, 3072], P(('gx', 'gy')), may hold values from -0.21875 to 0.21875
- w_down: float32 [3072, 768], P(('gx', 'gy')), may hold values from -0.109375 to 0.109375
- vecs: float32 [8, 768], P(None, ('gx', 'gy'))
- b_up: float32 [3072], P(('gx', 'gy')), may hold values from -1.8 to 1.8
- first_qkv: float32 [3, 768, 768], P(None, ('gx', 'gy')), may hold values from -1536 to 1536
- first_out: float32 [768, 768], P(('gx', 'gy')), may hold values from -1536 to 1536
- first_up: float32 [768, 3072], P(('gx', 'gy')), may hold values from -1536 to 1536
- first_down: float32 [3072, 768], P(('gx', 'gy')), may hold values from -1536 to 1536
- first_vecs: float32 [8, 768], P(None, ('gx', 'gy')), may hold values from -1536 to 1536
- first_bup: float32 [3072], P(('gx', 'gy')), may hold values from -1536 to 1536
- second_qkv: float32 [3, 768, 768], P(None, ('gx', 'gy')), may hold values from 32768 to 262144
- second_out: float32 [768, 768], P(('gx', 'gy')), may hold values from 32768 to 262144
- second_up: float32 [768, 3072], P(('gx', 'gy')), may hold values from 32768 to 262144
- second_down: float32 [3072, 768], P(('gx', 'gy')), may hold values from 32768 to 262144
- second_vecs: float32 [8, 768], P(None, ('gx', 'gy')), may hold values from 32768 to 262144
- second_bup: float32 [3072], P(('gx', 'gy')), may hold values from 32768 to 262144
- ema_qkv: float32 [3, 768, 768], P(None, ('gx', 'gy')), may hold values from -0.21875 to 0.21875
- ema_out: float32 [768, 768], P(('gx', 'gy')), may hold values from -0.875 to 0.875
- ema_up: float32 [768, 3072], P(('gx', 'gy')), may hold values from -0.21875 to 0.21875
- ema_down: float32 [3072, 768], P(('gx', 'gy')), may hold values from -0.109375 to 0.109375
- ema_vecs: float32 [8, 768], P(None, ('gx', 'gy'))
- ema_bup: float32 [3072], P(('gx', 'gy')), may hold values from -1.8 to 1.8
Outputs:
- layer_out: bfloat16 [65536, 768], P(('gx', 'gy'))
- grad_tokens: bfloat16 [65536, 768], P(('gx', 'gy'))
- new_qkv: float32 [3, 768, 768], P(None, ('gx', 'gy'))
- new_out: float32 [768, 768], P(('gx', 'gy'))
- new_up: float32 [768, 3072], P(('gx', 'gy'))
- new_down: float32 [3072, 768], P(('gx', 'gy'))
- new_vecs: float32 [8, 768], P(None, ('gx', 'gy'))
- new_bup: float32 [3072], P(('gx', 'gy'))
- firsts_qkv: float32 [3, 768, 768], P(None, ('gx', 'gy'))
- firsts_out: float32 [768, 768], P(('gx', 'gy'))
- firsts_up: float32 [768, 3072], P(('gx', 'gy'))
- firsts_down: float32 [3072, 768], P(('gx', 'gy'))
- firsts_vecs: float32 [8, 768], P(None, ('gx', 'gy'))
- firsts_bup: float32 [3072], P(('gx', 'gy'))
- seconds_qkv: float32 [3, 768, 768], P(None, ('gx', 'gy'))
- seconds_out: float32 [768, 768], P(('gx', 'gy'))
- seconds_up: float32 [768, 3072], P(('gx', 'gy'))
- seconds_down: float32 [3072, 768], P(('gx', 'gy'))
- seconds_vecs: float32 [8, 768], P(None, ('gx', 'gy'))
- seconds_bup: float32 [3072], P(('gx', 'gy'))
- ema_new_qkv: float32 [3, 768, 768], P(None, ('gx', 'gy'))
- ema_new_out: float32 [768, 768], P(('gx', 'gy'))
- ema_new_up: float32 [768, 3072], P(('gx', 'gy'))
- ema_new_down: float32 [3072, 768], P(('gx', 'gy'))
- ema_new_vecs: float32 [8, 768], P(None, ('gx', 'gy'))
- ema_new_bup: float32 [3072], P(('gx', 'gy'))
- copy_qkv: bfloat16 [3, 768, 768], P(None, ('gx', 'gy'))
- copy_out: bfloat16 [768, 768], P(('gx', 'gy'))
- copy_up: bfloat16 [768, 3072], P(('gx', 'gy'))
- copy_down: bfloat16 [3072, 768], P(('gx', 'gy'))
- copy_vecs: bfloat16 [8, 768], P(None, ('gx', 'gy'))
- copy_bup: bfloat16 [3072], P(('gx', 'gy'))
- trust_ratios: float32 [15], replicated
- norm_pairs: float32 [2, 15], replicated
Inputs may be any that keep to these rules, and one draw needn't show every extreme that they name: `seg_lengths`: each row's 4 lengths are its pairs' token counts in order and sum to 512.
All inputs are finite; a program needn't handle non-finite values.
Results may differ from a plain program's by a relative error of at most 0.014.
The roundings to bfloat16 on the way count: a program that leaves them out, or rounds other values in their place, can miss the bound.
Values may be sent and summed in bfloat16 or wider, within the bound.
No kernel may reach another device: no remote copies, remote signals or barrier semaphores. Data moves between devices by JAX's collectives and lax.ppermute only.
A program may use at most 256 MiB of HBM per device.

v0:
```python
import jax
import jax.numpy as jnp
from jax import lax
from jax.sharding import PartitionSpec as P

HEADS = 12
HD = 64
STEP = 7


norm_eps = 1e-12
beta_one = 0.5
beta_two = 0.5
adam_eps = 1e-06
decay_rate = 0.01
learn_rate = 0.3
ema_rate = 0.5
ratio_eps = 1e-06


def layer_norm(values, gain_row, bias_row):
    center = values - jnp.mean(values, axis=-1, keepdims=True)
    spread = jnp.mean(center * center, axis=-1, keepdims=True)
    return center * lax.rsqrt(spread + norm_eps) * gain_row + bias_row


def gelu_exact(values):
    return jax.nn.gelu(values, approximate=False)


def segment_ids(seg_lengths, length):
    bounds = jnp.cumsum(seg_lengths, axis=1)
    places = jnp.arange(length, dtype=jnp.int32)
    return jnp.sum((places[None, :, None] >= bounds[:, None, :]).astype(jnp.int32), axis=2)


def gather_weights(shards):
    return (
        lax.all_gather(shards[0], ("gx", "gy"), axis=1, tiled=True),
        lax.all_gather(shards[1], ("gx", "gy"), axis=0, tiled=True),
        lax.all_gather(shards[2], ("gx", "gy"), axis=0, tiled=True),
        lax.all_gather(shards[3], ("gx", "gy"), axis=0, tiled=True),
        lax.all_gather(shards[4], ("gx", "gy"), axis=1, tiled=True),
        lax.all_gather(shards[5], ("gx", "gy"), axis=0, tiled=True),
    )


def reduce_grads(grads):
    return (
        lax.psum_scatter(grads[0], ("gx", "gy"), scatter_dimension=1, tiled=True),
        lax.psum_scatter(grads[1], ("gx", "gy"), scatter_dimension=0, tiled=True),
        lax.psum_scatter(grads[2], ("gx", "gy"), scatter_dimension=0, tiled=True),
        lax.psum_scatter(grads[3], ("gx", "gy"), scatter_dimension=0, tiled=True),
        lax.psum_scatter(grads[4], ("gx", "gy"), scatter_dimension=1, tiled=True),
        lax.psum_scatter(grads[5], ("gx", "gy"), scatter_dimension=0, tiled=True),
    )


def tensor_squares(tensors):
    return jnp.concatenate(
        [
            jnp.sum(tensors[0] * tensors[0], axis=(1, 2)),
            jnp.sum(tensors[1] * tensors[1])[None],
            jnp.sum(tensors[2] * tensors[2])[None],
            jnp.sum(tensors[3] * tensors[3])[None],
            jnp.sum(tensors[4] * tensors[4], axis=1),
            jnp.sum(tensors[5] * tensors[5])[None],
        ]
    )


def spread_ratios(ratios):
    return (
        ratios[0:3][:, None, None],
        ratios[3],
        ratios[4],
        ratios[5],
        ratios[6:14][:, None],
        ratios[14],
    )


def attend_forward(inputs):
    queries, keys_low, values_low, seg_row = inputs
    score_scale = HD ** (-0.5)
    same_seg = seg_row[:, None] == seg_row[None, :]
    raw_scores = (
        jnp.einsum("qhd,khd->hqk", queries, keys_low, preferred_element_type=jnp.float32)
        * score_scale
    )
    masked = jnp.where(same_seg[None], raw_scores, -1e30)
    row_peak = jnp.max(masked, axis=-1, keepdims=True)
    exponent = jnp.exp(masked - row_peak)
    row_total = jnp.sum(exponent, axis=-1, keepdims=True)
    attn_probs = exponent / row_total
    log_total = row_peak + jnp.log(row_total)
    mixed = jnp.einsum(
        "hqk,khd->qhd",
        attn_probs.astype(jnp.bfloat16),
        values_low,
        preferred_element_type=jnp.float32,
    )
    return (mixed.astype(jnp.bfloat16), log_total)


def attend_backward(inputs):
    queries, keys_low, values_low, seg_row, log_total, grad_mixed = inputs
    score_scale = HD ** (-0.5)
    same_seg = seg_row[:, None] == seg_row[None, :]
    again_scores = (
        jnp.einsum("qhd,khd->hqk", queries, keys_low, preferred_element_type=jnp.float32)
        * score_scale
    )
    again_masked = jnp.where(same_seg[None], again_scores, -1e30)
    again_probs = jnp.exp(again_masked - log_total)
    grad_value = jnp.einsum(
        "hqk,qhd->khd",
        again_probs.astype(jnp.bfloat16),
        grad_mixed,
        preferred_element_type=jnp.float32,
    )
    grad_probs = jnp.einsum(
        "qhd,khd->hqk", grad_mixed, values_low, preferred_element_type=jnp.float32
    )
    grad_scores = again_probs * (
        grad_probs - jnp.sum(grad_probs * again_probs, axis=-1, keepdims=True)
    )
    grad_scores = grad_scores.astype(jnp.bfloat16)
    grad_query = (
        jnp.einsum("hqk,khd->qhd", grad_scores, keys_low, preferred_element_type=jnp.float32)
        * score_scale
    )
    grad_key = (
        jnp.einsum("hqk,qhd->khd", grad_scores, queries, preferred_element_type=jnp.float32)
        * score_scale
    )
    return (
        grad_query.astype(jnp.bfloat16),
        grad_key.astype(jnp.bfloat16),
        grad_value.astype(jnp.bfloat16),
    )


def on_device(
    tokens,
    seg_lengths,
    cotangent,
    w_qkv,
    w_out,
    w_up,
    w_down,
    vecs,
    b_up,
    first_qkv,
    first_out,
    first_up,
    first_down,
    first_vecs,
    first_bup,
    second_qkv,
    second_out,
    second_up,
    second_down,
    second_vecs,
    second_bup,
    ema_qkv,
    ema_out,
    ema_up,
    ema_down,
    ema_vecs,
    ema_bup,
):
    f32 = jnp.float32
    bf16 = jnp.bfloat16
    row_count = seg_lengths.shape[0]
    tok_count = tokens.shape[0]
    length = tok_count // row_count
    model_width = tokens.shape[1]
    masters = (w_qkv, w_out, w_up, w_down, vecs, b_up)
    halves = tuple((master.astype(bf16) for master in masters))
    full_qkv, full_out, full_up, full_down, full_vecs, full_bup = gather_weights(halves)
    vec_rows = full_vecs.astype(f32)
    up_bias = full_bup.astype(f32)
    seg_ids = segment_ids(seg_lengths, length)
    bias_qkv = jnp.stack([vec_rows[0], jnp.zeros_like(vec_rows[0]), vec_rows[1]])
    projected = (
        jnp.einsum("td,sde->ste", tokens, full_qkv, preferred_element_type=f32)
        + bias_qkv[:, None, :]
    )
    qkv_low = projected.astype(bf16).reshape(3, row_count, length, HEADS, HD)
    queries, keys_low, values_low = (qkv_low[0], qkv_low[1], qkv_low[2])
    mixed, log_total = lax.map(attend_forward, (queries, keys_low, values_low, seg_ids))
    mixed = mixed.reshape(tok_count, model_width)
    attn_out = jnp.dot(mixed, full_out, preferred_element_type=f32) + vec_rows[2]
    resid_one = tokens.astype(f32) + attn_out
    hidden = layer_norm(resid_one, vec_rows[3], vec_rows[4])
    hidden_low = hidden.astype(bf16)
    pre_act = jnp.dot(hidden_low, full_up, preferred_element_type=f32) + up_bias
    active = gelu_exact(pre_act).astype(bf16)
    ffn_out = jnp.dot(active, full_down, preferred_element_type=f32) + vec_rows[5]
    resid_two = hidden + ffn_out
    layer_out = layer_norm(resid_two, vec_rows[6], vec_rows[7]).astype(bf16)
    back_qkv, back_out, back_up, back_down, back_vecs, back_bup = gather_weights(halves)
    grad_out = cotangent.astype(f32)
    unused_two, norm_two_vjp = jax.vjp(layer_norm, resid_two, vec_rows[6], vec_rows[7])
    grad_resid_two, grad_gain_two, grad_bias_two = norm_two_vjp(grad_out)
    grad_ffn = grad_resid_two.astype(bf16)
    grad_wdown = jnp.einsum("tf,td->fd", active, grad_ffn, preferred_element_type=f32)
    grad_bias_down = jnp.sum(grad_ffn.astype(f32), axis=0)
    grad_active = jnp.einsum("td,fd->tf", grad_ffn, back_down, preferred_element_type=f32)
    unused_act, gelu_vjp = jax.vjp(gelu_exact, pre_act)
    grad_inner = gelu_vjp(grad_active)[0].astype(bf16)
    grad_wup = jnp.einsum("td,tf->df", hidden_low, grad_inner, preferred_element_type=f32)
    grad_bias_up = jnp.sum(grad_inner.astype(f32), axis=0)
    grad_hidden = grad_resid_two + jnp.einsum(
        "tf,df->td", grad_inner, back_up, preferred_element_type=f32
    )
    unused_one, norm_one_vjp = jax.vjp(layer_norm, resid_one, vec_rows[3], vec_rows[4])
    grad_resid_one, grad_gain_one, grad_bias_one = norm_one_vjp(grad_hidden)
    grad_attn = grad_resid_one.astype(bf16)
    grad_wout = jnp.einsum("td,te->de", mixed, grad_attn, preferred_element_type=f32)
    grad_bias_out = jnp.sum(grad_attn.astype(f32), axis=0)
    grad_mixed = jnp.einsum("te,de->td", grad_attn, back_out, preferred_element_type=f32).astype(
        bf16
    )
    grad_mixed = grad_mixed.reshape(row_count, length, HEADS, HD)
    grad_query, grad_key, grad_value = lax.map(
        attend_backward, (queries, keys_low, values_low, seg_ids, log_total, grad_mixed)
    )
    grad_proj = jnp.stack([grad_query, grad_key, grad_value]).reshape(3, tok_count, model_width)
    grad_wqkv = jnp.einsum("td,ste->sde", tokens, grad_proj, preferred_element_type=f32)
    grad_input = grad_resid_one + jnp.einsum(
        "ste,sde->td", grad_proj, back_qkv, preferred_element_type=f32
    )
    grad_bias_query = jnp.sum(grad_proj[0].astype(f32), axis=0)
    grad_bias_value = jnp.sum(grad_proj[2].astype(f32), axis=0)
    grad_vecs = jnp.stack(
        [
            grad_bias_query,
            grad_bias_value,
            grad_bias_out,
            grad_gain_one,
            grad_bias_one,
            grad_bias_down,
            grad_gain_two,
            grad_bias_two,
        ]
    )
    reduced = reduce_grads((grad_wqkv, grad_wout, grad_wup, grad_wdown, grad_vecs, grad_bias_up))
    firsts_in = (first_qkv, first_out, first_up, first_down, first_vecs, first_bup)
    seconds_in = (second_qkv, second_out, second_up, second_down, second_vecs, second_bup)
    averages = (ema_qkv, ema_out, ema_up, ema_down, ema_vecs, ema_bup)
    corr_one = 1.0 - beta_one**STEP
    corr_two = 1.0 - beta_two**STEP
    firsts = []
    seconds = []
    updates = []
    for member in range(6):
        first_new = beta_one * firsts_in[member] + (1.0 - beta_one) * reduced[member]
        second_new = (
            beta_two * seconds_in[member] + (1.0 - beta_two) * reduced[member] * reduced[member]
        )
        update = (
            first_new / corr_one / (jnp.sqrt(second_new / corr_two) + adam_eps)
            + decay_rate * masters[member]
        )
        firsts.append(first_new)
        seconds.append(second_new)
        updates.append(update)
    sq_weight, sq_update = lax.psum(
        (tensor_squares(masters), tensor_squares(updates)), ("gx", "gy")
    )
    ratios = jnp.sqrt(sq_weight) / jnp.sqrt(sq_update + ratio_eps)
    scales = spread_ratios(ratios)
    renewed = [
        masters[member] - learn_rate * scales[member] * updates[member] for member in range(6)
    ]
    emas = [ema_rate * averages[member] + (1.0 - ema_rate) * renewed[member] for member in range(6)]
    norm_pairs = jnp.stack([jnp.sqrt(sq_weight), jnp.sqrt(sq_update)])
    return (
        layer_out,
        grad_input.astype(bf16),
        renewed[0],
        renewed[1],
        renewed[2],
        renewed[3],
        renewed[4],
        renewed[5],
        firsts[0],
        firsts[1],
        firsts[2],
        firsts[3],
        firsts[4],
        firsts[5],
        seconds[0],
        seconds[1],
        seconds[2],
        seconds[3],
        seconds[4],
        seconds[5],
        emas[0],
        emas[1],
        emas[2],
        emas[3],
        emas[4],
        emas[5],
        renewed[0].astype(bf16),
        renewed[1].astype(bf16),
        renewed[2].astype(bf16),
        renewed[3].astype(bf16),
        renewed[4].astype(bf16),
        renewed[5].astype(bf16),
        ratios,
        norm_pairs,
    )


def solution(mesh):
    in_specs = (
        P(("gx", "gy"), None),
        P(("gx", "gy"), None),
        P(("gx", "gy"), None),
        P(None, ("gx", "gy"), None),
        P(("gx", "gy"), None),
        P(("gx", "gy"), None),
        P(("gx", "gy"), None),
        P(None, ("gx", "gy")),
        P(("gx", "gy")),
        P(None, ("gx", "gy"), None),
        P(("gx", "gy"), None),
        P(("gx", "gy"), None),
        P(("gx", "gy"), None),
        P(None, ("gx", "gy")),
        P(("gx", "gy")),
        P(None, ("gx", "gy"), None),
        P(("gx", "gy"), None),
        P(("gx", "gy"), None),
        P(("gx", "gy"), None),
        P(None, ("gx", "gy")),
        P(("gx", "gy")),
        P(None, ("gx", "gy"), None),
        P(("gx", "gy"), None),
        P(("gx", "gy"), None),
        P(("gx", "gy"), None),
        P(None, ("gx", "gy")),
        P(("gx", "gy")),
    )
    out_specs = (
        P(("gx", "gy"), None),
        P(("gx", "gy"), None),
        P(None, ("gx", "gy"), None),
        P(("gx", "gy"), None),
        P(("gx", "gy"), None),
        P(("gx", "gy"), None),
        P(None, ("gx", "gy")),
        P(("gx", "gy")),
        P(None, ("gx", "gy"), None),
        P(("gx", "gy"), None),
        P(("gx", "gy"), None),
        P(("gx", "gy"), None),
        P(None, ("gx", "gy")),
        P(("gx", "gy")),
        P(None, ("gx", "gy"), None),
        P(("gx", "gy"), None),
        P(("gx", "gy"), None),
        P(("gx", "gy"), None),
        P(None, ("gx", "gy")),
        P(("gx", "gy")),
        P(None, ("gx", "gy"), None),
        P(("gx", "gy"), None),
        P(("gx", "gy"), None),
        P(("gx", "gy"), None),
        P(None, ("gx", "gy")),
        P(("gx", "gy")),
        P(None, ("gx", "gy"), None),
        P(("gx", "gy"), None),
        P(("gx", "gy"), None),
        P(("gx", "gy"), None),
        P(None, ("gx", "gy")),
        P(("gx", "gy")),
        P(),
        P(),
    )
    return jax.shard_map(
        on_device, mesh=mesh, in_specs=in_specs, out_specs=out_specs, check_vma=False
    )
```

profile of v0, /device:TPU:0, one launch (start us, length us, event | category | flops | bytes accessed | tf_op | source)
XLA Modules:
  0.0 1165.7 jit_solution(3272147129303991919)
XLA Ops:
  14.8 43.5 %all-gather = bf16[32,24,8]{1,2,0:T(8,128)(2,1)S(1)} all-gather(bf16[1,24,8]{1,2,0:T(8,128)(2,1)S(1)} %convert_bitcast_fusion), channel_id=1, replica_groups=mesh['gx'=8,'gy'=4] {'gx','gy'}, dimensions={0}, use_global_device_ids=true | all-gather | bytes 12672 | tf_op jit(solution)/shard_map/all_gather | solution.py:43
  60.3 4.7 copy.209
  65.8 37.0 %all-reduce = bf16[3072]{0:T(1024)(128)(2,1)S(1)} all-reduce(bf16[3072]{0:T(1024)(128)(2,1)S(1)} %dynamic-update-slice), channel_id=1, replica_groups=mesh['gx'=8,'gy'=4] {'gx','gy'}, use_global_device_ids=true, to_apply=%add | all-reduce | flops 3072 | bytes 12288
  106.4 11.4 fusion.63
  121.1 6.2 squeeze.42
  138.1 6.2 squeeze.44
  150.6 48.8 %while.26 = (s32[]{:T(128)}, bf16[4,512,12,64]{1,3,2,0:T(8,128)(2,1)}, f32[4,12,512,1]{2,1,3,0:T(8,128)}, bf16[4,512,12,64]{1,3,2,0:T(8,128)(2,1)}, s32[4,512]{1...) while((s32[]{:T(128)}, ...), condition=%wide.region_5.6_spmd, body=%wide.region_2.5_spmd.sunk | while | flops 843704320 | bytes 42156632 | solution.py:192
  157.4 5.5 fusion.153
  169.5 5.5 fusion.153
  181.6 5.5 fusion.153
  193.7 5.5 fusion.153
  199.4 5.5 copy.215
  207.6 6.6 fusion.108
  218.0 70.2 %multiply_convert_fusion.3 = (bf16[2048,3072]{1,0:T(8,128)(2,1)}, f32[2048,3072]{1,0:T(8,128)}, f32[2048,3072]{1,0:T(8,128)}) fusion(f32[3072]{0:T(1024)S(1)} %copy-done.48, bf16[768,3072]{1,0:T(8,128)(2,1)} %all-gather.10.cloned.1.call-done, bf16[2048,768]{0,1:T(8,128)(2,1)S(1)} %fusion.90.clone.4), kind=kOutput, calls=%fused_computation.68 | convolution fusion | flops 10078912512 | bytes 70791168 | tf_op jit(solution)/shard_map/dot_general | solution.py:198
  288.3 18.0 %fusion.109 = (f32[2048]{0:T(1024)S(1)}, f32[2048,768]{0,1:T(8,128)}) fusion(f32[768]{0:T(1024)S(1)} %copy-done.50, bf16[2048,3072]{1,0:T(8,128)(2,1)} %get-tuple-element.480, bf16[3072,768]{1,0:T(8,128)(2,1)} %all-gather.12.cloned.1.call-done, f32[768]{0:T(1024)S(1)} %copy-done.38, f32[768]{0:T(1024)S(1)} %copy-done.32, f32[2048]{0:T(1024)S(1)} %copy-done.27, ...), kind=kOutput, calls=%fused_computation.208 | convolution fusion | flops 9674684416 | bytes 29918208 | tf_op jit(solution)/shard_map/dot_general | solution.py:200
  306.4 5.3 fusion.66
  315.8 5.7 convert_reduce_fusion.2
  321.5 33.7 %convert_reduce_fusion = (f32[3072]{0:T(1024)}, bf16[2048,3072]{1,0:T(8,128)(2,1)}) fusion(f32[2048,3072]{1,0:T(8,128)} %get-tuple-element.481, bf16[2048,768]{0,1:T(8,128)(2,1)} %get-tuple-element.467, bf16[3072,768]{1,0:T(8,128)(2,1)} %all-gather.12.cloned.1.call-done, f32[2048,3072]{1,0:T(8,128)} %get-tuple-element.505, f32[3072]{0:T(1024)S(1)} %copy-done.48), kind=kOutput, calls=%fused_computation.66 | convolution fusion | flops 9770628096 | bytes 70803456 | tf_op jit(solution)/shard_map/td,fd->tf/dot_general | solution.py:210
  355.2 20.7 %multiply_reduce_fusion.1 = (f32[768]{0:T(1024)}, f32[2048]{0:T(1024)S(1)}, f32[768]{0:T(1024)}, f32[2048,768]{0,1:T(8,128)S(1)}) fusion(f32[2048,768]{0,1:T(8,128)} %copy-done.2, f32[2048]{0:T(1024)S(1)} %copy-done.27, f32[2048]{0:T(1024)S(1)} %copy-done.20, f32[768]{0:T(1024)S(1)} %copy-done.32, bf16[2048,3072]{1,0:T(8,128)(2,1)} %get-tuple-element.510, ...), kind=kOutput, calls=%fused_computation.97 | convolution fusion | flops 9690411008 | bytes 39391232 | tf_op jit(solution)/shard_map/tf,df->td/dot_general | solution.py:215
  388.3 5.3 convolution_convert_fusion
  411.6 132.2 %while.27 = (s32[]{:T(128)}, bf16[4,512,12,64]{1,3,2,0:T(8,128)(2,1)}, bf16[4,512,12,64]{1,3,2,0:T(8,128)(2,1)}, bf16[4,512,12,64]{1,3,2,0:T(8,128)(2,1)}, bf16[...) while((s32[]{:T(128)}, ...), condition=%wide.region_16.17_spmd, body=%wide.region_14.16_spmd.sunk | while | flops 2062673920 | bytes 103468144 | solution.py:227
  416.3 10.1 multiply_reduce_fusion.18
  426.5 7.1 multiply_convert_fusion.5
  439.7 5.1 fusion.165
  449.4 10.1 multiply_reduce_fusion.18
  459.6 7.1 multiply_convert_fusion.5
  472.7 5.1 fusion.165
  482.4 10.1 multiply_reduce_fusion.18
  492.6 7.0 multiply_convert_fusion.5
  505.7 5.1 fusion.165
  515.4 10.1 multiply_reduce_fusion.18
  525.5 7.0 multiply_convert_fusion.5
  538.6 5.1 fusion.165
  543.8 6.1 copy.223
  549.9 6.3 stack.44
  564.9 6.3 stack.45
  580.0 4.7 stack.46
  587.5 14.1 %fusion.74 = f32[3,768,768]{1,2,0:T(8,128)} fusion(bf16[2048,768]{1,0:T(8,128)(2,1)} %param.31, bf16[1,2048,768]{2,1,0:T(8,128)(2,1)} %copy.228, bf16[1,2048,768]{2,1,0:T(8,128)(2,1)} %copy.227, bf16[1,2048,768]{2,1,0:T(8,128)(2,1)} %copy.226), kind=kOutput, calls=%fused_computation.117 | convolution fusion | flops 7257194496 | bytes 19660800 | tf_op jit(solution)/shard_map/td,ste->sde/dot_general | solution.py:231
  601.6 11.0 copy.231
  614.5 15.3 %fusion.111 = f32[3072,768]{1,0:T(8,128)} fusion(bf16[2048,3072]{1,0:T(8,128)(2,1)} %get-tuple-element.480, bf16[2048,768]{0,1:T(8,128)(2,1)S(1)} %copy-done.12), kind=kOutput, calls=%fused_computation.210 | convolution fusion | flops 9663676416 | bytes 25165824 | tf_op jit(solution)/shard_map/tf,td->fd/dot_general | solution.py:208
  630.6 17.4 %fusion.87 = f32[768,3072]{1,0:T(8,128)} fusion(bf16[2048,3072]{1,0:T(8,128)(2,1)} %get-tuple-element.510, f32[2048,768]{0,1:T(8,128)} %copy-done.2, f32[768]{0:T(1024)S(1)} %copy-done.39, f32[768]{0:T(1024)S(1)} %copy-done.33, f32[2048]{0:T(1024)S(1)} %copy-done.28, f32[2048]{0:T(1024)S(1)} %copy-done.21), kind=kOutput, calls=%fused_computation.195 | convolution fusion | flops 9671540736 | bytes 28334080 | tf_op jit(solution)/shard_map/td,tf->df/dot_general | solution.py:213
  655.8 14.1 %fusion.68 = bf16[2048,768]{0,1:T(8,128)(2,1)} fusion(f32[2048,768]{0,1:T(8,128)} %copy-done.7, f32[2048]{0:T(1024)S(1)} %copy-done.35, bf16[3,768,768]{2,1,0:T(8,128)(2,1)} %all-gather.6.cloned.1.call-done, bf16[1,2048,768]{2,1,0:T(8,128)(2,1)} %copy.228, bf16[1,2048,768]{2,1,0:T(8,128)(2,1)} %copy.227, bf16[1,2048,768]{2,1,0:T(8,128)(2,1)} %copy.226), kind=kOutput, calls=%fused_computation.95 | convolution fusion | flops 7261913088 | bytes 22421504 | tf_op jit(solution)/shard_map/ste,sde->td/dot_general | solution.py:232
  669.9 4.9 copy.235
  675.7 43.0 %all-reduce.5 = (f32[8,768]{1,0:T(8,128)}, f32[3072]{0:T(1024)}) all-reduce(f32[8,768]{1,0:T(8,128)S(1)} %stack.52, f32[3072]{0:T(1024)} %get-tuple-element.509), channel_id=6, replica_groups=mesh['gx'=8,'gy'=4] {'gx','gy'}, use_global_device_ids=true, to_apply=%region_40.41.clone | all-reduce | flops 9216 | bytes 73728
  723.8 80.4 %all-reduce.8.cloned.1.call-done = f32[3,768,768]{2,0,1:T(4,128)} async-done(((f32[3,768,768]{2,0,1:T(4,128)}), f32[3,768,768]{2,0,1:T(4,128)}) %all-reduce.8.cloned.1.call-update) | async-done | bytes 7077904
  807.3 138.4 %reduce-scatter.9.cloned.1.call-done = f32[96,768]{1,0:T(8,128)} async-done(((f32[3072,768]{1,0:T(8,128)}), f32[96,768]{1,0:T(8,128)}) %reduce-scatter.9.cloned.1.call-update) | async-done | bytes 294928 | tf_op jit(solution)/shard_map/reduce_scatter | solution.py:53
  948.5 138.7 %reduce-scatter.7.cloned.1.call-done = f32[24,3072]{1,0:T(8,128)} async-done(((f32[768,3072]{1,0:T(8,128)}), f32[24,3072]{1,0:T(8,128)}) %reduce-scatter.7.cloned.1.call-update) | async-done | bytes 294928 | tf_op jit(solution)/shard_map/reduce_scatter | solution.py:52
  1098.6 39.5 %all-reduce.4 = (f32[15]{0:T(128)S(1)}, f32[15]{0:T(128)S(1)}) all-reduce(f32[15]{0:T(128)S(1)} %concatenate.8, f32[15]{0:T(128)S(1)} %copy-done.57), channel_id=1, replica_groups=mesh['gx'=8,'gy'=4] {'gx','gy'}, use_global_device_ids=true, to_apply=%region_45.46 | all-reduce | flops 30 | bytes 240 | tf_op jit(solution)/shard_map/psum | solution.py:270
  (268 shorter events, 216.3 us)
Async XLA Ops:
  7.2 57.8 %copy-start.54 = (f32[96]{0:T(128)S(1)}, f32[96]{0:T(128)}, u32[]{:S(2)}) copy-start(f32[96]{0:T(128)} %param.39) | copy-start | bytes 1156
  7.2 96.2 %copy-start.10 = (bf16[2048,768]{1,0:T(8,128)(2,1)S(1)}, bf16[2048,768]{1,0:T(8,128)(2,1)}, u32[]{:S(2)}) copy-start(bf16[2048,768]{1,0:T(8,128)(2,1)} %param.33) | copy-start | bytes 9437188
  7.2 99.2 %all-gather.6.cloned.1.call-start = ((), (), s32[]{:S(2)}) async-start(), calls=%async_computation.3 | async-start | bytes 3649536 | tf_op jit(solution)/shard_map/all_gather | solution.py:39
  9.1 198.5 %all-gather.8.cloned.1.call-start = ((), (), s32[]{:S(2)}) async-start(), calls=%async_computation.4 | async-start | bytes 1216512 | tf_op jit(solution)/shard_map/all_gather | solution.py:40
  10.6 207.3 %all-gather.10.cloned.1.call-start = ((), (), s32[]{:S(2)}) async-start(), calls=%async_computation.5 | async-start | bytes 4866048 | tf_op jit(solution)/shard_map/all_gather | solution.py:41
  12.3 275.9 %all-gather.12.cloned.1.call-start = ((), (), s32[]{:S(2)}) async-start(), calls=%async_computation.6 | async-start | bytes 4866048 | tf_op jit(solution)/shard_map/all_gather | solution.py:42
  14.1 707.5 %reduce-scatter.5.cloned.1.call-start = ((), (), s32[]{:S(2)}) async-start(), calls=%async_computation.7 | async-start | bytes 2433024 | tf_op jit(solution)/shard_map/reduce_scatter | solution.py:51
  199.4 8.2 copy-start
  199.4 8.2 copy-start.22
  199.4 8.2 copy-start.51
  218.0 70.3 %copy-start.20 = (f32[2048]{0:T(1024)S(1)}, f32[2048]{0:T(1024)}, u32[]{:S(2)}) copy-start(f32[2048]{0:T(1024)} %copy-done.19) | copy-start | bytes 24580
  218.0 70.3 %copy-start.27 = (f32[2048]{0:T(1024)S(1)}, f32[2048]{0:T(1024)}, u32[]{:S(2)}) copy-start(f32[2048]{0:T(1024)} %copy-done.26) | copy-start | bytes 24580
  218.0 70.3 %copy-start.32 = (f32[768]{0:T(1024)S(1)}, f32[768]{0:T(1024)}, u32[]{:S(2)}) copy-start(f32[768]{0:T(1024)} %get-tuple-element.406) | copy-start | bytes 9220
  218.0 70.3 %copy-start.38 = (f32[768]{0:T(1024)S(1)}, f32[768]{0:T(1024)}, u32[]{:S(2)}) copy-start(f32[768]{0:T(1024)} %get-tuple-element.405) | copy-start | bytes 9220
  218.0 70.3 %copy-start.50 = (f32[768]{0:T(1024)S(1)}, f32[768]{0:T(1024)}, u32[]{:S(2)}) copy-start(f32[768]{0:T(1024)} %get-tuple-element.404) | copy-start | bytes 9220
  288.3 18.1 %copy-start.4 = (bf16[2048,768]{0,1:T(8,128)(2,1)S(1)}, bf16[2048,768]{0,1:T(8,128)(2,1)}, u32[]{:S(2)}) copy-start(bf16[2048,768]{0,1:T(8,128)(2,1)} %copy.216) | copy-start | bytes 9437188
  288.3 18.1 %copy-start.29 = (f32[768]{0:T(1024)S(1)}, f32[768]{0:T(1024)}, u32[]{:S(2)}) copy-start(f32[768]{0:T(1024)} %get-tuple-element.402) | copy-start | bytes 9220
  306.4 5.3 copy-start.3
  355.2 20.7 %copy-start.24 = (f32[2048]{0:T(1024)S(1)}, f32[2048]{0:T(1024)}, u32[]{:S(2)}) copy-start(f32[2048]{0:T(1024)} %copy-done.23) | copy-start | bytes 24580
  379.8 4.4 copy-start.11
  405.5 6.1 copy-start.1
  405.5 398.7 %all-reduce.8.cloned.1.call-start = ((), (), s32[]{:S(2)}) async-start(), calls=%async_computation.10 | async-start | bytes 18874368
  549.9 10.9 copy-start.8
  564.9 11.0 copy-start.6
  612.6 333.0 %reduce-scatter.9.cloned.1.call-start = ((), (), s32[]{:S(2)}) async-start(), calls=%async_computation.9 | async-start | bytes 9732096 | tf_op jit(solution)/shard_map/reduce_scatter | solution.py:53
  629.9 457.3 %reduce-scatter.7.cloned.1.call-start = ((), (), s32[]{:S(2)}) async-start(), calls=%async_computation.8 | async-start | bytes 9732096 | tf_op jit(solution)/shard_map/reduce_scatter | solution.py:52
  648.0 6.0 copy-start.36
  648.0 6.0 copy-start.53
  648.0 6.0 copy-start.52
  648.0 6.1 copy-start.46
  648.0 6.6 copy-start.41
  648.0 7.2 copy-start.40
  648.0 7.8 copy-start.35
  669.9 50.6 %copy-start.30 = (f32[8,24]{1,0:T(8,128)S(1)}, f32[8,24]{1,0:T(8,128)}, u32[]{:S(2)}) copy-start(f32[8,24]{1,0:T(8,128)} %param.38) | copy-start | bytes 2308
  669.9 51.6 %copy-start.17 = (f32[24,768]{1,0:T(8,128)S(1)}, f32[24,768]{1,0:T(8,128)}, u32[]{:S(2)}) copy-start(f32[24,768]{1,0:T(8,128)} %param.35) | copy-start | bytes 221188
  669.9 275.8 %copy-start.13 = (f32[96,768]{1,0:T(8,128)S(1)}, f32[96,768]{1,0:T(8,128)}, u32[]{:S(2)}) copy-start(f32[96,768]{1,0:T(8,128)} %param.37) | copy-start | bytes 884740
  669.9 425.9 %copy-start.9 = (bf16[2048,768]{0,1:T(8,128)(2,1)S(1)}, bf16[2048,768]{0,1:T(8,128)(2,1)}, u32[]{:S(2)}) copy-start(bf16[2048,768]{0,1:T(8,128)(2,1)} %get-tuple-element.489) | copy-start | bytes 9437188
  721.5 424.3 %copy-start.42 = (f32[8,24]{1,0:T(8,128)}, f32[8,24]{1,0:T(8,128)S(1)}, u32[]{:S(2)}) copy-start(f32[8,24]{1,0:T(8,128)S(1)} %get-tuple-element.464) | copy-start | bytes 2308
  721.5 424.2 %copy-start.43 = (f32[8,24]{1,0:T(8,128)}, f32[8,24]{1,0:T(8,128)S(1)}, u32[]{:S(2)}) copy-start(f32[8,24]{1,0:T(8,128)S(1)} %get-tuple-element.465) | copy-start | bytes 2308
  807.3 339.1 %copy-start.49 = (f32[8,24]{1,0:T(8,128)S(1)}, f32[8,24]{1,0:T(8,128)}, u32[]{:S(2)}) copy-start(f32[8,24]{1,0:T(8,128)} %param.56) | copy-start | bytes 2308
  807.3 339.7 %copy-start.55 = (f32[96]{0:T(128)S(1)}, f32[96]{0:T(128)}, u32[]{:S(2)}) copy-start(f32[96]{0:T(128)} %param.39) | copy-start | bytes 1156
  1093.2 5.5 copy-start.57
  1098.6 59.1 %copy-start.25 = (f32[24,768]{1,0:T(8,128)S(1)}, f32[24,768]{1,0:T(8,128)}, u32[]{:S(2)}) copy-start(f32[24,768]{1,0:T(8,128)} %param.53) | copy-start | bytes 221188
  1138.2 20.2 %copy-start.47 = (f32[15]{0:T(128)}, f32[15]{0:T(128)S(1)}, u32[]{:S(2)}) copy-start(f32[15]{0:T(128)S(1)} %get-tuple-element.495) | copy-start | bytes 184
  1143.9 14.5 %copy-start.14 = (f32[96,768]{1,0:T(8,128)}, f32[96,768]{1,0:T(8,128)S(1)}, u32[]{:S(2)}) copy-start(f32[96,768]{1,0:T(8,128)S(1)} %get-tuple-element.453) | copy-start | bytes 884740
  1146.4 12.0 %copy-start.44 = (f32[8,24]{1,0:T(8,128)}, f32[8,24]{1,0:T(8,128)S(1)}, u32[]{:S(2)}) copy-start(f32[8,24]{1,0:T(8,128)S(1)} %get-tuple-element.451) | copy-start | bytes 2308
  1147.5 10.9 copy-start.56
  1150.6 7.8 copy-start.15
  (18 other events, 39.7 us)
Sparse Core Ops, SparseCore 0:
  11.6 62.7 all-gather.5
  77.8 52.9 all-gather.7
  134.3 62.5 all-gather.9
  200.2 62.4 all-gather.11
  405.6 99.4 reduce-scatter.4
  612.8 191.3 all-reduce.7
  810.1 135.5 reduce-scatter.8
  952.6 134.4 reduce-scatter.6
where the time goes:
time: 1180 us; the launch traced here: 1170 us
  matrix products  363 us (31%)
  waiting for transfers between devices  358 us (30%)
  blocking collectives  163 us (14%)
  local copies, waits for them, and re-layouts  157 us (13%)
  other arithmetic  107 us (9%)
  between operations  17.9 us (2%)
    reduce_scatter x1, waiting for transfers between devices, reduce_grads(): lax.psum_scatter(grads[2], ('gx', 'gy'), scatter_dimension=0, tiled=True)  139 us
    reduce_scatter x1, waiting for transfers between devices, reduce_grads(): lax.psum_scatter(grads[3], ('gx', 'gy'), scatter_dimension=0, tiled=True)  138 us
    unnamed x9, waiting for transfers between devices  80.5 us
    unnamed x2, blocking collectives  80 us
    dot_general x1, matrix products, on_device(): pre_act = jnp.dot(hidden_low, full_up, preferred_element_type=f32) + up_bias  70.2 us
    all_gather x1, blocking collectives, gather_weights(): lax.all_gather(shards[4], ('gx', 'gy'), axis=1, tiled=True)  43.5 us
    dot_general x4, matrix products, attend_backward(): jnp.einsum('qhd,khd->hqk', grad_mixed, values_low, preferred_element_type...  40.5 us
    psum x1, blocking collectives, on_device(): lax.psum((tensor_squares(masters), tensor_squares(updates)), ('gx', 'gy'))  39.5 us
  transfers between devices with their start and end apart: 8, of which 3 were waited for; matrix products, arithmetic and copies ran while one was open for 40% of the time, Pallas kernels for 0%

commit v1 on v0

v1 whole, which is shorter than its diff:
```python
import functools

import jax
import jax.numpy as jnp
from jax import lax
from jax.experimental import pallas as pl
from jax.experimental.pallas import tpu as pltpu
from jax.sharding import PartitionSpec as P

STEP = 7
ALL = ("gx", "gy")
norm_eps = 1e-12
beta_one = 0.5
beta_two = 0.5
adam_eps = 1e-06
decay_rate = 0.01
learn_rate = 0.3
ema_rate = 0.5
ratio_eps = 1e-06

HEADS = 12
HD = 64
PAIR = 2 * HD
MASKED = -1e30
CHIPS = 16
MIB = 1 << 20
f32 = jnp.float32
bf16 = jnp.bfloat16
NT = (((1,), (1,)), ((), ()))
NN = (((1,), (0,)), ((), ()))
TN = (((0,), (0,)), ((), ()))


def dot(a, b, dims=NN):
    return lax.dot_general(a, b, dims, preferred_element_type=f32)


def seg_of(bounds_ref, row, shape, dim):
    place = lax.broadcasted_iota(jnp.int32, shape, dim)
    total = jnp.zeros(shape, jnp.int32)
    for k in range(bounds_ref.shape[1]):
        total += (place >= bounds_ref[row, k]).astype(jnp.int32)
    return total


def seg_columns(bounds_ref, row, length):
    shape = (length, PAIR)
    seg = seg_of(bounds_ref, row, shape, 0)
    lane = lax.broadcasted_iota(jnp.int32, shape, 1)
    low = lane < HD
    spot = jnp.where(low, lane, lane - HD)
    same = spot == seg
    inside = spot < 4
    query_cols = jnp.where(same, 1.0, 0.0).astype(bf16)
    key_cols = jnp.where(inside, jnp.where(same, 0.0, MASKED), 0.0).astype(bf16)
    return low, query_cols, key_cols


def load_qkv(where_ref, raws, w_scr, sem):
    chip, core = where_ref[0], where_ref[1]
    half = w_scr.shape[2] // 2
    copies = []
    for side in range(2):
        col = pl.multiple_of((core if side == 0 else 1 - core) * half, PAIR)
        for xy in range(4):
            raw = raws[side * 4 + xy]
            for z in range(4):
                at = where_ref[2 + xy * 4 + z]
                rows = w_scr.shape[1] // CHIPS
                for s in range(3):
                    copies.append(
                        pltpu.make_async_copy(
                            raw.at[pl.ds((3 * z + s) * rows, rows), :],
                            w_scr.at[s, pl.ds(pl.multiple_of(at * rows, 16), rows), pl.ds(col, half)],
                            sem,
                        )
                    )
    for c in copies:
        c.start()
    for c in copies:
        c.wait()


def key_span(block, step, reach, length):
    first = max(0, block * step - (reach - 1)) // step * step
    last = min(length, -(-((block + 1) * step - 1 + reach) // step) * step)
    return first, last


def attend_forward_kernel(
    where_ref, bounds_ref, x_ref, vec_ref, *rest
):
    raws = rest[:8]
    qkv_ref, o_ref, lse_ref, wout_ref, w_scr, qkv_scr, sem, out_sem = rest[8:]
    row = pl.program_id(0)
    length = x_ref.shape[0]
    width = x_ref.shape[1]

    @pl.when(row == 0)
    def _():
        load_qkv(where_ref, raws, w_scr, sem)
        pltpu.make_async_copy(w_scr, wout_ref, out_sem).start()

    x = x_ref[...]
    q = (dot(x, w_scr[0]) + vec_ref[0:1, :]).astype(bf16) * jnp.asarray(HD**-0.5, bf16)
    qkv_scr[:, 0:width] = q
    qkv_scr[:, width : 2 * width] = dot(x, w_scr[1]).astype(bf16)
    qkv_scr[:, 2 * width : 3 * width] = (dot(x, w_scr[2]) + vec_ref[1:2, :]).astype(bf16)
    qkv_ref[...] = qkv_scr[...]
    low, query_cols, key_cols = seg_columns(bounds_ref, row, length)
    sub = lax.broadcasted_iota(jnp.int32, (PAIR, length), 0)
    step = 128
    reach = 256

    def pair_body(pair, _):
        at = pl.multiple_of(pair * PAIR, PAIR)
        qp = qkv_scr[:, pl.ds(at, PAIR)]
        kp = qkv_scr[:, pl.ds(width + at, PAIR)]
        vt = qkv_scr[:, pl.ds(2 * width + at, PAIR)].T
        outs = []
        logs = []
        for even in (True, False):
            pick = low if even else jnp.logical_not(low)
            qa = jnp.where(pick, qp, query_cols)
            ka = jnp.where(pick, kp, key_cols)
            if even:
                va = jnp.where(sub < HD, vt, (sub == HD).astype(bf16))
            else:
                va = jnp.where(sub < HD, (sub == 0).astype(bf16), vt)
            blocks = []
            lse_blocks = []
            for b in range(length // step):
                first, last = key_span(b, step, reach, length)
                scores = dot(ka[first:last], qa[b * step : (b + 1) * step], NT)
                peak = jnp.max(scores, axis=0, keepdims=True)
                probs = jnp.exp(scores - peak).astype(bf16)
                mixed = dot(va[:, first:last], probs)
                total = mixed[HD : HD + 1] if even else mixed[0:1]
                mine = mixed[:HD] if even else mixed[HD:]
                blocks.append((mine * (1.0 / total)).astype(bf16))
                lse_blocks.append(peak + jnp.log(total))
            outs.append(jnp.concatenate(blocks, axis=1))
            logs.append(jnp.concatenate(lse_blocks, axis=1))
        o_ref[:, pl.ds(at, PAIR)] = jnp.concatenate(outs, axis=0).T
        lse_ref[0, pl.ds(pair, 1)] = jnp.concatenate(logs, axis=0)[None]
        return 0

    lax.fori_loop(0, width // PAIR, pair_body, 0, unroll=True)

    @pl.when(row == pl.num_programs(0) - 1)
    def _():
        pltpu.make_async_copy(w_scr, wout_ref, out_sem).wait()


def attend_forward(where, bounds, tokens, vec_rows, raws):
    rows = bounds.shape[0]
    tok, width = tokens.shape
    length = tok // rows
    pairs = width // PAIR
    any_spec = pl.BlockSpec(memory_space=pl.ANY)
    return pl.pallas_call(
        attend_forward_kernel,
        grid_spec=pltpu.PrefetchScalarGridSpec(
            num_scalar_prefetch=2,
            grid=(rows,),
            in_specs=[
                pl.BlockSpec((length, width), lambda r, *_: (r, 0)),
                pl.BlockSpec(vec_rows.shape, lambda r, *_: (0, 0)),
            ]
            + [any_spec] * 8,
            out_specs=[
                pl.BlockSpec((length, 3 * width), lambda r, *_: (r, 0)),
                pl.BlockSpec((length, width), lambda r, *_: (r, 0)),
                pl.BlockSpec((1, pairs, 2, length), lambda r, *_: (r, 0, 0, 0)),
                any_spec,
            ],
            scratch_shapes=[
                pltpu.VMEM((3, width, width), bf16),
                pltpu.VMEM((length, 3 * width), bf16),
                pltpu.SemaphoreType.DMA,
                pltpu.SemaphoreType.DMA,
            ],
        ),
        out_shape=[
            jax.ShapeDtypeStruct((tok, 3 * width), bf16),
            jax.ShapeDtypeStruct((tok, width), bf16),
            jax.ShapeDtypeStruct((rows, pairs, 2, length), f32),
            jax.ShapeDtypeStruct((3, width, width), bf16),
        ],
        compiler_params=pltpu.CompilerParams(vmem_limit_bytes=56 * MIB),
        name="attend_forward",
    )(where, bounds, tokens, vec_rows, *raws)


def lane_mean(v):
    return jnp.mean(v, axis=1, keepdims=True)


def norm_parts(v):
    center = v - lane_mean(v)
    scale = lax.rsqrt(lane_mean(center * center) + 1e-12)
    return center * scale, scale


def norm_back(grad, unit, scale, gain):
    grad_unit = grad * gain
    return scale * (grad_unit - lane_mean(grad_unit) - unit * lane_mean(grad_unit * unit))


def fold(v):
    return jnp.sum(v.reshape(v.shape[0] // 8, 8, v.shape[1]), axis=0)


def gelu_both(z):
    size = jnp.abs(z)
    t = pl.reciprocal(1.0 + (0.3275911 * 0.5**0.5) * size, approx=APPROX)
    e = jnp.exp(-0.5 * z * z)
    poly = 0.5 * 1.061405429
    for a in (-1.453152027, 1.421413741, -0.284496736, 0.254829592):
        poly = poly * t + 0.5 * a
    tail = poly * t * e
    cdf = jnp.where(z >= 0, 1.0 - tail, tail)
    return z * cdf, cdf + z * e * 0.3989422804014327


APPROX = False
FC = 768
SLOTS = 4


def middle_kernel(
    where_ref, mixed_ref, x_ref, cot_ref, vec_ref, packed_ref,
    out_ref, gmixed_ref, gres_ref, gvec_ref, mine_a, theirs_a, mine_b, theirs_b,
    w1, w2, wo, acc1, acc2, acco, accv, act, slope, stage_a, stage_b, in_sem, out_sem,
):
    step = pl.program_id(0)
    width = x_ref.shape[1]
    chunks = w1.shape[1] // width

    @pl.when(step == 0)
    def _():
        copies = [pltpu.make_async_copy(packed_ref.at[:, pl.ds(2 * chunks * width, width)], wo, in_sem)]
        copies.append(pltpu.make_async_copy(packed_ref.at[:, pl.ds(0, chunks * width)], w1, in_sem))
        for j in range(chunks):
            copies.append(
                pltpu.make_async_copy(
                    packed_ref.at[:, pl.ds((chunks + j) * width, width)], w2.at[pl.ds(j * width, width), :], in_sem
                )
            )
        for c in copies:
            c.start()
        acc1[...] = jnp.zeros_like(acc1)
        acc2[...] = jnp.zeros_like(acc2)
        acco[...] = jnp.zeros_like(acco)
        accv[...] = jnp.zeros_like(accv)
        for c in copies:
            c.wait()

    mixed = mixed_ref[...]
    res_one = x_ref[...].astype(f32) + dot(mixed, wo[...]) + vec_ref[2:3, :]
    unit_one, scale_one = norm_parts(res_one)
    hidden = unit_one * vec_ref[3:4, :] + vec_ref[4:5, :]
    hidden_low = hidden.astype(bf16)
    ffn = hidden + vec_ref[5:6, :]
    for j in range(w1.shape[1] // FC):
        cols = slice(j * FC, (j + 1) * FC)
        at = j * FC // width
        inner = slice(j * FC - at * width, (j + 1) * FC - at * width)
        z = dot(hidden_low, w1[:, cols]) + vec_ref[8 + at : 9 + at, inner]
        g, d = gelu_both(z)
        g = g.astype(bf16)
        act[:, cols] = g
        slope[:, cols] = d.astype(slope.dtype)
        ffn += dot(g, w2[cols, :])
    unit_two, scale_two = norm_parts(ffn)
    out_ref[...] = (unit_two * vec_ref[6:7, :] + vec_ref[7:8, :]).astype(bf16)
    grad = cot_ref[...].astype(f32)
    accv[6] += fold(grad * unit_two)
    accv[7] += fold(grad)
    grad_two = norm_back(grad, unit_two, scale_two, vec_ref[6:7, :])
    grad_ffn = grad_two.astype(bf16)
    accv[5] += fold(grad_ffn.astype(f32))
    grad_hidden = grad_two
    hidden_t = hidden_low.T
    for j in range(w1.shape[1] // FC):
        cols = slice(j * FC, (j + 1) * FC)
        at = j * FC // width
        inner = slice(j * FC - at * width, (j + 1) * FC - at * width)
        gz = (dot(grad_ffn, w2[cols, :], NT) * slope[:, cols].astype(f32)).astype(bf16)
        accv[8 + at, :, inner] += fold(gz.astype(f32))
        acc2[cols, :] += dot(act[:, cols], grad_ffn, TN)
        acc1[:, cols] += dot(hidden_t, gz)
        grad_hidden += dot(gz, w1[:, cols], NT)
    accv[3] += fold(grad_hidden * unit_one)
    accv[4] += fold(grad_hidden)
    grad_one = norm_back(grad_hidden, unit_one, scale_one, vec_ref[3:4, :])
    gres_ref[...] = grad_one
    grad_attn = grad_one.astype(bf16)
    accv[2] += fold(grad_attn.astype(f32))
    acco[...] += dot(mixed, grad_attn, TN)
    gmixed_ref[...] = dot(grad_attn, wo[...], NT).astype(bf16)

    @pl.when(step == pl.num_programs(0) - 1)
    def _():
        gvec_ref[...] = jnp.sum(accv[...], axis=1)
        part = stage_a.shape[1]
        amount = mine_a.shape[0]

        def send(n, side, dst_a, dst_b, wait):
            core = where_ref[1] if side == 0 else 1 - where_ref[1]
            row = pl.multiple_of((where_ref[2 + n] * 2 + core) * part, 8)
            rows = pl.ds(row, part)
            slot = side + 2 * lax.rem(n, SLOTS)
            copy_a = pltpu.make_async_copy(stage_a.at[slot], dst_a.at[n], out_sem.at[slot, 0])
            copy_b = pltpu.make_async_copy(stage_b.at[slot], dst_b.at[n], out_sem.at[slot, 1])

            @pl.when(wait)
            def _():
                copy_a.wait()
                copy_b.wait()

            stage_a[slot] = acc1[rows, :].astype(bf16)
            for j in range(chunks):
                stage_b[slot, :, j * width : (j + 1) * width] = acc2[
                    pl.ds(pl.multiple_of(j * width + row, 8), part), :
                ].astype(bf16)
            stage_b[slot, :, chunks * width :] = acco[rows, :].astype(bf16)
            copy_a.start()
            copy_b.start()
            return copy_a, copy_b

        def body(n, _):
            send(n, 1, theirs_a, theirs_b, n >= SLOTS)
            send(n, 0, mine_a, mine_b, n >= SLOTS)
            return 0

        lax.fori_loop(0, amount, body, 0)
        for slot in range(2 * SLOTS):
            pltpu.make_async_copy(stage_a.at[slot], mine_a.at[0], out_sem.at[slot, 0]).wait()
            pltpu.make_async_copy(stage_b.at[slot], mine_b.at[0], out_sem.at[slot, 1]).wait()


def middle(where, mixed, tokens, cotangent, vec_rows, packed, block=256):
    tok, width = tokens.shape
    chunks = (packed.shape[1] // width - 1) // 2
    chips = CHIPS
    part = width // (2 * chips)
    any_spec = pl.BlockSpec(memory_space=pl.ANY)
    row_spec = pl.BlockSpec((block, width), lambda r, *_: (r, 0))
    vec_spec = pl.BlockSpec((vec_rows.shape[0], width), lambda r, *_: (0, 0))
    ff = chunks * width
    return pl.pallas_call(
        middle_kernel,
        grid_spec=pltpu.PrefetchScalarGridSpec(
            num_scalar_prefetch=1,
            grid=(tok // block,),
            in_specs=[row_spec, row_spec, row_spec, vec_spec, any_spec],
            out_specs=[row_spec, row_spec, row_spec, vec_spec] + [any_spec] * 4,
            scratch_shapes=[
                pltpu.VMEM((width, ff), bf16),
                pltpu.VMEM((ff, width), bf16),
                pltpu.VMEM((width, width), bf16),
                pltpu.VMEM((width, ff), f32),
                pltpu.VMEM((ff, width), f32),
                pltpu.VMEM((width, width), f32),
                pltpu.VMEM((vec_rows.shape[0], 8, width), f32),
                pltpu.VMEM((block, ff), bf16),
                pltpu.VMEM((block, ff), bf16),
                pltpu.VMEM((2 * SLOTS, part, ff), bf16),
                pltpu.VMEM((2 * SLOTS, part, ff + width), bf16),
                pltpu.SemaphoreType.DMA,
                pltpu.SemaphoreType.DMA((2 * SLOTS, 2)),
            ],
        ),
        out_shape=[
            jax.ShapeDtypeStruct((tok, width), bf16),
            jax.ShapeDtypeStruct((tok, width), bf16),
            jax.ShapeDtypeStruct((tok, width), f32),
            jax.ShapeDtypeStruct(vec_rows.shape, f32),
            jax.ShapeDtypeStruct((chips, part, ff), bf16),
            jax.ShapeDtypeStruct((chips, part, ff), bf16),
            jax.ShapeDtypeStruct((chips, part, ff + width), bf16),
            jax.ShapeDtypeStruct((chips, part, ff + width), bf16),
        ],
        compiler_params=pltpu.CompilerParams(vmem_limit_bytes=60 * MIB),
        name="middle",
    )(where, mixed, tokens, cotangent, vec_rows, packed)


def attend_backward_kernel(
    where_ref, bounds_ref, x_ref, q_ref, k_ref, v_ref, mixed_ref, gmixed_ref, lse_ref,
    gqkv_ref, gbias_ref, mine_ref, theirs_ref,
    acc, accb, probs_scr, grads_scr, stage, out_sem,
):
    row = pl.program_id(0)
    length, width = q_ref.shape
    pairs = width // PAIR
    low, query_cols, key_cols = seg_columns(bounds_ref, row, length)
    step = 128
    reach = 256

    @pl.when(row == 0)
    def _():
        acc[...] = jnp.zeros_like(acc)
        accb[...] = jnp.zeros_like(accb)
        probs_scr[...] = jnp.zeros_like(probs_scr)
        grads_scr[...] = jnp.zeros_like(grads_scr)

    head_of = lax.broadcasted_iota(jnp.int32, (8, width), 1) // HD
    pick_head = (head_of == lax.broadcasted_iota(jnp.int32, (8, width), 0)).astype(bf16)
    product = gmixed_ref[...].astype(f32) * mixed_ref[...].astype(f32)
    upper = product.astype(bf16)
    lower = (product - upper.astype(f32)).astype(bf16)
    means = dot(pick_head, upper, NT) + dot(pick_head, lower, NT)
    none = jnp.zeros((length, PAIR), bf16)

    for pair in range(pairs):
        at = slice(pair * PAIR, (pair + 1) * PAIR)
        qp, kp, vp, gp = q_ref[:, at], k_ref[:, at], v_ref[:, at], gmixed_ref[:, at]
        kt = kp.T
        for side in range(2):
            pick = low if side == 0 else jnp.logical_not(low)
            qa = jnp.where(pick, qp, query_cols)
            ka = jnp.where(pick, kp, key_cols)
            va = jnp.where(pick, vp, none)
            for b in range(length // step):
                first, last = key_span(b, step, reach, length)
                block = slice(b * step, (b + 1) * step)
                cols = slice(side * length + b * step, side * length + (b + 1) * step)
                scores = dot(ka[first:last], qa[block], NT)
                probs = jnp.exp(scores - lse_ref[0, pair, side : side + 1, block])
                gprobs = dot(va[first:last], gp[block], NT)
                head = 2 * pair + side
                grads = probs * (gprobs - means[head : head + 1, block])
                probs_scr[first:last, cols] = probs.astype(bf16)
                grads_scr[first:last, cols] = grads.astype(bf16)
        gq_t = jnp.concatenate(
            [dot(kt[:HD], grads_scr[:, :length]), dot(kt[HD:], grads_scr[:, length:])], axis=0
        )
        gq = (gq_t * HD**-0.5).astype(bf16).T
        both_q = jnp.concatenate([jnp.where(low, qp, none), jnp.where(low, none, qp)], axis=0)
        both_g = jnp.concatenate([jnp.where(low, gp, none), jnp.where(low, none, gp)], axis=0)
        gk = dot(grads_scr[...], both_q).astype(bf16)
        gv = dot(probs_scr[...], both_g).astype(bf16)
        for s, part in enumerate((gq, gk, gv)):
            spot = slice(s * width + pair * PAIR, s * width + (pair + 1) * PAIR)
            gqkv_ref[:, spot] = part
            if s != 1:
                accb[:, spot] += fold(part.astype(f32))
    acc[...] += dot(x_ref[...], gqkv_ref[...], TN)

    @pl.when(row == pl.num_programs(0) - 1)
    def _():
        gbias_ref[...] = jnp.broadcast_to(jnp.sum(accb[...], axis=0, keepdims=True), gbias_ref.shape)
        part = stage.shape[1]
        amount = mine_ref.shape[0]

        def send(n, side, dst):
            core = where_ref[1] if side == 0 else 1 - where_ref[1]
            rows = pl.ds(pl.multiple_of((where_ref[2 + n] * 2 + core) * part, 8), part)
            slot = side * amount + n
            stage[slot] = acc[rows, :].astype(bf16)
            pltpu.make_async_copy(stage.at[slot], dst.at[n], out_sem).start()

        def body(n, _):
            send(n, 1, theirs_ref)
            send(n, 0, mine_ref)
            return 0

        lax.fori_loop(0, amount, body, 0)
        pltpu.make_async_copy(stage.at[pl.ds(0, amount)], mine_ref, out_sem).wait()
        pltpu.make_async_copy(stage.at[pl.ds(amount, amount)], theirs_ref, out_sem).wait()


def attend_backward(where, bounds, tokens, qkv, mixed, gmixed, lse, group, groups):
    rows = bounds.shape[0]
    tok, model = tokens.shape
    length = tok // rows
    width = model // groups
    pairs = width // PAIR
    chips = CHIPS
    part = model // (2 * chips)
    any_spec = pl.BlockSpec(memory_space=pl.ANY)
    own = lambda s: pl.BlockSpec((length, width), lambda r, *_: (r, s * groups + group))
    return pl.pallas_call(
        attend_backward_kernel,
        grid_spec=pltpu.PrefetchScalarGridSpec(
            num_scalar_prefetch=2,
            grid=(rows,),
            in_specs=[
                pl.BlockSpec((length, model), lambda r, *_: (r, 0)),
                own(0), own(1), own(2), own(0), own(0),
                pl.BlockSpec((1, pairs, 2, length), lambda r, *_: (r, group, 0, 0)),
            ],
            out_specs=[
                pl.BlockSpec((length, 3 * width), lambda r, *_: (r, 0)),
                pl.BlockSpec((8, 3 * width), lambda r, *_: (0, 0)),
                any_spec,
                any_spec,
            ],
            scratch_shapes=[
                pltpu.VMEM((model, 3 * width), f32),
                pltpu.VMEM((8, 3 * width), f32),
                pltpu.VMEM((length, 2 * length), bf16),
                pltpu.VMEM((length, 2 * length), bf16),
                pltpu.VMEM((2 * chips, part, 3 * width), bf16),
                pltpu.SemaphoreType.DMA,
            ],
        ),
        out_shape=[
            jax.ShapeDtypeStruct((tok, 3 * width), bf16),
            jax.ShapeDtypeStruct((8, 3 * width), f32),
            jax.ShapeDtypeStruct((chips, part, 3 * width), bf16),
            jax.ShapeDtypeStruct((chips, part, 3 * width), bf16),
        ],
        compiler_params=pltpu.CompilerParams(vmem_limit_bytes=56 * MIB),
        name="attend_backward",
    )(where, bounds, tokens, qkv, qkv, qkv, mixed, gmixed, lse)


def input_grad_kernel(gres_ref, w_ref, *rest):
    parts, out_ref = rest[:-1], rest[-1]
    total = gres_ref[...]
    width = parts[0].shape[1] // 3
    for g, part in enumerate(parts):
        for s in range(3):
            total += dot(part[:, s * width : (s + 1) * width], w_ref[s, :, g * width : (g + 1) * width], NT)
    out_ref[...] = total.astype(bf16)


def input_grad(gres, weights, parts, block=512):
    tok, model = gres.shape
    return pl.pallas_call(
        input_grad_kernel,
        grid=(tok // block,),
        in_specs=[
            pl.BlockSpec((block, model), lambda r: (r, 0)),
            pl.BlockSpec(weights.shape, lambda r: (0, 0, 0)),
        ]
        + [pl.BlockSpec((block, p.shape[1]), lambda r: (r, 0)) for p in parts],
        out_specs=pl.BlockSpec((block, model), lambda r: (r, 0)),
        out_shape=jax.ShapeDtypeStruct((tok, model), bf16),
        compiler_params=pltpu.CompilerParams(vmem_limit_bytes=56 * MIB),
        name="input_grad",
    )(gres, weights, *parts)


class Ring:
    def __init__(self, sizes):
        self.sizes = sizes
        self.amount = sizes["gx"] * sizes["gy"]
        self.near = sizes == {"gx": 8, "gy": 4}

    def index(self):
        return lax.axis_index("gx") * self.sizes["gy"] + lax.axis_index("gy")

    def swap(self, value, bits):
        return lax.ppermute(value, ALL, [(i, i ^ bits) for i in range(self.amount)])

    def core(self, value):
        return self.swap(value, 1)

    def plane(self, value, k):
        return self.swap(value, k << 1)

    def line(self, value, k):
        return self.swap(value, k << 3)


def where_am_i(ring):
    if not ring.near:
        return jnp.asarray([0, 0] + list(range(CHIPS)), jnp.int32)
    me = ring.index()
    chip = me // 2
    order = [chip ^ ((z << 2) | xy) for xy in range(4) for z in range(4)]
    return jnp.stack([chip, me % 2] + order).astype(jnp.int32)


def gather_first(ring, w_qkv, vec_part):
    low = w_qkv.astype(bf16)
    part, width = low.shape[1], low.shape[2]
    half = width // 2
    vec_rows = vec_part.shape[0]
    vec_part = vec_part.astype(bf16)
    if not ring.near:
        full = lax.all_gather(low, ALL, axis=1, tiled=True)
        blocks = full.reshape(3, CHIPS, width // CHIPS, 2, half).transpose(3, 1, 0, 2, 4)
        blocks = blocks.reshape(8, 4 * 3 * width // CHIPS, half)
        vecs = lax.all_gather(vec_part, ALL, axis=1, tiled=True)
        return [blocks[i] for i in range(8)], vecs.astype(f32)
    me = ring.index()
    core = me % 2
    spread = jnp.zeros((16, width), bf16)
    spread = lax.dynamic_update_slice(spread, vec_part, (0, me * part))
    spread = spread.reshape(32, half)
    left, right = low[:, :, :half], low[:, :, half:]
    keep = jnp.where(core == 0, left, right)
    give = jnp.where(core == 0, right, left)
    got = ring.core(jnp.concatenate([give.reshape(3 * part, half), spread], axis=0))
    came = got[: 3 * part].reshape(3, part, half)
    block = jnp.where(
        core == 0, jnp.concatenate([keep, came], axis=1), jnp.concatenate([came, keep], axis=1)
    ).reshape(6 * part, half)
    payload = jnp.concatenate([block, spread + got[3 * part :]], axis=0)
    cut = 6 * part
    lines = [payload] + [ring.line(payload, k) for k in (1, 2, 3)]
    total = lines[0][cut:] + lines[1][cut:] + lines[2][cut:] + lines[3][cut:]
    payload = jnp.concatenate([v[:cut] for v in lines] + [total], axis=0)
    mine = [payload] + [ring.plane(payload, k) for k in (1, 2, 3)]
    theirs = [ring.core(v) for v in mine]
    cut = 4 * cut
    total = mine[0][cut:] + mine[1][cut:] + mine[2][cut:] + mine[3][cut:]
    return mine + theirs, total.reshape(16, width)[:vec_rows].astype(f32)


def gather_rest(w_out, w_up, w_down):
    part, width = w_out.shape
    chunks = w_up.shape[1] // width
    up = w_up.astype(bf16).reshape(part, width, chunks).transpose(0, 2, 1).reshape(part, chunks * width)
    down = w_down.astype(bf16).reshape(part, chunks * width)
    packed = jnp.concatenate([up, down, w_out.astype(bf16)], axis=1)
    return lax.all_gather(packed, ALL, axis=0, tiled=True)


def scatter(ring, mine, theirs, vec=None):
    chips, part, width = mine.shape
    if not ring.near:
        full = jnp.stack([mine, theirs], axis=1).reshape(2 * chips * part, width)
        total = lax.psum_scatter(full, ALL, scatter_dimension=0, tiled=True).astype(f32)
        if vec is not None:
            vec = lax.psum(vec, ALL)
        return total, vec
    came = ring.core(theirs)
    if vec is not None:
        vec = vec + ring.core(vec)

    def packed(rows, vec):
        rows = rows.astype(bf16).reshape(-1, width)
        if vec is None:
            return rows
        return jnp.concatenate([rows, vec.reshape(-1, width).astype(bf16)], axis=0)

    def added(rows, vec, parts):
        cut = rows.shape[0] * rows.shape[1]
        for p in parts:
            rows = rows + p[:cut].reshape(rows.shape).astype(f32)
            if vec is not None:
                vec = vec + p[cut:].reshape(vec.shape).astype(f32)
        return rows, vec

    def near(xy):
        at = slice(4 * xy, 4 * xy + 4)
        return mine[at].astype(f32) + came[at].astype(f32)

    parts = [ring.plane(packed(near(k), vec), k) for k in (1, 2, 3)]
    rows, vec = added(near(0), vec, parts)
    parts = [ring.line(packed(rows[k : k + 1], vec), k) for k in (1, 2, 3)]
    rows, vec = added(rows[:1], vec, parts)
    return rows[0], vec


def sum_small(ring, values):
    if not ring.near:
        return lax.psum(values, ALL)
    row = jnp.zeros((1, 128), f32).at[0, : values.shape[0]].set(values)
    spread = jnp.broadcast_to(row[None], (ring.amount, 1, 128))
    came = lax.all_to_all(spread, ALL, 0, 0)
    return jnp.sum(came, axis=(0, 1))[: values.shape[0]]


def tensor_squares(tensors):
    return jnp.concatenate(
        [
            jnp.sum(tensors[0] * tensors[0], axis=(1, 2)),
            jnp.sum(tensors[1] * tensors[1])[None],
            jnp.sum(tensors[2] * tensors[2])[None],
            jnp.sum(tensors[3] * tensors[3])[None],
            jnp.sum(tensors[4] * tensors[4], axis=1),
            jnp.sum(tensors[5] * tensors[5])[None],
        ]
    )


def spread_ratios(ratios):
    return (
        ratios[0:3][:, None, None],
        ratios[3],
        ratios[4],
        ratios[5],
        ratios[6:14][:, None],
        ratios[14],
    )


GROUPS = 2


def on_device(
    ring,
    tokens,
    seg_lengths,
    cotangent,
    *params,
):
    masters = params[0:6]
    firsts_in = params[6:12]
    seconds_in = params[12:18]
    averages = params[18:24]
    w_qkv, w_out, w_up, w_down, vecs, b_up = masters
    part, width = w_out.shape
    chunks = w_up.shape[1] // width
    bounds = jnp.stack(
        [jnp.sum(seg_lengths[:, : k + 1], axis=1) for k in range(seg_lengths.shape[1])], axis=1
    ).astype(jnp.int32)
    where = where_am_i(ring)
    packed = gather_rest(w_out, w_up, w_down)
    vec_part = jnp.concatenate([vecs, b_up.reshape(part, chunks).T], axis=0)
    raws, vec_rows = gather_first(ring, w_qkv, vec_part)
    vec_rows = jnp.concatenate([vec_rows, jnp.zeros((4, width), f32)], axis=0)
    qkv, mixed, lse, full_qkv = attend_forward(where, bounds, tokens, vec_rows, raws)
    layer_out, gmixed, gres, gvec, mine_a, theirs_a, mine_b, theirs_b = middle(
        where, mixed, tokens, cotangent, vec_rows, packed
    )
    grad_up, _ = scatter(ring, mine_a, theirs_a)
    grad_rest, _ = scatter(ring, mine_b, theirs_b)
    backs = [
        attend_backward(where, bounds, tokens, qkv, mixed, gmixed, lse, g, GROUPS) for g in range(GROUPS)
    ]
    grad_input = input_grad(gres, full_qkv, [b[0] for b in backs])
    own = width // GROUPS
    gbias = jnp.concatenate([b[1][0].reshape(3, own) for b in backs], axis=1)
    gvec = jnp.concatenate([gbias[0:1], gbias[2:3], gvec[2:12]], axis=0)
    sums = []
    for g, b in enumerate(backs):
        total, back_vec = scatter(ring, b[2], b[3], gvec if g == GROUPS - 1 else None)
        sums.append(total.reshape(part, 3, own))
    grad_qkv = jnp.concatenate(sums, axis=2).transpose(1, 0, 2)
    gvec = lax.dynamic_slice(back_vec, (0, ring.index() * part), (12, part))
    ff = chunks * width
    reduced = (
        grad_qkv,
        grad_rest[:, ff:],
        grad_up.reshape(part, chunks, width).transpose(0, 2, 1).reshape(part, ff),
        grad_rest[:, :ff].reshape(part * chunks, width),
        gvec[:8],
        gvec[8:].T.reshape(part * chunks),
    )
    corr_one = 1.0 - beta_one**STEP
    corr_two = 1.0 - beta_two**STEP
    firsts = []
    seconds = []
    updates = []
    for member in range(6):
        first_new = beta_one * firsts_in[member] + (1.0 - beta_one) * reduced[member]
        second_new = (
            beta_two * seconds_in[member] + (1.0 - beta_two) * reduced[member] * reduced[member]
        )
        update = (
            first_new / corr_one / (jnp.sqrt(second_new / corr_two) + adam_eps)
            + decay_rate * masters[member]
        )
        firsts.append(first_new)
        seconds.append(second_new)
        updates.append(update)
    squares = sum_small(ring, jnp.concatenate([tensor_squares(masters), tensor_squares(updates)]))
    sq_weight, sq_update = squares[:15], squares[15:]
    ratios = jnp.sqrt(sq_weight) / jnp.sqrt(sq_update + ratio_eps)
    scales = spread_ratios(ratios)
    renewed = [
        masters[member] - learn_rate * scales[member] * updates[member] for member in range(6)
    ]
    emas = [ema_rate * averages[member] + (1.0 - ema_rate) * renewed[member] for member in range(6)]
    norm_pairs = jnp.stack([jnp.sqrt(sq_weight), jnp.sqrt(sq_update)])
    copies = [v.astype(bf16) for v in renewed]
    return (layer_out, grad_input, *renewed, *firsts, *seconds, *emas, *copies, ratios, norm_pairs)


def solution(mesh):
    ring = Ring(dict(mesh.shape))
    rows = P(ALL, None)
    kinds = (P(None, ALL, None), rows, rows, rows, P(None, ALL), P(ALL))
    return jax.shard_map(
        functools.partial(on_device, ring),
        mesh=mesh,
        in_specs=(rows, rows, rows) + kinds * 4,
        out_specs=(rows, rows) + kinds * 5 + (P(), P()),
        check_vma=False,
    )
```

time: 1180 us -> 475 us (0.40)
  matrix products: 363 us -> 0 us
  waiting for transfers between devices: 358 us -> 128 us
  Pallas kernels: 0 us -> 205 us
  blocking collectives: 163 us -> 0 us
  local copies, waits for them, and re-layouts: 157 us -> 20.1 us
  other arithmetic: 107 us -> 51.7 us
  starting transfers between devices: 0.33 us -> 44.4 us
    dot_general x40 -> x0, matrix products: 363 us -> none  [the longest x1 70.2 us: on_device(): pre_act = jnp.dot(hidden_low, full_up, preferred_element_type=f32) + up_bias]
    reduce_scatter x3 -> x0, waiting for transfers between devices: 277 us -> none  [the longest x1 139 us: reduce_grads(): lax.psum_scatter(grads[2], ('gx', 'gy'), scatter_dimension=0, tiled=True)]
    pallas_call x0 -> x5, Pallas kernels: none -> 205 us  [the longest x1 104 us: middle(): pl.pallas_call(middle_kernel, grid_spec=pltpu.PrefetchScalarGridSpec(num_...]
    ppermute x0 -> x40, waiting for transfers between devices: none -> 116 us  [swap(): return lax.ppermute(value, ALL, [(i, i ^ bits) for i in range(self.amount)])]
    unnamed x9 -> x1, waiting for transfers between devices: 80.5 us -> 0.02 us
    unnamed x2 -> x0, blocking collectives: 80 us -> none
    all_gather x1 -> x0, blocking collectives: 43.5 us -> none  [gather_weights(): lax.all_gather(shards[4], ('gx', 'gy'), axis=1, tiled=True)]
    ppermute x0 -> x40, starting transfers between devices: none -> 41.1 us  [swap(): return lax.ppermute(value, ALL, [(i, i ^ bits) for i in range(self.amount)])]
  transfers between devices with their start and end apart: 8 -> 42, of which waited for: 3 -> 24; matrix products, arithmetic and copies ran while one was open for 40% -> 9% of each run, Pallas kernels for 0% -> 10%
where the time goes in v1:
time: 475 us; the launch traced here: 468 us
  Pallas kernels  205 us (43%)
  waiting for transfers between devices  128 us (27%)
  other arithmetic  51.7 us (11%)
  starting transfers between devices  44.4 us (9%)
  local copies, waits for them, and re-layouts  20.1 us (4%)
  between operations  18 us (4%)
    ppermute x40, waiting for transfers between devices, swap(): return lax.ppermute(value, ALL, [(i, i ^ bits) for i in range(self.amount)])  116 us
    pallas_call x1, Pallas kernels, middle(): pl.pallas_call(middle_kernel, grid_spec=pltpu.PrefetchScalarGridSpec(num_...  104 us
    pallas_call x2, Pallas kernels, attend_backward(): pl.pallas_call(attend_backward_kernel, grid_spec=pltpu.PrefetchScalarGrid...  56.7 us
    ppermute x40, starting transfers between devices, swap(): return lax.ppermute(value, ALL, [(i, i ^ bits) for i in range(self.amount)])  41.1 us
    pallas_call x1, Pallas kernels, attend_forward(): pl.pallas_call(attend_forward_kernel, grid_spec=pltpu.PrefetchScalarGridS...  29.7 us
    pallas_call x1, Pallas kernels, input_grad(): pl.pallas_call(input_grad_kernel, grid=(tok // block,), in_specs=[pl.Bloc...  15.1 us
    all_gather x1, waiting for transfers between devices, gather_rest(): return lax.all_gather(packed, ALL, axis=0, tiled=True)  12.1 us
    another operation x7, other arithmetic  9.73 us
  transfers between devices with their start and end apart: 42, of which 24 were waited for; matrix products, arithmetic and copies ran while one was open for 9% of the time, Pallas kernels for 10%

profile of v1, /device:TPU:0, one launch (start us, length us, event | category | flops | bytes accessed | tf_op | source)
XLA Modules:
  0.0 467.6 jit_solution(1909958863090949902)
XLA Ops:
  14.5 3.0 collective-permute-start.1
  17.5 2.2 collective-permute-start.3
  21.5 17.9 %collective-permute-done.2 = bf16[176,384]{1,0:T(8,128)(2,1)S(1)} collective-permute-done((bf16[176,384]{1,0:T(8,128)(2,1)S(1)}, bf16[176,384]{1,0:T(8,128)(2,1)S(1)}, u32[]{:S(2)}, u32[]{:S(2)}) %collective-permute-start.2) | collective-permute-done | bytes 135200 | tf_op jit(solution)/shard_map/ppermute | solution.py:558
  39.5 2.2 collective-permute-start.6
  43.3 16.8 %collective-permute-done.6.rest_3_ = bf16[608,384]{1,0:T(8,128)(2,1)S(1)} collective-permute-done((bf16[608,384]{1,0:T(8,128)(2,1)S(1)}, bf16[608,384]{1,0:T(8,128)(2,1)S(1)}, u32[]{:S(2)}, u32[]{:S(2)}) %collective-permute-start.6) | collective-permute-done | bytes 466976 | tf_op jit(solution)/shard_map/ppermute | solution.py:558
  60.1 4.4 collective-permute-done.5.rest_2_
  64.6 4.6 collective-permute-done.4.rest_1_
  72.8 29.7 %attend_forward.1 = (bf16[2048,2304]{1,0:T(8,128)(2,1)}, bf16[2048,768]{1,0:T(8,128)(2,1)}, f32[4,6,2,512]{3,2,1,0:T(2,128)}, bf16[3,768,768]{2,1,0:T(8,128)(2,1)}) custom-call(s32[18]{0:T(128)} %stack.94.where_ref, s32[4,4]{1,0:T(4,128)} %pad_add_fusion.bounds_ref, bf16[2048,768]{1,0:T(8,128)(2,1)} %x_ref.7, f32[16,768]{1,0:T(8,128)} %pad_convert_fusion.vec_ref, ...), custom_call_target="tpu_custom_call" | custom-call | tf_op jit(solution)/shard_map/attend_forward/pallas_call | solution.py:161
  102.5 12.1 %all-gather.2.cloned.1.call-done.packed_ref = bf16[768,6912]{1,0:T(8,128)(2,1)} async-done(((bf16[24,6912]{1,0:T(8,128)(2,1)}), bf16[768,6912]{1,0:T(8,128)(2,1)}) %all-gather.2.cloned.1.call-update) | async-done | bytes 10616848 | tf_op jit(solution)/shard_map/all_gather | solution.py:622
  114.6 103.8 %middle.1 = (bf16[2048,768]{1,0:T(8,128)(2,1)}, bf16[2048,768]{1,0:T(8,128)(2,1)}, f32[2048,768]{1,0:T(8,128)}, f32[16,768]{1,0:T(8,128)}, bf16[16,24,3072]{2,1,...) custom-call(s32[18]{0:T(128)} %stack.94.where_ref, ...), custom_call_target="tpu_custom_call" | custom-call | tf_op jit(solution)/shard_map/middle/pallas_call | solution.py:352
  218.5 28.3 %attend_backward.3 = (bf16[2048,1152]{1,0:T(8,128)(2,1)}, f32[8,1152]{1,0:T(8,128)}, bf16[16,24,1152]{2,1,0:T(8,128)(2,1)}, bf16[16,24,1152]{2,1,0:T(8,128)(2,1)}) custom-call(s32[18]{0:T(128)} %stack.94.where_ref, s32[4,4]{1,0:T(4,128)} %pad_add_fusion.bounds_ref, bf16[2048,768]{1,0:T(8,128)(2,1)} %x_ref.7, ...), custom_call_target="tpu_custom_call" | custom-call | tf_op jit(solution)/shard_map/attend_backward/pallas_call | solution.py:485
  246.8 28.4 %attend_backward.2 = (bf16[2048,1152]{1,0:T(8,128)(2,1)}, f32[8,1152]{1,0:T(8,128)}, bf16[16,24,1152]{2,1,0:T(8,128)(2,1)}, bf16[16,24,1152]{2,1,0:T(8,128)(2,1)}) custom-call(s32[18]{0:T(128)} %stack.94.where_ref, s32[4,4]{1,0:T(4,128)} %pad_add_fusion.bounds_ref, bf16[2048,768]{1,0:T(8,128)(2,1)} %x_ref.7, ...), custom_call_target="tpu_custom_call" | custom-call | tf_op jit(solution)/shard_map/attend_backward/pallas_call | solution.py:485
  280.5 1.6 add_convert_fusion.11
  282.1 1.5 collective-permute-start.14
  283.7 1.5 collective-permute-start.12
  287.9 3.5 collective-permute-done.14
  292.8 3.3 collective-permute-done.12
  298.2 2.0 fusion.30
  303.2 4.9 %collective-permute-done.21 = bf16[104,1152]{1,0:T(8,128)(2,1)} collective-permute-done((bf16[104,1152]{1,0:T(8,128)(2,1)}, bf16[104,1152]{1,0:T(8,128)(2,1)}, u32[]{:S(2)}, u32[]{:S(2)}) %collective-permute-start.21) | collective-permute-done | bytes 239648 | tf_op jit(solution)/shard_map/ppermute | solution.py:558
  308.1 1.8 collective-permute-start.17
  314.2 2.0 fusion.31
  318.2 1.5 fusion.32
  319.7 1.5 pad_maximum_fusion.7
  321.3 1.6 collective-permute-start.23
  323.8 1.9 collective-permute-start.25
  327.4 1.7 collective-permute-done.24
  331.1 1.6 fusion.9
  333.5 3.5 add_convert_fusion.5
  341.9 1.9 multiply_reduce_fusion.4
  343.8 8.2 %collective-permute-done.36 = bf16[96,3072]{1,0:T(8,128)(2,1)} collective-permute-done((bf16[96,3072]{1,0:T(8,128)(2,1)}, bf16[96,3072]{1,0:T(8,128)(2,1)}, u32[]{:S(2)}, u32[]{:S(2)}) %collective-permute-start.36) | collective-permute-done | bytes 589856 | tf_op jit(solution)/shard_map/ppermute | solution.py:558
  352.1 4.8 %collective-permute-done.34 = bf16[96,3072]{1,0:T(8,128)(2,1)} collective-permute-done((bf16[96,3072]{1,0:T(8,128)(2,1)}, bf16[96,3072]{1,0:T(8,128)(2,1)}, u32[]{:S(2)}, u32[]{:S(2)}) %collective-permute-start.34) | collective-permute-done | bytes 589856 | tf_op jit(solution)/shard_map/ppermute | solution.py:558
  358.2 2.4 fusion.26
  361.3 2.0 collective-permute-start.39
  364.2 2.1 add_convert_fusion.2
  367.2 1.5 collective-permute-start.27
  371.1 2.9 collective-permute-done.38
  375.4 11.8 %collective-permute-done.29 = bf16[96,3840]{1,0:T(8,128)(2,1)} collective-permute-done((bf16[96,3840]{1,0:T(8,128)(2,1)}, bf16[96,3840]{1,0:T(8,128)(2,1)}, u32[]{:S(2)}, u32[]{:S(2)}) %collective-permute-start.29) | collective-permute-done | bytes 737312 | tf_op jit(solution)/shard_map/ppermute | solution.py:558
  387.2 8.9 %collective-permute-done.27 = bf16[96,3840]{1,0:T(8,128)(2,1)} collective-permute-done((bf16[96,3840]{1,0:T(8,128)(2,1)}, bf16[96,3840]{1,0:T(8,128)(2,1)}, u32[]{:S(2)}, u32[]{:S(2)}) %collective-permute-start.27) | collective-permute-done | bytes 737312 | tf_op jit(solution)/shard_map/ppermute | solution.py:558
  396.1 1.9 collective-permute-done.28
  398.0 2.5 fusion.28
  401.9 2.1 collective-permute-start.32
  405.1 2.1 collective-permute-done.30
  407.3 6.2 %collective-permute-done.32 = bf16[24,3840]{1,0:T(8,128)(2,1)S(1)} collective-permute-done((bf16[24,3840]{1,0:T(8,128)(2,1)S(1)}, bf16[24,3840]{1,0:T(8,128)(2,1)S(1)}, u32[]{:S(2)}, u32[]{:S(2)}) %collective-permute-start.32) | collective-permute-done | bytes 184352 | tf_op jit(solution)/shard_map/ppermute | solution.py:558
  413.5 6.7 %collective-permute-done.31 = bf16[24,3840]{1,0:T(8,128)(2,1)S(1)} collective-permute-done((bf16[24,3840]{1,0:T(8,128)(2,1)S(1)}, bf16[24,3840]{1,0:T(8,128)(2,1)S(1)}, u32[]{:S(2)}, u32[]{:S(2)}) %collective-permute-start.31) | collective-permute-done | bytes 184352 | tf_op jit(solution)/shard_map/ppermute | solution.py:558
  421.1 1.9 multiply_reduce_fusion
  423.0 5.3 %concatenate.77 = f32[30]{0:T(128)S(1)} concatenate(f32[3]{0:T(128)S(1)} %get-tuple-element.193, f32[1]{0:T(128)} %bitcast.26, f32[1]{0:T(128)} %bitcast.27, f32[1]{0:T(128)} %bitcast.28, f32[8]{0:T(128)S(1)} %get-tuple-element.197, f32[1]{0:T(128)} %bitcast.29, f32[3]{0:T(128)S(1)} %get-tuple-element.192, f32[1]{0:T(128)} %bitcast.68, f32[1]{0:T(128)} %bitcast.83, f32[1]{0:T(128)} %bitcast.84, ...), dimensions={0} | concatenate | bytes 240 | tf_op jit(solution)/shard_map/concatenate | solution.py:765
  429.6 3.2 all-to-all-start
  432.8 15.1 %input_grad.1 = bf16[2048,768]{1,0:T(8,128)(2,1)} custom-call(f32[2048,768]{1,0:T(8,128)} %get-tuple-element.68.gres_ref, bf16[3,768,768]{2,1,0:T(8,128)(2,1)} %get-tuple-element.69.w_ref, bf16[2048,1152]{1,0:T(8,128)(2,1)} %get-tuple-element.73.rest_0_, bf16[2048,1152]{1,0:T(8,128)(2,1)} %get-tuple-element.74.rest_1_), custom_call_target="tpu_custom_call" | custom-call | tf_op jit(solution)/shard_map/input_grad/pallas_call | solution.py:533
  (274 shorter events, 67.5 us)
Async XLA Ops:
  7.2 107.4 %all-gather.2.cloned.1.call-start = ((), (), s32[]{:S(2)}) async-start(), calls=%async_computation.1 | async-start | bytes 10948608 | tf_op jit(solution)/shard_map/all_gather | solution.py:622
  12.8 1.7 collective-permute-start
  14.5 6.9 %collective-permute-start.1 = (bf16[176,384]{1,0:T(8,128)(2,1)S(1)}, bf16[176,384]{1,0:T(8,128)(2,1)S(1)}, u32[]{:S(2)}, u32[]{:S(2)}) collective-permute-start(bf16[176,384]{1,0:T(8,128)(2,1)S(1)} %pad_maximum_fusion.4), channel_id=1, source_target_pairs={{0,8},{1,9},{2,10},{3,11},{4,12},{5,13},{6,14},{7,15},{8,0},{9,1},... | collective-permute-start | bytes 405512 | tf_op jit(solution)/shard_map/ppermute | solution.py:558
  17.5 21.9 %collective-permute-start.3 = (bf16[176,384]{1,0:T(8,128)(2,1)S(1)}, bf16[176,384]{1,0:T(8,128)(2,1)S(1)}, u32[]{:S(2)}, u32[]{:S(2)}) collective-permute-start(bf16[176,384]{1,0:T(8,128)(2,1)S(1)} %pad_maximum_fusion.4), channel_id=1, source_target_pairs={{0,24},{1,25},{2,26},{3,27},{4,28},{5,29},{6,30},{7,31},{8,16},{9,... | collective-permute-start | bytes 405512 | tf_op jit(solution)/shard_map/ppermute | solution.py:558
  19.7 19.7 %collective-permute-start.2 = (bf16[176,384]{1,0:T(8,128)(2,1)S(1)}, bf16[176,384]{1,0:T(8,128)(2,1)S(1)}, u32[]{:S(2)}, u32[]{:S(2)}) collective-permute-start(bf16[176,384]{1,0:T(8,128)(2,1)S(1)} %pad_maximum_fusion.4), channel_id=1, source_target_pairs={{0,16},{1,17},{2,18},{3,19},{4,20},{5,21},{6,22},{7,23},{8,24},{9,... | collective-permute-start | bytes 405512 | tf_op jit(solution)/shard_map/ppermute | solution.py:558
  39.5 20.5 %collective-permute-start.6 = (bf16[608,384]{1,0:T(8,128)(2,1)S(1)}, bf16[608,384]{1,0:T(8,128)(2,1)S(1)}, u32[]{:S(2)}, u32[]{:S(2)}) collective-permute-start(bf16[608,384]{1,0:T(8,128)(2,1)S(1)} %get-tuple-element.236.rest_0_), channel_id=1, source_target_pairs={{0,6},{1,7},{2,4},{3,5},{4,2},{5,3},{6,0},{7,1},{8,14},{9,15},{10,... | collective-permute-start | bytes 1400840 | tf_op jit(solution)/shard_map/ppermute | solution.py:558
  41.7 22.8 %collective-permute-start.5 = (bf16[608,384]{1,0:T(8,128)(2,1)S(1)}, bf16[608,384]{1,0:T(8,128)(2,1)S(1)}, u32[]{:S(2)}, u32[]{:S(2)}) collective-permute-start(bf16[608,384]{1,0:T(8,128)(2,1)S(1)} %get-tuple-element.236.rest_0_), channel_id=1, source_target_pairs={{0,4},{1,5},{2,6},{3,7},{4,0},{5,1},{6,2},{7,3},{8,12},{9,13},{10,... | collective-permute-start | bytes 1400840 | tf_op jit(solution)/shard_map/ppermute | solution.py:558
  42.4 26.8 %collective-permute-start.4 = (bf16[608,384]{1,0:T(8,128)(2,1)S(1)}, bf16[608,384]{1,0:T(8,128)(2,1)S(1)}, u32[]{:S(2)}, u32[]{:S(2)}) collective-permute-start(bf16[608,384]{1,0:T(8,128)(2,1)S(1)} %get-tuple-element.236.rest_0_), channel_id=1, source_target_pairs={{0,2},{1,3},{2,0},{3,1},{4,6},{5,7},{6,4},{7,5},{8,10},{9,11},{10,... | collective-permute-start | bytes 1400840 | tf_op jit(solution)/shard_map/ppermute | solution.py:558
  43.2 28.5 %collective-permute-start.7 = (bf16[608,384]{1,0:T(8,128)(2,1)S(1)}, bf16[608,384]{1,0:T(8,128)(2,1)S(1)}, u32[]{:S(2)}, u32[]{:S(2)}) collective-permute-start(bf16[608,384]{1,0:T(8,128)(2,1)S(1)} %get-tuple-element.236.rest_0_), channel_id=1, source_target_pairs={{0,1},{1,0},{2,3},{3,2},{4,5},{5,4},{6,7},{7,6},{8,9},{9,8},{10,11... | collective-permute-start | bytes 1400840 | tf_op jit(solution)/shard_map/ppermute | solution.py:558
  60.1 11.6 %collective-permute-start.10 = (bf16[608,384]{1,0:T(8,128)(2,1)S(1)}, bf16[608,384]{1,0:T(8,128)(2,1)S(1)}, u32[]{:S(2)}, u32[]{:S(2)}) collective-permute-start(bf16[608,384]{1,0:T(8,128)(2,1)S(1)} %collective-permute-done.6.rest_3_), channel_id=1, source_target_pairs={{0,1},{1,0},{2,3},{3,2},{4,5},{5,4},{6,7},{7,6},{8,9},{9,8},{10,11... | collective-permute-start | bytes 1400840 | tf_op jit(solution)/shard_map/ppermute | solution.py:558
  64.5 7.2 %collective-permute-start.9 = (bf16[608,384]{1,0:T(8,128)(2,1)S(1)}, bf16[608,384]{1,0:T(8,128)(2,1)S(1)}, u32[]{:S(2)}, u32[]{:S(2)}) collective-permute-start(bf16[608,384]{1,0:T(8,128)(2,1)S(1)} %collective-permute-done.5.rest_2_), channel_id=1, source_target_pairs={{0,1},{1,0},{2,3},{3,2},{4,5},{5,4},{6,7},{7,6},{8,9},{9,8},{10,11... | collective-permute-start | bytes 1400840 | tf_op jit(solution)/shard_map/ppermute | solution.py:558
  69.2 2.5 collective-permute-start.8
  276.0 4.5 collective-permute-start.11
  277.1 8.0 %collective-permute-start.18 = (bf16[16,24,1152]{2,1,0:T(8,128)(2,1)}, bf16[16,24,1152]{2,1,0:T(8,128)(2,1)}, u32[]{:S(2)}, u32[]{:S(2)}) collective-permute-start(bf16[16,24,1152]{2,1,0:T(8,128)(2,1)} %get-tuple-element.78), channel_id=1, source_target_pairs={{0,1},{1,0},{2,3},{3,2},{4,5},{5,4},{6,7},{7,6},{8,9},{9,8},{10,11... | collective-permute-start | bytes 2654216 | tf_op jit(solution)/shard_map/ppermute | solution.py:558
  277.5 2.3 collective-permute-start.19
  278.7 54.8 %collective-permute-start.33 = (bf16[16,24,3072]{2,1,0:T(8,128)(2,1)}, bf16[16,24,3072]{2,1,0:T(8,128)(2,1)}, u32[]{:S(2)}, u32[]{:S(2)}) collective-permute-start(bf16[16,24,3072]{2,1,0:T(8,128)(2,1)} %get-tuple-element.85), channel_id=1, source_target_pairs={{0,1},{1,0},{2,3},{3,2},{4,5},{5,4},{6,7},{7,6},{8,9},{9,8},{10,11... | collective-permute-start | bytes 7077896 | tf_op jit(solution)/shard_map/ppermute | solution.py:558
  279.0 85.3 %collective-permute-start.26 = (bf16[16,24,3840]{2,1,0:T(8,128)(2,1)}, bf16[16,24,3840]{2,1,0:T(8,128)(2,1)S(1)}, u32[]{:S(2)}, u32[]{:S(2)}) collective-permute-start(bf16[16,24,3840]{2,1,0:T(8,128)(2,1)} %get-tuple-element.83), channel_id=1, source_target_pairs={{0,1},{1,0},{2,3},{3,2},{4,5},{5,4},{6,7},{7,6},{8,9},{9,8},{10,11... | collective-permute-start | bytes 8847368 | tf_op jit(solution)/shard_map/ppermute | solution.py:558
  282.1 9.3 %collective-permute-start.14 = (bf16[96,1152]{1,0:T(8,128)(2,1)S(1)}, bf16[96,1152]{1,0:T(8,128)(2,1)S(1)}, u32[]{:S(2)}, u32[]{:S(2)}) collective-permute-start(bf16[96,1152]{1,0:T(8,128)(2,1)S(1)} %bitcast.183), channel_id=1, source_target_pairs={{0,6},{1,7},{2,4},{3,5},{4,2},{5,3},{6,0},{7,1},{8,14},{9,15},{10,... | collective-permute-start | bytes 663560 | tf_op jit(solution)/shard_map/ppermute | solution.py:558
  283.7 12.5 %collective-permute-start.12 = (bf16[96,1152]{1,0:T(8,128)(2,1)S(1)}, bf16[96,1152]{1,0:T(8,128)(2,1)S(1)}, u32[]{:S(2)}, u32[]{:S(2)}) collective-permute-start(bf16[96,1152]{1,0:T(8,128)(2,1)S(1)} %bitcast.182), channel_id=1, source_target_pairs={{0,2},{1,3},{2,0},{3,1},{4,6},{5,7},{6,4},{7,5},{8,10},{9,11},{10,... | collective-permute-start | bytes 663560 | tf_op jit(solution)/shard_map/ppermute | solution.py:558
  285.1 11.6 %collective-permute-start.13 = (bf16[96,1152]{1,0:T(8,128)(2,1)S(1)}, bf16[96,1152]{1,0:T(8,128)(2,1)S(1)}, u32[]{:S(2)}, u32[]{:S(2)}) collective-permute-start(bf16[96,1152]{1,0:T(8,128)(2,1)S(1)} %bitcast.181), channel_id=1, source_target_pairs={{0,4},{1,5},{2,6},{3,7},{4,0},{5,1},{6,2},{7,3},{8,12},{9,13},{10,... | collective-permute-start | bytes 663560 | tf_op jit(solution)/shard_map/ppermute | solution.py:558
  291.4 9.9 %collective-permute-start.20 = (bf16[104,1152]{1,0:T(8,128)(2,1)S(1)}, bf16[104,1152]{1,0:T(8,128)(2,1)S(1)}, u32[]{:S(2)}, u32[]{:S(2)}) collective-permute-start(bf16[104,1152]{1,0:T(8,128)(2,1)S(1)} %get-tuple-element.267), channel_id=1, source_target_pairs={{0,2},{1,3},{2,0},{3,1},{4,6},{5,7},{6,4},{7,5},{8,10},{9,11},{10,... | collective-permute-start | bytes 718856 | tf_op jit(solution)/shard_map/ppermute | solution.py:558
  296.2 12.0 %collective-permute-start.21 = (bf16[104,1152]{1,0:T(8,128)(2,1)}, bf16[104,1152]{1,0:T(8,128)(2,1)}, u32[]{:S(2)}, u32[]{:S(2)}) collective-permute-start(bf16[104,1152]{1,0:T(8,128)(2,1)} %get-tuple-element.268), channel_id=1, source_target_pairs={{0,4},{1,5},{2,6},{3,7},{4,0},{5,1},{6,2},{7,3},{8,12},{9,13},{10,... | collective-permute-start | bytes 718856 | tf_op jit(solution)/shard_map/ppermute | solution.py:558
  296.7 16.4 %collective-permute-start.22 = (bf16[104,1152]{1,0:T(8,128)(2,1)}, bf16[104,1152]{1,0:T(8,128)(2,1)S(1)}, u32[]{:S(2)}, u32[]{:S(2)}) collective-permute-start(bf16[104,1152]{1,0:T(8,128)(2,1)} %get-tuple-element.269), channel_id=1, source_target_pairs={{0,6},{1,7},{2,4},{3,5},{4,2},{5,3},{6,0},{7,1},{8,14},{9,15},{10,... | collective-permute-start | bytes 718856 | tf_op jit(solution)/shard_map/ppermute | solution.py:558
  301.3 20.0 %collective-permute-start.15 = (bf16[24,1152]{1,0:T(8,128)(2,1)}, bf16[24,1152]{1,0:T(8,128)(2,1)}, u32[]{:S(2)}, u32[]{:S(2)}) collective-permute-start(bf16[24,1152]{1,0:T(8,128)(2,1)} %get-tuple-element.256), channel_id=1, source_target_pairs={{0,8},{1,9},{2,10},{3,11},{4,12},{5,13},{6,14},{7,15},{8,0},{9,1},... | collective-permute-start | bytes 165896 | tf_op jit(solution)/shard_map/ppermute | solution.py:558
  308.1 14.8 %collective-permute-start.17 = (bf16[24,1152]{1,0:T(8,128)(2,1)}, bf16[24,1152]{1,0:T(8,128)(2,1)}, u32[]{:S(2)}, u32[]{:S(2)}) collective-permute-start(bf16[24,1152]{1,0:T(8,128)(2,1)} %get-tuple-element.257), channel_id=1, source_target_pairs={{0,24},{1,25},{2,26},{3,27},{4,28},{5,29},{6,30},{7,31},{8,16},{9,... | collective-permute-start | bytes 165896 | tf_op jit(solution)/shard_map/ppermute | solution.py:558
  313.2 10.6 %collective-permute-start.16 = (bf16[24,1152]{1,0:T(8,128)(2,1)}, bf16[24,1152]{1,0:T(8,128)(2,1)}, u32[]{:S(2)}, u32[]{:S(2)}) collective-permute-start(bf16[24,1152]{1,0:T(8,128)(2,1)} %get-tuple-element.258), channel_id=1, source_target_pairs={{0,16},{1,17},{2,18},{3,19},{4,20},{5,21},{6,22},{7,23},{8,24},{9,... | collective-permute-start | bytes 165896 | tf_op jit(solution)/shard_map/ppermute | solution.py:558
  321.3 5.4 %collective-permute-start.23 = (bf16[32,1152]{1,0:T(8,128)(2,1)}, bf16[32,1152]{1,0:T(8,128)(2,1)}, u32[]{:S(2)}, u32[]{:S(2)}) collective-permute-start(bf16[32,1152]{1,0:T(8,128)(2,1)} %get-tuple-element.264), channel_id=1, source_target_pairs={{0,8},{1,9},{2,10},{3,11},{4,12},{5,13},{6,14},{7,15},{8,0},{9,1},... | collective-permute-start | bytes 221192 | tf_op jit(solution)/shard_map/ppermute | solution.py:558
  322.9 6.2 %collective-permute-start.24 = (bf16[32,1152]{1,0:T(8,128)(2,1)}, bf16[32,1152]{1,0:T(8,128)(2,1)}, u32[]{:S(2)}, u32[]{:S(2)}) collective-permute-start(bf16[32,1152]{1,0:T(8,128)(2,1)} %get-tuple-element.265), channel_id=1, source_target_pairs={{0,16},{1,17},{2,18},{3,19},{4,20},{5,21},{6,22},{7,23},{8,24},{9,... | collective-permute-start | bytes 221192 | tf_op jit(solution)/shard_map/ppermute | solution.py:558
  323.8 6.6 %collective-permute-start.25 = (bf16[32,1152]{1,0:T(8,128)(2,1)}, bf16[32,1152]{1,0:T(8,128)(2,1)}, u32[]{:S(2)}, u32[]{:S(2)}) collective-permute-start(bf16[32,1152]{1,0:T(8,128)(2,1)} %get-tuple-element.266), channel_id=1, source_target_pairs={{0,24},{1,25},{2,26},{3,27},{4,28},{5,29},{6,30},{7,31},{8,16},{9,... | collective-permute-start | bytes 221192 | tf_op jit(solution)/shard_map/ppermute | solution.py:558
  337.1 15.0 %collective-permute-start.36 = (bf16[96,3072]{1,0:T(8,128)(2,1)}, bf16[96,3072]{1,0:T(8,128)(2,1)}, u32[]{:S(2)}, u32[]{:S(2)}) collective-permute-start(bf16[96,3072]{1,0:T(8,128)(2,1)} %bitcast.73), channel_id=1, source_target_pairs={{0,6},{1,7},{2,4},{3,5},{4,2},{5,3},{6,0},{7,1},{8,14},{9,15},{10,... | collective-permute-start | bytes 1769480 | tf_op jit(solution)/shard_map/ppermute | solution.py:558
  338.5 18.3 %collective-permute-start.34 = (bf16[96,3072]{1,0:T(8,128)(2,1)}, bf16[96,3072]{1,0:T(8,128)(2,1)}, u32[]{:S(2)}, u32[]{:S(2)}) collective-permute-start(bf16[96,3072]{1,0:T(8,128)(2,1)} %bitcast.69), channel_id=1, source_target_pairs={{0,2},{1,3},{2,0},{3,1},{4,6},{5,7},{6,4},{7,5},{8,10},{9,11},{10,... | collective-permute-start | bytes 1769480 | tf_op jit(solution)/shard_map/ppermute | solution.py:558
  339.1 19.1 %collective-permute-start.35 = (bf16[96,3072]{1,0:T(8,128)(2,1)}, bf16[96,3072]{1,0:T(8,128)(2,1)}, u32[]{:S(2)}, u32[]{:S(2)}) collective-permute-start(bf16[96,3072]{1,0:T(8,128)(2,1)} %bitcast.71), channel_id=1, source_target_pairs={{0,4},{1,5},{2,6},{3,7},{4,0},{5,1},{6,2},{7,3},{8,12},{9,13},{10,... | collective-permute-start | bytes 1769480 | tf_op jit(solution)/shard_map/ppermute | solution.py:558
  341.9 111.0 %copy-start.39 = (f32[8,24]{1,0:T(8,128)}, f32[8,24]{1,0:T(8,128)S(1)}, u32[]{:S(2)}) copy-start(f32[8,24]{1,0:T(8,128)S(1)} %get-tuple-element.214) | copy-start | bytes 2308
  341.9 111.0 %copy-start.40 = (f32[8,24]{1,0:T(8,128)}, f32[8,24]{1,0:T(8,128)S(1)}, u32[]{:S(2)}) copy-start(f32[8,24]{1,0:T(8,128)S(1)} %get-tuple-element.215) | copy-start | bytes 2308
  343.8 111.7 %copy-start.13 = (f32[3,24,768]{2,1,0:T(8,128)}, f32[3,24,768]{2,1,0:T(8,128)S(1)}, u32[]{:S(2)}) copy-start(f32[3,24,768]{2,1,0:T(8,128)S(1)} %get-tuple-element.226) | copy-start | bytes 663556
  360.7 8.0 %collective-permute-start.37 = (bf16[24,3072]{1,0:T(8,128)(2,1)S(1)}, bf16[24,3072]{1,0:T(8,128)(2,1)S(1)}, u32[]{:S(2)}, u32[]{:S(2)}) collective-permute-start(bf16[24,3072]{1,0:T(8,128)(2,1)S(1)} %get-tuple-element.253), channel_id=1, source_target_pairs={{0,8},{1,9},{2,10},{3,11},{4,12},{5,13},{6,14},{7,15},{8,0},{9,1},... | collective-permute-start | bytes 442376 | tf_op jit(solution)/shard_map/ppermute | solution.py:558
  361.3 9.8 %collective-permute-start.39 = (bf16[24,3072]{1,0:T(8,128)(2,1)S(1)}, bf16[24,3072]{1,0:T(8,128)(2,1)S(1)}, u32[]{:S(2)}, u32[]{:S(2)}) collective-permute-start(bf16[24,3072]{1,0:T(8,128)(2,1)S(1)} %get-tuple-element.254), channel_id=1, source_target_pairs={{0,24},{1,25},{2,26},{3,27},{4,28},{5,29},{6,30},{7,31},{8,16},{9,... | collective-permute-start | bytes 442376 | tf_op jit(solution)/shard_map/ppermute | solution.py:558
  363.3 10.7 %collective-permute-start.38 = (bf16[24,3072]{1,0:T(8,128)(2,1)S(1)}, bf16[24,3072]{1,0:T(8,128)(2,1)S(1)}, u32[]{:S(2)}, u32[]{:S(2)}) collective-permute-start(bf16[24,3072]{1,0:T(8,128)(2,1)S(1)} %get-tuple-element.255), channel_id=1, source_target_pairs={{0,16},{1,17},{2,18},{3,19},{4,20},{5,21},{6,22},{7,23},{8,24},{9,... | collective-permute-start | bytes 442376 | tf_op jit(solution)/shard_map/ppermute | solution.py:558
  366.5 20.6 %collective-permute-start.29 = (bf16[96,3840]{1,0:T(8,128)(2,1)}, bf16[96,3840]{1,0:T(8,128)(2,1)}, u32[]{:S(2)}, u32[]{:S(2)}) collective-permute-start(bf16[96,3840]{1,0:T(8,128)(2,1)} %bitcast.59), channel_id=1, source_target_pairs={{0,6},{1,7},{2,4},{3,5},{4,2},{5,3},{6,0},{7,1},{8,14},{9,15},{10,... | collective-permute-start | bytes 2211848 | tf_op jit(solution)/shard_map/ppermute | solution.py:558
  367.2 28.9 %collective-permute-start.27 = (bf16[96,3840]{1,0:T(8,128)(2,1)}, bf16[96,3840]{1,0:T(8,128)(2,1)}, u32[]{:S(2)}, u32[]{:S(2)}) collective-permute-start(bf16[96,3840]{1,0:T(8,128)(2,1)} %bitcast.55), channel_id=1, source_target_pairs={{0,2},{1,3},{2,0},{3,1},{4,6},{5,7},{6,4},{7,5},{8,10},{9,11},{10,... | collective-permute-start | bytes 2211848 | tf_op jit(solution)/shard_map/ppermute | solution.py:558
  368.6 29.3 %collective-permute-start.28 = (bf16[96,3840]{1,0:T(8,128)(2,1)}, bf16[96,3840]{1,0:T(8,128)(2,1)}, u32[]{:S(2)}, u32[]{:S(2)}) collective-permute-start(bf16[96,3840]{1,0:T(8,128)(2,1)} %bitcast.57), channel_id=1, source_target_pairs={{0,4},{1,5},{2,6},{3,7},{4,0},{5,1},{6,2},{7,3},{8,12},{9,13},{10,... | collective-permute-start | bytes 2211848 | tf_op jit(solution)/shard_map/ppermute | solution.py:558
  400.6 6.7 %collective-permute-start.30 = (bf16[24,3840]{1,0:T(8,128)(2,1)S(1)}, bf16[24,3840]{1,0:T(8,128)(2,1)S(1)}, u32[]{:S(2)}, u32[]{:S(2)}) collective-permute-start(bf16[24,3840]{1,0:T(8,128)(2,1)S(1)} %get-tuple-element.250), channel_id=1, source_target_pairs={{0,8},{1,9},{2,10},{3,11},{4,12},{5,13},{6,14},{7,15},{8,0},{9,1},... | collective-permute-start | bytes 552968 | tf_op jit(solution)/shard_map/ppermute | solution.py:558
  401.9 11.6 %collective-permute-start.32 = (bf16[24,3840]{1,0:T(8,128)(2,1)S(1)}, bf16[24,3840]{1,0:T(8,128)(2,1)S(1)}, u32[]{:S(2)}, u32[]{:S(2)}) collective-permute-start(bf16[24,3840]{1,0:T(8,128)(2,1)S(1)} %get-tuple-element.251), channel_id=1, source_target_pairs={{0,24},{1,25},{2,26},{3,27},{4,28},{5,29},{6,30},{7,31},{8,16},{9,... | collective-permute-start | bytes 552968 | tf_op jit(solution)/shard_map/ppermute | solution.py:558
  404.0 16.2 %collective-permute-start.31 = (bf16[24,3840]{1,0:T(8,128)(2,1)S(1)}, bf16[24,3840]{1,0:T(8,128)(2,1)S(1)}, u32[]{:S(2)}, u32[]{:S(2)}) collective-permute-start(bf16[24,3840]{1,0:T(8,128)(2,1)S(1)} %get-tuple-element.252), channel_id=1, source_target_pairs={{0,16},{1,17},{2,18},{3,19},{4,20},{5,21},{6,22},{7,23},{8,24},{9,... | collective-permute-start | bytes 552968 | tf_op jit(solution)/shard_map/ppermute | solution.py:558
  405.1 53.6 %copy-start.7 = (f32[24,3072]{1,0:T(8,128)}, f32[24,3072]{1,0:T(8,128)S(1)}, u32[]{:S(2)}) copy-start(f32[24,3072]{1,0:T(8,128)S(1)} %get-tuple-element.218) | copy-start | bytes 884740
  405.1 53.6 %copy-start.8 = (f32[24,3072]{1,0:T(8,128)}, f32[24,3072]{1,0:T(8,128)S(1)}, u32[]{:S(2)}) copy-start(f32[24,3072]{1,0:T(8,128)S(1)} %get-tuple-element.219) | copy-start | bytes 884740
  423.0 34.0 %copy-start.10 = (f32[96,768]{1,0:T(8,128)}, f32[96,768]{1,0:T(8,128)S(1)}, u32[]{:S(2)}) copy-start(f32[96,768]{1,0:T(8,128)S(1)} %get-tuple-element.217) | copy-start | bytes 884740
  429.6 18.3 %all-to-all-start = ((f32[32,1,128]{2,1,0:T(1,128)}), f32[32,1,128]{2,1,0:T(1,128)S(1)}, u32[]{:S(2)}, u32[]{:S(2)}) async-start(f32[32,1,128]{2,1,0:T(1,128)} %broadcast_in_dim.49), calls=%async_computation | async-start | bytes 32768 | tf_op jit(solution)/shard_map/all_to_all | solution.py:667
  (45 other events, 491.4 us)
Sparse Core Ops, SparseCore 0:
  12.1 102.5 all-gather.1

commit v2 on v1

--- a/solution.py
+++ b/solution.py
@@ -7,16 +7,7 @@
 from jax.experimental.pallas import tpu as pltpu
 from jax.sharding import PartitionSpec as P
 
-STEP = 7
 ALL = ("gx", "gy")
-norm_eps = 1e-12
-beta_one = 0.5
-beta_two = 0.5
-adam_eps = 1e-06
-decay_rate = 0.01
-learn_rate = 0.3
-ema_rate = 0.5
-ratio_eps = 1e-06
 
 HEADS = 12
 HD = 64
@@ -33,6 +24,10 @@
 
 def dot(a, b, dims=NN):
     return lax.dot_general(a, b, dims, preferred_element_type=f32)
+
+
+def cost(us):
+    return pl.CostEstimate(flops=int(us * 1.1e9), bytes_accessed=int(us * 1e6), transcendentals=0)
 
 
 def seg_of(bounds_ref, row, shape, dim):
@@ -91,7 +86,7 @@
     where_ref, bounds_ref, x_ref, vec_ref, *rest
 ):
     raws = rest[:8]
-    qkv_ref, o_ref, lse_ref, wout_ref, w_scr, qkv_scr, sem, out_sem = rest[8:]
+    qkv_ref, o_ref, probs_ref, share_ref, wout_ref, w_scr, qkv_scr, sem, out_sem = rest[8:]
     row = pl.program_id(0)
     length = x_ref.shape[0]
     width = x_ref.shape[1]
@@ -118,31 +113,38 @@
         kp = qkv_scr[:, pl.ds(width + at, PAIR)]
         vt = qkv_scr[:, pl.ds(2 * width + at, PAIR)].T
         outs = []
-        logs = []
-        for even in (True, False):
-            pick = low if even else jnp.logical_not(low)
+        tops = []
+        for side in range(2):
+            pick = low if side == 0 else jnp.logical_not(low)
             qa = jnp.where(pick, qp, query_cols)
             ka = jnp.where(pick, kp, key_cols)
-            if even:
+            if side == 0:
                 va = jnp.where(sub < HD, vt, (sub == HD).astype(bf16))
             else:
                 va = jnp.where(sub < HD, (sub == 0).astype(bf16), vt)
             blocks = []
-            lse_blocks = []
+            shares = []
             for b in range(length // step):
                 first, last = key_span(b, step, reach, length)
                 scores = dot(ka[first:last], qa[b * step : (b + 1) * step], NT)
                 peak = jnp.max(scores, axis=0, keepdims=True)
                 probs = jnp.exp(scores - peak).astype(bf16)
+                cols = slice(side * length + b * step, side * length + (b + 1) * step)
+                probs_ref[0, pair, first:last, cols] = probs
+                if first > 0:
+                    probs_ref[0, pair, 0:first, cols] = jnp.zeros((first, step), bf16)
+                if last < length:
+                    probs_ref[0, pair, last:length, cols] = jnp.zeros((length - last, step), bf16)
                 mixed = dot(va[:, first:last], probs)
-                total = mixed[HD : HD + 1] if even else mixed[0:1]
-                mine = mixed[:HD] if even else mixed[HD:]
-                blocks.append((mine * (1.0 / total)).astype(bf16))
-                lse_blocks.append(peak + jnp.log(total))
+                total = mixed[HD : HD + 1] if side == 0 else mixed[0:1]
+                mine = mixed[:HD] if side == 0 else mixed[HD:]
+                share = 1.0 / total
+                blocks.append((mine * share).astype(bf16))
+                shares.append(share)
             outs.append(jnp.concatenate(blocks, axis=1))
-            logs.append(jnp.concatenate(lse_blocks, axis=1))
+            tops.append(jnp.concatenate(shares, axis=1))
         o_ref[:, pl.ds(at, PAIR)] = jnp.concatenate(outs, axis=0).T
-        lse_ref[0, pl.ds(pair, 1)] = jnp.concatenate(logs, axis=0)[None]
+        share_ref[0, pl.ds(pair, 1)] = jnp.concatenate(tops, axis=0)[None]
         return 0
 
     lax.fori_loop(0, width // PAIR, pair_body, 0, unroll=True)
@@ -171,6 +173,7 @@
             out_specs=[
                 pl.BlockSpec((length, 3 * width), lambda r, *_: (r, 0)),
                 pl.BlockSpec((length, width), lambda r, *_: (r, 0)),
+                pl.BlockSpec((1, pairs, length, 2 * length), lambda r, *_: (r, 0, 0, 0)),
                 pl.BlockSpec((1, pairs, 2, length), lambda r, *_: (r, 0, 0, 0)),
                 any_spec,
             ],
@@ -184,10 +187,12 @@
         out_shape=[
             jax.ShapeDtypeStruct((tok, 3 * width), bf16),
             jax.ShapeDtypeStruct((tok, width), bf16),
+            jax.ShapeDtypeStruct((rows, pairs, length, 2 * length), bf16),
             jax.ShapeDtypeStruct((rows, pairs, 2, length), f32),
             jax.ShapeDtypeStruct((3, width, width), bf16),
         ],
         compiler_params=pltpu.CompilerParams(vmem_limit_bytes=56 * MIB),
+        cost_estimate=cost(30),
         name="attend_forward",
     )(where, bounds, tokens, vec_rows, *raws)
 
@@ -213,7 +218,7 @@
 
 def gelu_both(z):
     size = jnp.abs(z)
-    t = pl.reciprocal(1.0 + (0.3275911 * 0.5**0.5) * size, approx=APPROX)
+    t = pl.reciprocal(1.0 + (0.3275911 * 0.5**0.5) * size, approx=False)
     e = jnp.exp(-0.5 * z * z)
     poly = 0.5 * 1.061405429
     for a in (-1.453152027, 1.421413741, -0.284496736, 0.254829592):
@@ -223,15 +228,14 @@
     return z * cdf, cdf + z * e * 0.3989422804014327
 
 
-APPROX = False
-FC = 768
 SLOTS = 4
+EARLY = 3
 
 
 def middle_kernel(
     where_ref, mixed_ref, x_ref, cot_ref, vec_ref, packed_ref,
-    out_ref, gmixed_ref, gres_ref, gvec_ref, mine_a, theirs_a, mine_b, theirs_b,
-    w1, w2, wo, acc1, acc2, acco, accv, act, slope, stage_a, stage_b, in_sem, out_sem,
+    out_ref, gmixed_ref, gres_ref, gvec_ref, down_ref, mine_ref, theirs_0, theirs_1, theirs_2, theirs_3,
+    w1, w2, wo, acc1, acc2, acco, accv, act, slope, stage, tall, in_sem, out_sem, tall_sem,
 ):
     step = pl.program_id(0)
     width = x_ref.shape[1]
@@ -262,16 +266,17 @@
     hidden = unit_one * vec_ref[3:4, :] + vec_ref[4:5, :]
     hidden_low = hidden.astype(bf16)
     ffn = hidden + vec_ref[5:6, :]
-    for j in range(w1.shape[1] // FC):
-        cols = slice(j * FC, (j + 1) * FC)
-        at = j * FC // width
-        inner = slice(j * FC - at * width, (j + 1) * FC - at * width)
-        z = dot(hidden_low, w1[:, cols]) + vec_ref[8 + at : 9 + at, inner]
+    z = dot(hidden_low, w1[:, 0:width]) + vec_ref[8:9, :]
+    for j in range(chunks):
+        cols = slice(j * width, (j + 1) * width)
+        if j + 1 < chunks:
+            z_next = dot(hidden_low, w1[:, (j + 1) * width : (j + 2) * width]) + vec_ref[9 + j : 10 + j, :]
         g, d = gelu_both(z)
         g = g.astype(bf16)
         act[:, cols] = g
         slope[:, cols] = d.astype(slope.dtype)
         ffn += dot(g, w2[cols, :])
+        z = z_next
     unit_two, scale_two = norm_parts(ffn)
     out_ref[...] = (unit_two * vec_ref[6:7, :] + vec_ref[7:8, :]).astype(bf16)
     grad = cot_ref[...].astype(f32)
@@ -282,12 +287,10 @@
     accv[5] += fold(grad_ffn.astype(f32))
     grad_hidden = grad_two
     hidden_t = hidden_low.T
-    for j in range(w1.shape[1] // FC):
-        cols = slice(j * FC, (j + 1) * FC)
-        at = j * FC // width
-        inner = slice(j * FC - at * width, (j + 1) * FC - at * width)
+    for j in range(chunks):
+        cols = slice(j * width, (j + 1) * width)
         gz = (dot(grad_ffn, w2[cols, :], NT) * slope[:, cols].astype(f32)).astype(bf16)
-        accv[8 + at, :, inner] += fold(gz.astype(f32))
+        accv[8 + j] += fold(gz.astype(f32))
         acc2[cols, :] += dot(act[:, cols], grad_ffn, TN)
         acc1[:, cols] += dot(hidden_t, gz)
         grad_hidden += dot(gz, w1[:, cols], NT)
@@ -303,41 +306,58 @@
     @pl.when(step == pl.num_programs(0) - 1)
     def _():
         gvec_ref[...] = jnp.sum(accv[...], axis=1)
-        part = stage_a.shape[1]
-        amount = mine_a.shape[0]
-
-        def send(n, side, dst_a, dst_b, wait):
+        part = stage.shape[1]
+        amount = mine_ref.shape[0]
+        ff = chunks * width
+
+        def send(n, side, dst, at, started):
             core = where_ref[1] if side == 0 else 1 - where_ref[1]
             row = pl.multiple_of((where_ref[2 + n] * 2 + core) * part, 8)
             rows = pl.ds(row, part)
-            slot = side + 2 * lax.rem(n, SLOTS)
-            copy_a = pltpu.make_async_copy(stage_a.at[slot], dst_a.at[n], out_sem.at[slot, 0])
-            copy_b = pltpu.make_async_copy(stage_b.at[slot], dst_b.at[n], out_sem.at[slot, 1])
-
-            @pl.when(wait)
+            slot = side * SLOTS + lax.rem(n, SLOTS)
+            copy = pltpu.make_async_copy(stage.at[slot], dst.at[at], out_sem.at[slot])
+
+            @pl.when(started)
             def _():
-                copy_a.wait()
-                copy_b.wait()
-
-            stage_a[slot] = acc1[rows, :].astype(bf16)
-            for j in range(chunks):
-                stage_b[slot, :, j * width : (j + 1) * width] = acc2[
+                copy.wait()
+
+            stage[slot, :, :ff] = acc1[rows, :].astype(bf16)
+            stage[slot, :, ff : ff + width] = acco[rows, :].astype(bf16)
+            for j in range(EARLY, chunks):
+                spot = ff + (1 + j - EARLY) * width
+                stage[slot, :, spot : spot + width] = acc2[
                     pl.ds(pl.multiple_of(j * width + row, 8), part), :
                 ].astype(bf16)
-            stage_b[slot, :, chunks * width :] = acco[rows, :].astype(bf16)
-            copy_a.start()
-            copy_b.start()
-            return copy_a, copy_b
-
-        def body(n, _):
-            send(n, 1, theirs_a, theirs_b, n >= SLOTS)
-            send(n, 0, mine_a, mine_b, n >= SLOTS)
+            copy.start()
+
+        depth = tall.shape[1]
+
+        def send_down(n, _):
+            slot = lax.rem(n, 4)
+            copy = pltpu.make_async_copy(
+                tall.at[slot], down_ref.at[pl.ds(pl.multiple_of(n * depth, depth), depth), :], tall_sem.at[slot]
+            )
+
+            @pl.when(n >= 4)
+            def _():
+                copy.wait()
+
+            for j in range(EARLY):
+                tall[slot, :, j * width : (j + 1) * width] = acc2[
+                    pl.ds(pl.multiple_of(j * width + n * depth, depth), depth), :
+                ].astype(bf16)
+            copy.start()
             return 0
 
-        lax.fori_loop(0, amount, body, 0)
+        lax.fori_loop(0, width // depth, send_down, 0)
+
+        for xy, dst in ((1, theirs_1), (2, theirs_2), (3, theirs_3), (0, theirs_0)):
+            lax.fori_loop(0, 4, lambda z, _: send(4 * xy + z, 1, dst, z, xy != 1) or 0, 0)
+        lax.fori_loop(0, amount, lambda n, _: send(n, 0, mine_ref, n, n >= SLOTS) or 0, 0)
         for slot in range(2 * SLOTS):
-            pltpu.make_async_copy(stage_a.at[slot], mine_a.at[0], out_sem.at[slot, 0]).wait()
-            pltpu.make_async_copy(stage_b.at[slot], mine_b.at[0], out_sem.at[slot, 1]).wait()
+            pltpu.make_async_copy(stage.at[slot], mine_ref.at[0], out_sem.at[slot]).wait()
+        for slot in range(4):
+            pltpu.make_async_copy(tall.at[slot], down_ref.at[pl.ds(0, depth), :], tall_sem.at[slot]).wait()
 
 
 def middle(where, mixed, tokens, cotangent, vec_rows, packed, block=256):
@@ -349,13 +369,14 @@
     row_spec = pl.BlockSpec((block, width), lambda r, *_: (r, 0))
     vec_spec = pl.BlockSpec((vec_rows.shape[0], width), lambda r, *_: (0, 0))
     ff = chunks * width
+    late = ff + (1 + chunks - EARLY) * width
     return pl.pallas_call(
         middle_kernel,
         grid_spec=pltpu.PrefetchScalarGridSpec(
             num_scalar_prefetch=1,
             grid=(tok // block,),
             in_specs=[row_spec, row_spec, row_spec, vec_spec, any_spec],
-            out_specs=[row_spec, row_spec, row_spec, vec_spec] + [any_spec] * 4,
+            out_specs=[row_spec, row_spec, row_spec, vec_spec] + [any_spec] * 6,
             scratch_shapes=[
                 pltpu.VMEM((width, ff), bf16),
                 pltpu.VMEM((ff, width), bf16),
@@ -366,10 +387,11 @@
                 pltpu.VMEM((vec_rows.shape[0], 8, width), f32),
                 pltpu.VMEM((block, ff), bf16),
                 pltpu.VMEM((block, ff), bf16),
-                pltpu.VMEM((2 * SLOTS, part, ff), bf16),
-                pltpu.VMEM((2 * SLOTS, part, ff + width), bf16),
+                pltpu.VMEM((2 * SLOTS, part, late), bf16),
+                pltpu.VMEM((4, 64, EARLY * width), bf16),
                 pltpu.SemaphoreType.DMA,
-                pltpu.SemaphoreType.DMA((2 * SLOTS, 2)),
+                pltpu.SemaphoreType.DMA((2 * SLOTS,)),
+                pltpu.SemaphoreType.DMA((4,)),
             ],
         ),
         out_shape=[
@@ -377,25 +399,25 @@
             jax.ShapeDtypeStruct((tok, width), bf16),
             jax.ShapeDtypeStruct((tok, width), f32),
             jax.ShapeDtypeStruct(vec_rows.shape, f32),
-            jax.ShapeDtypeStruct((chips, part, ff), bf16),
-            jax.ShapeDtypeStruct((chips, part, ff), bf16),
-            jax.ShapeDtypeStruct((chips, part, ff + width), bf16),
-            jax.ShapeDtypeStruct((chips, part, ff + width), bf16),
-        ],
+            jax.ShapeDtypeStruct((width, EARLY * width), bf16),
+            jax.ShapeDtypeStruct((chips, part, late), bf16),
+        ]
+        + [jax.ShapeDtypeStruct((4, part, late), bf16)] * 4,
         compiler_params=pltpu.CompilerParams(vmem_limit_bytes=60 * MIB),
+        cost_estimate=cost(104),
         name="middle",
     )(where, mixed, tokens, cotangent, vec_rows, packed)
 
 
 def attend_backward_kernel(
-    where_ref, bounds_ref, x_ref, q_ref, k_ref, v_ref, mixed_ref, gmixed_ref, lse_ref,
+    where_ref, x_ref, q_ref, k_ref, v_ref, mixed_ref, gmixed_ref, probs_ref, share_ref,
     gqkv_ref, gbias_ref, mine_ref, theirs_ref,
-    acc, accb, probs_scr, grads_scr, stage, out_sem,
+    acc, accb, grads_scr, gscr, stage, out_sem,
 ):
     row = pl.program_id(0)
     length, width = q_ref.shape
     pairs = width // PAIR
-    low, query_cols, key_cols = seg_columns(bounds_ref, row, length)
+    low = lax.broadcasted_iota(jnp.int32, (length, PAIR), 1) < HD
     step = 128
     reach = 256
 
@@ -403,12 +425,20 @@
     def _():
         acc[...] = jnp.zeros_like(acc)
         accb[...] = jnp.zeros_like(accb)
-        probs_scr[...] = jnp.zeros_like(probs_scr)
         grads_scr[...] = jnp.zeros_like(grads_scr)
 
-    head_of = lax.broadcasted_iota(jnp.int32, (8, width), 1) // HD
-    pick_head = (head_of == lax.broadcasted_iota(jnp.int32, (8, width), 0)).astype(bf16)
-    product = gmixed_ref[...].astype(f32) * mixed_ref[...].astype(f32)
+    heads = -(-width // HD // 8) * 8
+    head_of = lax.broadcasted_iota(jnp.int32, (heads, width), 1) // HD
+    pick_head = (head_of == lax.broadcasted_iota(jnp.int32, (heads, width), 0)).astype(bf16)
+    share = jnp.concatenate([share_ref[0, p] for p in range(pairs)], axis=0)
+    if heads > 2 * pairs:
+        share = jnp.concatenate([share, jnp.zeros((heads - 2 * pairs, length), f32)], axis=0)
+    upper = share.astype(bf16)
+    lower = (share - upper.astype(f32)).astype(bf16)
+    spread = dot(upper, pick_head, TN) + dot(lower, pick_head, TN)
+    scaled = (gmixed_ref[...].astype(f32) * spread).astype(bf16)
+    gscr[...] = scaled
+    product = scaled.astype(f32) * mixed_ref[...].astype(f32)
     upper = product.astype(bf16)
     lower = (product - upper.astype(f32)).astype(bf16)
     means = dot(pick_head, upper, NT) + dot(pick_head, lower, NT)
@@ -416,23 +446,18 @@
 
     for pair in range(pairs):
         at = slice(pair * PAIR, (pair + 1) * PAIR)
-        qp, kp, vp, gp = q_ref[:, at], k_ref[:, at], v_ref[:, at], gmixed_ref[:, at]
+        qp, kp, vp, gp = q_ref[:, at], k_ref[:, at], v_ref[:, at], gscr[:, at]
         kt = kp.T
         for side in range(2):
             pick = low if side == 0 else jnp.logical_not(low)
-            qa = jnp.where(pick, qp, query_cols)
-            ka = jnp.where(pick, kp, key_cols)
             va = jnp.where(pick, vp, none)
             for b in range(length // step):
                 first, last = key_span(b, step, reach, length)
                 block = slice(b * step, (b + 1) * step)
                 cols = slice(side * length + b * step, side * length + (b + 1) * step)
-                scores = dot(ka[first:last], qa[block], NT)
-                probs = jnp.exp(scores - lse_ref[0, pair, side : side + 1, block])
                 gprobs = dot(va[first:last], gp[block], NT)
                 head = 2 * pair + side
-                grads = probs * (gprobs - means[head : head + 1, block])
-                probs_scr[first:last, cols] = probs.astype(bf16)
+                grads = probs_ref[0, pair, first:last, cols].astype(f32) * (gprobs - means[head : head + 1, block])
                 grads_scr[first:last, cols] = grads.astype(bf16)
         gq_t = jnp.concatenate(
             [dot(kt[:HD], grads_scr[:, :length]), dot(kt[HD:], grads_scr[:, length:])], axis=0
@@ -441,7 +466,7 @@
         both_q = jnp.concatenate([jnp.where(low, qp, none), jnp.where(low, none, qp)], axis=0)
         both_g = jnp.concatenate([jnp.where(low, gp, none), jnp.where(low, none, gp)], axis=0)
         gk = dot(grads_scr[...], both_q).astype(bf16)
-        gv = dot(probs_scr[...], both_g).astype(bf16)
+        gv = dot(probs_ref[0, pair], both_g).astype(bf16)
         for s, part in enumerate((gq, gk, gv)):
             spot = slice(s * width + pair * PAIR, s * width + (pair + 1) * PAIR)
             gqkv_ref[:, spot] = part
@@ -472,8 +497,8 @@
         pltpu.make_async_copy(stage.at[pl.ds(amount, amount)], theirs_ref, out_sem).wait()
 
 
-def attend_backward(where, bounds, tokens, qkv, mixed, gmixed, lse, group, groups):
-    rows = bounds.shape[0]
+def attend_backward(where, tokens, qkv, mixed, gmixed, probs, share, group, groups):
+    rows = probs.shape[0]
     tok, model = tokens.shape
     length = tok // rows
     width = model // groups
@@ -485,11 +510,12 @@
     return pl.pallas_call(
         attend_backward_kernel,
         grid_spec=pltpu.PrefetchScalarGridSpec(
-            num_scalar_prefetch=2,
+            num_scalar_prefetch=1,
             grid=(rows,),
             in_specs=[
                 pl.BlockSpec((length, model), lambda r, *_: (r, 0)),
                 own(0), own(1), own(2), own(0), own(0),
+                pl.BlockSpec((1, pairs, length, 2 * length), lambda r, *_: (r, group, 0, 0)),
                 pl.BlockSpec((1, pairs, 2, length), lambda r, *_: (r, group, 0, 0)),
             ],
             out_specs=[
@@ -502,7 +528,7 @@
                 pltpu.VMEM((model, 3 * width), f32),
                 pltpu.VMEM((8, 3 * width), f32),
                 pltpu.VMEM((length, 2 * length), bf16),
-                pltpu.VMEM((length, 2 * length), bf16),
+                pltpu.VMEM((length, width), bf16),
                 pltpu.VMEM((2 * chips, part, 3 * width), bf16),
                 pltpu.SemaphoreType.DMA,
             ],
@@ -514,8 +540,9 @@
             jax.ShapeDtypeStruct((chips, part, 3 * width), bf16),
         ],
         compiler_params=pltpu.CompilerParams(vmem_limit_bytes=56 * MIB),
+        cost_estimate=cost(57 // groups),
         name="attend_backward",
-    )(where, bounds, tokens, qkv, qkv, qkv, mixed, gmixed, lse)
+    )(where, tokens, qkv, qkv, qkv, mixed, gmixed, probs, share)
 
 
 def input_grad_kernel(gres_ref, w_ref, *rest):
@@ -541,8 +568,235 @@
         out_specs=pl.BlockSpec((block, model), lambda r: (r, 0)),
         out_shape=jax.ShapeDtypeStruct((tok, model), bf16),
         compiler_params=pltpu.CompilerParams(vmem_limit_bytes=56 * MIB),
+        cost_estimate=cost(0.1),
         name="input_grad",
     )(gres, weights, *parts)
+
+
+beta_one = 0.5
+beta_two = 0.5
+adam_eps = 1e-06
+decay_rate = 0.01
+learn_rate = 0.3
+ema_rate = 0.5
+ratio_eps = 1e-06
+STEP = 7
+
+
+def whole_sum(v):
+    return jnp.sum(jnp.sum(v, axis=0, keepdims=True), axis=1, keepdims=True)
+
+
+def spread_vec(vec, part):
+    return jnp.concatenate([vec[:, c * 128 : (c + 1) * 128] for c in range(vec.shape[1] // 128)], axis=0)
+
+
+def joined_vec(rows):
+    return jnp.concatenate([rows[16 * c : 16 * c + 16] for c in range(rows.shape[0] // 16)], axis=1)
+
+
+def near_kernel(mine_ref, came_ref, vec_ref, vec_came_ref, *sent_refs):
+    part, width = mine_ref.shape[1:]
+    vec = spread_vec(vec_ref[...] + vec_came_ref[...], part)
+    for xy in range(3):
+        for z in range(4):
+            at = 4 * xy + 4 + z
+            sent_refs[xy][z, :, :width] = (mine_ref[at].astype(f32) + came_ref[at].astype(f32)).astype(bf16)
+            sent_refs[xy][z, :, width:] = vec[z * part : (z + 1) * part].astype(bf16)
+
+
+def near(mine, came, vec, vec_came):
+    chips, part, width = mine.shape
+    return pl.pallas_call(
+        near_kernel,
+        out_shape=[jax.ShapeDtypeStruct((4, part, width + 128), bf16)] * 3,
+        compiler_params=pltpu.CompilerParams(vmem_limit_bytes=56 * MIB),
+        cost_estimate=cost(0.1),
+        name="near",
+    )(mine, came, vec, vec_came)
+
+
+def line_kernel(with_vec, *refs):
+    mine_ref, came_ref = refs[:2]
+    parts = refs[2:5]
+    refs = refs[5:]
+    if with_vec:
+        vec_ref, vec_came_ref = refs[:2]
+        refs = refs[2:]
+    part, width = mine_ref.shape[1:]
+    if with_vec:
+        vec = spread_vec(vec_ref[...] + vec_came_ref[...], part)
+        blocks = []
+        for z in range(4):
+            block = vec[z * part : (z + 1) * part]
+            for p in parts:
+                block = block + p[z, :, width:].astype(f32)
+            blocks.append(block)
+        low = jnp.concatenate(blocks, axis=1).astype(bf16)
+        refs[4][...] = joined_vec(jnp.concatenate(blocks, axis=0))
+    for z in range(4):
+        rows = mine_ref[z].astype(f32) + came_ref[z].astype(f32)
+        for p in parts:
+            rows = rows + p[z, :, :width].astype(f32)
+        if z == 0:
+            refs[0][...] = rows
+        else:
+            refs[z][:, :width] = rows.astype(bf16)
+            if with_vec:
+                refs[z][:, width:] = low
+
+
+def line(mine, came, parts, vecs=()):
+    chips, part, width = mine.shape
+    wide = width + (512 if vecs else 0)
+    full = lambda a: pl.BlockSpec(a.shape, lambda i: (0,) * a.ndim)
+    first = pl.BlockSpec((4, part, width), lambda i: (0, 0, 0))
+    shapes = [jax.ShapeDtypeStruct((part, width), f32)] + [jax.ShapeDtypeStruct((part, wide), bf16)] * 3
+    if vecs:
+        shapes.append(jax.ShapeDtypeStruct(vecs[0].shape, f32))
+    return pl.pallas_call(
+        functools.partial(line_kernel, bool(vecs)),
+        grid=(1,),
+        in_specs=[first, first] + [full(p) for p in parts] + [full(v) for v in vecs],
+        out_specs=[full(o) for o in shapes],
+        out_shape=shapes,
+        compiler_params=pltpu.CompilerParams(vmem_limit_bytes=56 * MIB),
+        cost_estimate=cost(0.1),
+        name="line",
+    )(mine, came, *parts, *vecs)
+
+
+def own_grads_kernel(amount, where_ref, rows_ref, vec_ref, *refs):
+    parts = refs[:amount]
+    gq_ref, gv_ref, gb_ref = refs[amount:]
+    part, width = rows_ref.shape
+    model = width // 3
+    rows = rows_ref[...]
+    for p in parts:
+        rows = rows + p[:, :width].astype(f32)
+    for s in range(3):
+        gq_ref[s] = rows[:, s * model : (s + 1) * model]
+    vec = vec_ref[...]
+    if amount:
+        blocks = []
+        for z in range(4):
+            block = jnp.zeros((part, 128), f32)
+            for p in parts:
+                block = block + p[:, width + z * 128 : width + (z + 1) * 128].astype(f32)
+            blocks.append(block)
+        vec = vec + joined_vec(jnp.concatenate(blocks, axis=0))
+    first = where_ref[0] * part
+    chunks = gb_ref.shape[1] // part
+
+    def picked(values, count, repeat):
+        place = lax.broadcasted_iota(jnp.int32, (model, count), 0)
+        wanted = first + lax.broadcasted_iota(jnp.int32, (model, count), 1) // repeat
+        pick = jnp.where(place == wanted, 1.0, 0.0)
+        return lax.dot_general(values, pick, NN, precision=lax.Precision.HIGHEST, preferred_element_type=f32)
+
+    gv_ref[...] = picked(vec[0:8], part, 1)
+    spread = picked(vec[8:16], chunks * part, chunks)
+    row = lax.broadcasted_iota(jnp.int32, spread.shape, 0)
+    lane = lax.broadcasted_iota(jnp.int32, spread.shape, 1)
+    gb_ref[...] = jnp.sum(jnp.where(lane % chunks == row, spread, 0.0), axis=0, keepdims=True)
+
+
+def own_grads(index, rows, vec, parts, chunks):
+    part, width = rows.shape
+    model = width // 3
+    spec = pl.BlockSpec(memory_space=pltpu.VMEM)
+    return pl.pallas_call(
+        functools.partial(own_grads_kernel, len(parts)),
+        in_specs=[pl.BlockSpec(memory_space=pltpu.SMEM)] + [spec] * (2 + len(parts)),
+        out_specs=[spec] * 3,
+        out_shape=[
+            jax.ShapeDtypeStruct((3, part, model), f32),
+            jax.ShapeDtypeStruct((8, part), f32),
+            jax.ShapeDtypeStruct((1, chunks * part), f32),
+        ],
+        compiler_params=pltpu.CompilerParams(vmem_limit_bytes=56 * MIB),
+        cost_estimate=cost(0.1),
+        name="own_grads",
+    )(index, rows, vec, *parts)
+
+
+def moments_kernel(kinds, *refs):
+    n = len(kinds)
+    grads, masters, firsts, seconds = (refs[i * n : (i + 1) * n] for i in range(4))
+    new_firsts, new_seconds, updates = (refs[(4 + i) * n : (5 + i) * n] for i in range(3))
+    squares_ref = refs[7 * n]
+    lane = lax.broadcasted_iota(jnp.int32, squares_ref.shape, 1)
+    row = lax.broadcasted_iota(jnp.int32, squares_ref.shape, 0)
+    squares = jnp.zeros(squares_ref.shape, f32)
+    corr_one = 1.0 - beta_one**STEP
+    corr_two = 1.0 - beta_two**STEP
+    for i, (spot, amount) in enumerate(kinds):
+        grad = grads[i][...]
+        master = masters[i][...]
+        first = beta_one * firsts[i][...] + (1.0 - beta_one) * grad
+        second = beta_two * seconds[i][...] + (1.0 - beta_two) * grad * grad
+        update = first / corr_one / (jnp.sqrt(second / corr_two) + adam_eps) + decay_rate * master
+        new_firsts[i][...] = first
+        new_seconds[i][...] = second
+        updates[i][...] = update
+        for k in range(amount):
+            if amount == 1:
+                pair = (master, update)
+            elif len(master.shape) == 3:
+                pair = (master[k], update[k])
+            else:
+                pair = (master[k : k + 1], update[k : k + 1])
+            for r, v in enumerate(pair):
+                squares = jnp.where((lane == spot + k) & (row == r), whole_sum(v * v), squares)
+    squares_ref[...] = squares
+
+
+def moments(kinds, grads, masters, firsts, seconds):
+    shapes = [jax.ShapeDtypeStruct(m.shape, f32) for m in masters]
+    n = len(kinds)
+    out = pl.pallas_call(
+        functools.partial(moments_kernel, kinds),
+        out_shape=shapes * 3 + [jax.ShapeDtypeStruct((8, 128), f32)],
+        compiler_params=pltpu.CompilerParams(vmem_limit_bytes=56 * MIB),
+        cost_estimate=cost(0.1),
+        name="moments",
+    )(*grads, *masters, *firsts, *seconds)
+    return out[:n], out[n : 2 * n], out[2 * n : 3 * n], out[3 * n]
+
+
+def renew_kernel(kinds, came_ref, *refs):
+    n = len(kinds)
+    masters, updates, averages = (refs[i * n : (i + 1) * n] for i in range(3))
+    news, emas, copies = (refs[(3 + i) * n : (4 + i) * n] for i in range(3))
+    norm_ref, ratio_ref = refs[6 * n :]
+    total = jnp.sum(came_ref[...], axis=0)
+    norms = jnp.sqrt(total)
+    ratios = norms[0:1] / jnp.sqrt(total[1:2] + ratio_eps)
+    norm_ref[...] = norms[0:2, : norm_ref.shape[1]]
+    ratio_ref[...] = ratios[:, : ratio_ref.shape[1]]
+    lane = lax.broadcasted_iota(jnp.int32, ratios.shape, 1)
+    for i, (spot, amount) in enumerate(kinds):
+        for k in range(amount):
+            at = ... if amount == 1 else (k if len(masters[i].shape) == 3 else slice(k, k + 1))
+            ratio = jnp.sum(jnp.where(lane == spot + k, ratios, 0.0), axis=1, keepdims=True)
+            new = masters[i][at] - learn_rate * ratio * updates[i][at]
+            news[i][at] = new
+            emas[i][at] = ema_rate * averages[i][at] + (1.0 - ema_rate) * new
+            copies[i][at] = new.astype(bf16)
+
+
+def renew(kinds, came, masters, updates, averages):
+    shapes = [jax.ShapeDtypeStruct(m.shape, f32) for m in masters]
+    halves = [jax.ShapeDtypeStruct(m.shape, bf16) for m in masters]
+    n = len(kinds)
+    out = pl.pallas_call(
+        functools.partial(renew_kernel, kinds),
+        out_shape=shapes * 2 + halves + [jax.ShapeDtypeStruct((2, 15), f32), jax.ShapeDtypeStruct((1, 15), f32)],
+        compiler_params=pltpu.CompilerParams(vmem_limit_bytes=56 * MIB),
+        cost_estimate=cost(0.1),
+        name="renew",
+    )(came, *masters, *updates, *averages)
+    return out[:n], out[n : 2 * n], out[2 * n : 3 * n], out[3 * n], out[3 * n + 1].reshape(15)
 
 
 class Ring:
@@ -622,77 +876,20 @@
     return lax.all_gather(packed, ALL, axis=0, tiled=True)
 
 
-def scatter(ring, mine, theirs, vec=None):
+def after(value, *others):
+    return lax.optimization_barrier((value,) + others)[0]
+
+
+def scatter_far(mine, theirs):
     chips, part, width = mine.shape
+    full = jnp.stack([mine, theirs], axis=1).reshape(2 * chips * part, width)
+    return lax.psum_scatter(full, ALL, scatter_dimension=0, tiled=True).astype(f32)
+
+
+def share(ring, squares):
     if not ring.near:
-        full = jnp.stack([mine, theirs], axis=1).reshape(2 * chips * part, width)
-        total = lax.psum_scatter(full, ALL, scatter_dimension=0, tiled=True).astype(f32)
-        if vec is not None:
-            vec = lax.psum(vec, ALL)
-        return total, vec
-    came = ring.core(theirs)
-    if vec is not None:
-        vec = vec + ring.core(vec)
-
-    def packed(rows, vec):
-        rows = rows.astype(bf16).reshape(-1, width)
-        if vec is None:
-            return rows
-        return jnp.concatenate([rows, vec.reshape(-1, width).astype(bf16)], axis=0)
-
-    def added(rows, vec, parts):
-        cut = rows.shape[0] * rows.shape[1]
-        for p in parts:
-            rows = rows + p[:cut].reshape(rows.shape).astype(f32)
-            if vec is not None:
-                vec = vec + p[cut:].reshape(vec.shape).astype(f32)
-        return rows, vec
-
-    def near(xy):
-        at = slice(4 * xy, 4 * xy + 4)
-        return mine[at].astype(f32) + came[at].astype(f32)
-
-    parts = [ring.plane(packed(near(k), vec), k) for k in (1, 2, 3)]
-    rows, vec = added(near(0), vec, parts)
-    parts = [ring.line(packed(rows[k : k + 1], vec), k) for k in (1, 2, 3)]
-    rows, vec = added(rows[:1], vec, parts)
-    return rows[0], vec
-
-
-def sum_small(ring, values):
-    if not ring.near:
-        return lax.psum(values, ALL)
-    row = jnp.zeros((1, 128), f32).at[0, : values.shape[0]].set(values)
-    spread = jnp.broadcast_to(row[None], (ring.amount, 1, 128))
-    came = lax.all_to_all(spread, ALL, 0, 0)
-    return jnp.sum(came, axis=(0, 1))[: values.shape[0]]
-
-
-def tensor_squares(tensors):
-    return jnp.concatenate(
-        [
-            jnp.sum(tensors[0] * tensors[0], axis=(1, 2)),
-            jnp.sum(tensors[1] * tensors[1])[None],
-            jnp.sum(tensors[2] * tensors[2])[None],
-            jnp.sum(tensors[3] * tensors[3])[None],
-            jnp.sum(tensors[4] * tensors[4], axis=1),
-            jnp.sum(tensors[5] * tensors[5])[None],
-        ]
-    )
-
-
-def spread_ratios(ratios):
-    return (
-        ratios[0:3][:, None, None],
-        ratios[3],
-        ratios[4],
-        ratios[5],
-        ratios[6:14][:, None],
-        ratios[14],
-    )
-
-
-GROUPS = 2
+        return lax.psum(squares, ALL)[None]
+    return lax.all_to_all(jnp.broadcast_to(squares[None], (ring.amount,) + squares.shape), ALL, 0, 0)
 
 
 def on_device(
@@ -703,8 +900,6 @@
     *params,
 ):
     masters = params[0:6]
-    firsts_in = params[6:12]
-    seconds_in = params[12:18]
     averages = params[18:24]
     w_qkv, w_out, w_up, w_down, vecs, b_up = masters
     part, width = w_out.shape
@@ -717,62 +912,83 @@
     vec_part = jnp.concatenate([vecs, b_up.reshape(part, chunks).T], axis=0)
     raws, vec_rows = gather_first(ring, w_qkv, vec_part)
     vec_rows = jnp.concatenate([vec_rows, jnp.zeros((4, width), f32)], axis=0)
-    qkv, mixed, lse, full_qkv = attend_forward(where, bounds, tokens, vec_rows, raws)
-    layer_out, gmixed, gres, gvec, mine_a, theirs_a, mine_b, theirs_b = middle(
+    qkv, mixed, probs, share_rows, full_qkv = attend_forward(where, bounds, tokens, vec_rows, raws)
+    layer_out, gmixed, gres, gvec, down, mine, *theirs = middle(
         where, mixed, tokens, cotangent, vec_rows, packed
     )
-    grad_up, _ = scatter(ring, mine_a, theirs_a)
-    grad_rest, _ = scatter(ring, mine_b, theirs_b)
-    backs = [
-        attend_backward(where, bounds, tokens, qkv, mixed, gmixed, lse, g, GROUPS) for g in range(GROUPS)
-    ]
-    grad_input = input_grad(gres, full_qkv, [b[0] for b in backs])
-    own = width // GROUPS
-    gbias = jnp.concatenate([b[1][0].reshape(3, own) for b in backs], axis=1)
-    gvec = jnp.concatenate([gbias[0:1], gbias[2:3], gvec[2:12]], axis=0)
-    sums = []
-    for g, b in enumerate(backs):
-        total, back_vec = scatter(ring, b[2], b[3], gvec if g == GROUPS - 1 else None)
-        sums.append(total.reshape(part, 3, own))
-    grad_qkv = jnp.concatenate(sums, axis=2).transpose(1, 0, 2)
-    gvec = lax.dynamic_slice(back_vec, (0, ring.index() * part), (12, part))
+    down = lax.psum_scatter(down, ALL, scatter_dimension=0, tiled=True)
+    firsts_in = list(params[6:12])
+    seconds_in = list(params[12:18])
+
+    def join_vec(gvec, gbias):
+        gbias = gbias[0].reshape(3, width)
+        return jnp.concatenate([gbias[0:1], gbias[2:3], gvec[2:]], axis=0)
+
+    if ring.near:
+        came = [None] * 4
+        for k in (1, 2, 3, 0):
+            came[k] = ring.core(theirs[k])
+        sent = [
+            (mine[4 * k : 4 * k + 4].astype(f32) + came[k].astype(f32)).astype(bf16) for k in (1, 2, 3)
+        ]
+        parts = [ring.plane(v, k + 1) for k, v in enumerate(sent)]
+        gate = after(gmixed, came[0], *sent)
+        gqkv, gbias, mine_q, theirs_q = attend_backward(where, tokens, qkv, mixed, gate, probs, share_rows, 0, 1)
+        gvec = join_vec(gvec, after(gbias, *parts))
+        came_q = ring.core(after(theirs_q, *parts))
+        vec_came = ring.core(gvec)
+        sent_q = near(mine_q, came_q, gvec, vec_came)
+        parts_q = [ring.plane(v, k + 1) for k, v in enumerate(sent_q)]
+        parts[0] = after(parts[0], *sent_q)
+        rows, *sent = line(mine, came[0], parts)
+        grad_input = input_grad(after(gres, *sent, *sent_q), full_qkv, [gqkv])
+        sent[2] = after(sent[2], grad_input)
+        parts = [ring.line(v, k + 1) for k, v in enumerate(sent)]
+        parts_q[0] = after(parts_q[0], grad_input, parts[0], parts[1])
+        rows_q, *sent_q, vec_q = line(mine_q, came_q, parts_q, (gvec, vec_came))
+        parts_q = [ring.line(v, k + 1) for k, v in enumerate(sent_q)]
+        rows = after(rows, *sent_q)
+        down = after(down, *sent_q)
+        grad_rest = rows + parts[0].astype(f32) + parts[1].astype(f32) + parts[2].astype(f32)
+    else:
+        gqkv, gbias, mine_q, theirs_q = attend_backward(where, tokens, qkv, mixed, gmixed, probs, share_rows, 0, 1)
+        grad_input = input_grad(gres, full_qkv, [gqkv])
+        grad_rest = scatter_far(mine, jnp.concatenate(theirs, axis=0))
+        rows_q, vec_q, parts_q = scatter_far(mine_q, theirs_q), lax.psum(join_vec(gvec, gbias), ALL), []
     ff = chunks * width
-    reduced = (
-        grad_qkv,
-        grad_rest[:, ff:],
-        grad_up.reshape(part, chunks, width).transpose(0, 2, 1).reshape(part, ff),
-        grad_rest[:, :ff].reshape(part * chunks, width),
-        gvec[:8],
-        gvec[8:].T.reshape(part * chunks),
+    kinds = ((3, 1), (4, 1), (5, 1))
+    grad_down = jnp.concatenate([down.astype(f32), grad_rest[:, ff + width :]], axis=1)
+    grads = (
+        grad_rest[:, ff : ff + width],
+        grad_rest[:, :ff].reshape(part, chunks, width).transpose(0, 2, 1).reshape(part, ff),
+        grad_down.reshape(part * chunks, width),
     )
-    corr_one = 1.0 - beta_one**STEP
-    corr_two = 1.0 - beta_two**STEP
-    firsts = []
-    seconds = []
-    updates = []
-    for member in range(6):
-        first_new = beta_one * firsts_in[member] + (1.0 - beta_one) * reduced[member]
-        second_new = (
-            beta_two * seconds_in[member] + (1.0 - beta_two) * reduced[member] * reduced[member]
-        )
-        update = (
-            first_new / corr_one / (jnp.sqrt(second_new / corr_two) + adam_eps)
-            + decay_rate * masters[member]
-        )
-        firsts.append(first_new)
-        seconds.append(second_new)
-        updates.append(update)
-    squares = sum_small(ring, jnp.concatenate([tensor_squares(masters), tensor_squares(updates)]))
-    sq_weight, sq_update = squares[:15], squares[15:]
-    ratios = jnp.sqrt(sq_weight) / jnp.sqrt(sq_update + ratio_eps)
-    scales = spread_ratios(ratios)
-    renewed = [
-        masters[member] - learn_rate * scales[member] * updates[member] for member in range(6)
-    ]
-    emas = [ema_rate * averages[member] + (1.0 - ema_rate) * renewed[member] for member in range(6)]
-    norm_pairs = jnp.stack([jnp.sqrt(sq_weight), jnp.sqrt(sq_update)])
-    copies = [v.astype(bf16) for v in renewed]
-    return (layer_out, grad_input, *renewed, *firsts, *seconds, *emas, *copies, ratios, norm_pairs)
+    firsts_r, seconds_r, updates_r, squares_r = moments(
+        kinds, grads, masters[1:4], firsts_in[1:4], seconds_in[1:4]
+    )
+    if parts_q:
+        parts_q[0] = after(parts_q[0], squares_r)
+    index = ring.index().reshape(1).astype(jnp.int32)
+    grads = own_grads(index, rows_q, vec_q, parts_q, chunks)
+    flat = lambda v: v.reshape(1, -1)
+    pick = lambda v: (v[0], v[4], flat(v[5]))
+    others = ((0, 3), (6, 8), (14, 1))
+    firsts_q, seconds_q, updates_q, squares_q = moments(
+        others, grads, pick(masters), pick(firsts_in), pick(seconds_in)
+    )
+    came = share(ring, squares_r + squares_q)
+    news, emas, copies, norms, ratios = renew(
+        kinds + others,
+        came,
+        tuple(masters[1:4]) + pick(masters),
+        tuple(updates_r) + tuple(updates_q),
+        tuple(averages[1:4]) + pick(averages),
+    )
+    order = lambda v: (v[3], v[0], v[1], v[2], v[4], v[5].reshape(-1))
+    out = [layer_out, grad_input]
+    for found in (news, list(firsts_r) + list(firsts_q), list(seconds_r) + list(seconds_q), emas, copies):
+        out.extend(order(found))
+    return (*out, ratios, norms)
 
 
 def solution(mesh):

time: 475 us -> 379 us (0.80)
  waiting for transfers between devices: 128 us -> 71 us
  other arithmetic: 51.7 us -> 10.6 us
  Pallas kernels: 205 us -> 224 us
  starting transfers between devices: 44.4 us -> 27.7 us
  blocking collectives: 0 us -> 11.6 us
  local copies, waits for them, and re-layouts: 20.1 us -> 11.4 us
    ppermute x40 -> x29, waiting for transfers between devices: 116 us -> 55.3 us  [swap(): return lax.ppermute(value, ALL, [(i, i ^ bits) for i in range(self.amount)])]
    pallas_call x0 -> x7, Pallas kernels: none -> 20.7 us  [the longest x2 6 us: line(): pl.pallas_call(functools.partial(line_kernel, bool(vecs)), grid=(1,), in_...]
    convert_element_type x18 -> x2, other arithmetic: 18.5 us -> 4.25 us  [the longest x1 3.34 us: on_device(): (mine[4 * k:4 * k + 4].astype(f32) + came[k].astype(f32)).astype(bf16)]
    ppermute x40 -> x29, starting transfers between devices: 41.1 us -> 27.7 us  [swap(): return lax.ppermute(value, ALL, [(i, i ^ bits) for i in range(self.amount)])]
    all_to_all x0 -> x1, blocking collectives: none -> 11.6 us  [share(): lax.all_to_all(jnp.broadcast_to(squares[None], (ring.amount,) + squares.s...]
    another operation x9 -> x2, other arithmetic: 10.4 us -> 0.01 us
    reduce_scatter x0 -> x1, waiting for transfers between devices: none -> 8.5 us  [on_device(): down = lax.psum_scatter(down, ALL, scatter_dimension=0, tiled=True)]
    pallas_call x2 -> x1, Pallas kernels: 56.7 us -> 48.8 us  [attend_backward(): pl.pallas_call(attend_backward_kernel, grid_spec=pltpu.PrefetchScalarGrid...]
  transfers between devices with their start and end apart: 42 -> 31, of which waited for: 24 -> 14; matrix products, arithmetic and copies ran while one was open for 9% -> 3% of each run, Pallas kernels for 10% -> 29%
where the time goes in v2:
time: 379 us; the launch traced here: 371 us
  Pallas kernels  224 us (59%)
  waiting for transfers between devices  71 us (19%)
  starting transfers between devices  27.7 us (7%)
  between operations  15.1 us (4%)
  blocking collectives  11.6 us (3%)
  local copies, waits for them, and re-layouts  11.4 us (3%)
  other arithmetic  10.6 us (3%)
    pallas_call x1, Pallas kernels, middle(): pl.pallas_call(middle_kernel, grid_spec=pltpu.PrefetchScalarGridSpec(num_...  107 us
    ppermute x29, waiting for transfers between devices, swap(): return lax.ppermute(value, ALL, [(i, i ^ bits) for i in range(self.amount)])  55.3 us
    pallas_call x1, Pallas kernels, attend_backward(): pl.pallas_call(attend_backward_kernel, grid_spec=pltpu.PrefetchScalarGrid...  48.8 us
    pallas_call x1, Pallas kernels, attend_forward(): pl.pallas_call(attend_forward_kernel, grid_spec=pltpu.PrefetchScalarGridS...  34.5 us
    ppermute x29, starting transfers between devices, swap(): return lax.ppermute(value, ALL, [(i, i ^ bits) for i in range(self.amount)])  27.7 us
    pallas_call x1, Pallas kernels, input_grad(): pl.pallas_call(input_grad_kernel, grid=(tok // block,), in_specs=[pl.Bloc...  13.3 us
    all_to_all x1, blocking collectives, share(): lax.all_to_all(jnp.broadcast_to(squares[None], (ring.amount,) + squares.s...  11.6 us
    reduce_scatter x1, waiting for transfers between devices, on_device(): down = lax.psum_scatter(down, ALL, scatter_dimension=0, tiled=True)  8.5 us
  transfers between devices with their start and end apart: 31, of which 14 were waited for; matrix products, arithmetic and copies ran while one was open for 3% of the time, Pallas kernels for 29%

profile of v2, /device:TPU:0, one launch (start us, length us, event | category | flops | bytes accessed | tf_op | source)
XLA Modules:
  0.0 371.3 jit_solution(12841058137127437082)
XLA Ops:
  7.3 0.9 convert_element_type.60
  8.2 1.0 convert_element_type.58
  9.2 1.0 convert_element_type.59
  11.3 0.8 pad_maximum_fusion
  12.9 0.8 collective-permute-start
  13.7 0.9 collective-permute-done
  14.7 3.0 collective-permute-start.1
  17.7 2.2 collective-permute-start.3
  20.3 1.3 collective-permute-done.1
  21.6 18.0 %collective-permute-done.2 = bf16[176,384]{1,0:T(8,128)(2,1)S(1)} collective-permute-done((bf16[176,384]{1,0:T(8,128)(2,1)S(1)}, bf16[176,384]{1,0:T(8,128)(2,1)S(1)}, u32[]{:S(2)}, u32[]{:S(2)}) %collective-permute-start.2) | collective-permute-done | bytes 135200 | tf_op jit(solution)/shard_map/ppermute | solution.py:812
  39.7 2.2 collective-permute-start.6
  42.4 0.8 collective-permute-start.4
  43.4 16.8 %collective-permute-done.6.rest_3_ = bf16[608,384]{1,0:T(8,128)(2,1)S(1)} collective-permute-done((bf16[608,384]{1,0:T(8,128)(2,1)S(1)}, bf16[608,384]{1,0:T(8,128)(2,1)S(1)}, u32[]{:S(2)}, u32[]{:S(2)}) %collective-permute-start.6) | collective-permute-done | bytes 466976 | tf_op jit(solution)/shard_map/ppermute | solution.py:812
  60.2 4.4 %collective-permute-done.5.rest_2_ = bf16[608,384]{1,0:T(8,128)(2,1)S(1)} collective-permute-done((bf16[608,384]{1,0:T(8,128)(2,1)S(1)}, bf16[608,384]{1,0:T(8,128)(2,1)S(1)}, u32[]{:S(2)}, u32[]{:S(2)}) %collective-permute-start.5) | collective-permute-done | bytes 466976 | tf_op jit(solution)/shard_map/ppermute | solution.py:812
  64.7 4.9 %collective-permute-done.4.rest_1_ = bf16[608,384]{1,0:T(8,128)(2,1)S(1)} collective-permute-done((bf16[608,384]{1,0:T(8,128)(2,1)S(1)}, bf16[608,384]{1,0:T(8,128)(2,1)S(1)}, u32[]{:S(2)}, u32[]{:S(2)}) %collective-permute-start.4) | collective-permute-done | bytes 466976 | tf_op jit(solution)/shard_map/ppermute | solution.py:812
  73.1 34.5 %attend_forward.1 = (bf16[2048,2304]{1,0:T(8,128)(2,1)}, bf16[2048,768]{1,0:T(8,128)(2,1)}, bf16[4,6,512,1024]{3,2,1,0:T(8,128)(2,1)}, f32[4,6,2,512]{3,2,1,0:T(2,128)}, bf16[3,768,768]{2,1,0:T(8,128)(2,1)}) custom-call(s32[18]{0:T(128)} %stack.85.where_ref, s32[4,4]{1,0:T(4,128)} %pad_add_fusion.bounds_ref, bf16[2048,768]{1,0:T(8,128)(2,1)} %x_ref.5, ...), custom_call_target="tpu_custom_call" | custom-call | flops 32999999488 | bytes 30000000 | tf_op jit(solution)/shard_map/attend_forward/pallas_call | solution.py:163
  107.6 7.2 %all-gather.2.cloned.1.call-done.packed_ref = bf16[768,6912]{1,0:T(8,128)(2,1)} async-done(((bf16[24,6912]{1,0:T(8,128)(2,1)}), bf16[768,6912]{1,0:T(8,128)(2,1)}) %all-gather.2.cloned.1.call-update) | async-done | bytes 10616848 | tf_op jit(solution)/shard_map/all_gather | solution.py:876
  114.8 106.6 %middle.1 = (bf16[2048,768]{1,0:T(8,128)(2,1)}, bf16[2048,768]{1,0:T(8,128)(2,1)}, f32[2048,768]{1,0:T(8,128)}, f32[16,768]{1,0:T(8,128)}, bf16[768,2304]{1,0:T(...) custom-call(s32[18]{0:T(128)} %stack.85.where_ref, ...), custom_call_target="tpu_custom_call" | custom-call | flops 114400002048 | bytes 104000000 | tf_op jit(solution)/shard_map/middle/pallas_call | solution.py:373
  222.5 1.7 collective-permute-done.12
  224.2 2.5 collective-permute-done.14
  226.7 1.4 collective-permute-done.15
  228.1 3.3 add_convert_fusion
  231.5 1.3 collective-permute-start.17
  232.8 1.4 collective-permute-start.16
  235.0 48.8 %attend_backward.1 = (bf16[2048,2304]{1,0:T(8,128)(2,1)}, f32[8,2304]{1,0:T(8,128)}, bf16[16,24,2304]{2,1,0:T(8,128)(2,1)}, bf16[16,24,2304]{2,1,0:T(8,128)(2,1)}) custom-call(s32[18]{0:T(128)} %stack.85.where_ref, bf16[2048,768]{1,0:T(8,128)(2,1)} %x_ref.5, bf16[2048,2304]{1,0:T(8,128)(2,1)} %get-tuple-element.124.q_ref.k_ref.v_ref, ...), custom_call_target="tpu_custom_call" | custom-call | flops 62699999232 | bytes 57000000 | tf_op jit(solution)/shard_map/attend_backward/pallas_call | solution.py:510
  284.0 0.8 fusion.1
  285.4 2.4 collective-permute-done.19.vec_came_ref.refs_6_
  289.1 3.2 near.1
  292.3 1.3 collective-permute-start.20
  294.2 1.6 collective-permute-start.24
  295.8 3.5 line.2
  299.3 1.1 collective-permute-start.21
  300.4 1.0 collective-permute-start.22
  301.4 13.3 %input_grad.1 = bf16[2048,768]{1,0:T(8,128)(2,1)} custom-call(f32[2048,768]{1,0:T(8,128)} %get-tuple-element.144.gres_ref, bf16[3,768,768]{2,1,0:T(8,128)(2,1)} %get-tuple-element.145.w_ref, bf16[2048,2304]{1,0:T(8,128)(2,1)} %get-tuple-element.146.rest_0_), custom_call_target="tpu_custom_call" | custom-call | flops 110000000 | bytes 100000 | tf_op jit(solution)/shard_map/input_grad/pallas_call | solution.py:560
  314.7 2.4 collective-permute-start.25
  317.1 0.9 collective-permute-done.23.refs_3_
  319.5 2.5 line.3
  322.1 1.5 collective-permute-start.26
  323.5 2.3 collective-permute-start.27
  327.4 1.2 copy.74.refs_1_
  329.2 8.5 %reduce-scatter.2.cloned.1.call-done = bf16[24,2304]{1,0:T(8,128)(2,1)} async-done(((bf16[768,2304]{1,0:T(8,128)(2,1)}), bf16[24,2304]{1,0:T(8,128)(2,1)}) %reduce-scatter.2.cloned.1.call-update) | async-done | bytes 110608 | tf_op jit(solution)/shard_map/reduce_scatter | solution.py:919
  337.7 0.9 convert_element_type.73
  338.7 0.8 reshape.156.refs_2_
  339.5 3.3 moments.2
  343.6 2.4 own_grads.1
  346.0 2.4 moments.3
  349.1 11.6 %all_to_all.5.came_ref = f32[32,8,128]{2,1,0:T(8,128)} all-to-all(f32[32,8,128]{2,1,0:T(8,128)S(1)} %broadcast_in_dim.5), channel_id=1, replica_groups=mesh['gx'=8,'gy'=4] {'gx','gy'}, dimensions={0} | all-to-all | bytes 262144 | tf_op jit(solution)/shard_map/all_to_all | solution.py:892
  360.6 3.3 renew.1
  (139 shorter events, 16.3 us)
Async XLA Ops:
  7.2 4.9 %copy-start.20 = (f32[96]{0:T(128)S(1)}, f32[96]{0:T(128)}, u32[]{:S(2)}) copy-start(f32[96]{0:T(128)} %param.35) | copy-start | bytes 1156
  7.2 4.9 %copy-start.17 = (f32[8,24]{1,0:T(8,128)S(1)}, f32[8,24]{1,0:T(8,128)}, u32[]{:S(2)}) copy-start(f32[8,24]{1,0:T(8,128)} %refs_4_.5) | copy-start | bytes 2308
  7.2 5.6 %copy-start.2 = (f32[3,24,768]{2,1,0:T(8,128)S(1)}, f32[3,24,768]{2,1,0:T(8,128)}, u32[]{:S(2)}) copy-start(f32[3,24,768]{2,1,0:T(8,128)} %refs_3_.5) | copy-start | bytes 663556
  7.2 107.5 %all-gather.2.cloned.1.call-start = ((), (), s32[]{:S(2)}) async-start(), calls=%async_computation.2 | async-start | bytes 10948608 | tf_op jit(solution)/shard_map/all_gather | solution.py:876
  9.2 34.0 %copy-start.18 = (s32[4,4]{1,0:T(4,128)S(1)}, s32[4,4]{1,0:T(4,128)}, u32[]{:S(2)}) copy-start(s32[4,4]{1,0:T(4,128)} %param.28) | copy-start | bytes 196
  12.1 325.7 %reduce-scatter.2.cloned.1.call-start = ((), (), s32[]{:S(2)}) async-start(), calls=%async_computation.3 | async-start | bytes 3649536 | tf_op jit(solution)/shard_map/reduce_scatter | solution.py:919
  12.9 1.7 collective-permute-start
  14.7 6.9 %collective-permute-start.1 = (bf16[176,384]{1,0:T(8,128)(2,1)S(1)}, bf16[176,384]{1,0:T(8,128)(2,1)S(1)}, u32[]{:S(2)}, u32[]{:S(2)}) collective-permute-start(bf16[176,384]{1,0:T(8,128)(2,1)S(1)} %pad_maximum_fusion.2), channel_id=1, source_target_pairs={{0,8},{1,9},{2,10},{3,11},{4,12},{5,13},{6,14},{7,15},{8,0},{9,1},... | collective-permute-start | bytes 405512 | tf_op jit(solution)/shard_map/ppermute | solution.py:812
  17.7 21.9 %collective-permute-start.3 = (bf16[176,384]{1,0:T(8,128)(2,1)S(1)}, bf16[176,384]{1,0:T(8,128)(2,1)S(1)}, u32[]{:S(2)}, u32[]{:S(2)}) collective-permute-start(bf16[176,384]{1,0:T(8,128)(2,1)S(1)} %pad_maximum_fusion.2), channel_id=1, source_target_pairs={{0,24},{1,25},{2,26},{3,27},{4,28},{5,29},{6,30},{7,31},{8,16},{9,... | collective-permute-start | bytes 405512 | tf_op jit(solution)/shard_map/ppermute | solution.py:812
  19.9 19.7 %collective-permute-start.2 = (bf16[176,384]{1,0:T(8,128)(2,1)S(1)}, bf16[176,384]{1,0:T(8,128)(2,1)S(1)}, u32[]{:S(2)}, u32[]{:S(2)}) collective-permute-start(bf16[176,384]{1,0:T(8,128)(2,1)S(1)} %pad_maximum_fusion.2), channel_id=1, source_target_pairs={{0,16},{1,17},{2,18},{3,19},{4,20},{5,21},{6,22},{7,23},{8,24},{9,... | collective-permute-start | bytes 405512 | tf_op jit(solution)/shard_map/ppermute | solution.py:812
  39.7 32.5 %copy-start.19 = (bf16[608,384]{1,0:T(8,128)(2,1)}, bf16[608,384]{1,0:T(8,128)(2,1)S(1)}, u32[]{:S(2)}) copy-start(bf16[608,384]{1,0:T(8,128)(2,1)S(1)} %get-tuple-element.202.rest_0_) | copy-start | bytes 1400836
  39.7 20.5 %collective-permute-start.6 = (bf16[608,384]{1,0:T(8,128)(2,1)S(1)}, bf16[608,384]{1,0:T(8,128)(2,1)S(1)}, u32[]{:S(2)}, u32[]{:S(2)}) collective-permute-start(bf16[608,384]{1,0:T(8,128)(2,1)S(1)} %get-tuple-element.202.rest_0_), channel_id=1, source_target_pairs={{0,6},{1,7},{2,4},{3,5},{4,2},{5,3},{6,0},{7,1},{8,14},{9,15},{10,... | collective-permute-start | bytes 1400840 | tf_op jit(solution)/shard_map/ppermute | solution.py:812
  41.8 22.8 %collective-permute-start.5 = (bf16[608,384]{1,0:T(8,128)(2,1)S(1)}, bf16[608,384]{1,0:T(8,128)(2,1)S(1)}, u32[]{:S(2)}, u32[]{:S(2)}) collective-permute-start(bf16[608,384]{1,0:T(8,128)(2,1)S(1)} %get-tuple-element.202.rest_0_), channel_id=1, source_target_pairs={{0,4},{1,5},{2,6},{3,7},{4,0},{5,1},{6,2},{7,3},{8,12},{9,13},{10,... | collective-permute-start | bytes 1400840 | tf_op jit(solution)/shard_map/ppermute | solution.py:812
  42.4 27.2 %collective-permute-start.4 = (bf16[608,384]{1,0:T(8,128)(2,1)S(1)}, bf16[608,384]{1,0:T(8,128)(2,1)S(1)}, u32[]{:S(2)}, u32[]{:S(2)}) collective-permute-start(bf16[608,384]{1,0:T(8,128)(2,1)S(1)} %get-tuple-element.202.rest_0_), channel_id=1, source_target_pairs={{0,2},{1,3},{2,0},{3,1},{4,6},{5,7},{6,4},{7,5},{8,10},{9,11},{10,... | collective-permute-start | bytes 1400840 | tf_op jit(solution)/shard_map/ppermute | solution.py:812
  43.4 28.8 %collective-permute-start.7 = (bf16[608,384]{1,0:T(8,128)(2,1)S(1)}, bf16[608,384]{1,0:T(8,128)(2,1)S(1)}, u32[]{:S(2)}, u32[]{:S(2)}) collective-permute-start(bf16[608,384]{1,0:T(8,128)(2,1)S(1)} %get-tuple-element.202.rest_0_), channel_id=1, source_target_pairs={{0,1},{1,0},{2,3},{3,2},{4,5},{5,4},{6,7},{7,6},{8,9},{9,8},{10,11... | collective-permute-start | bytes 1400840 | tf_op jit(solution)/shard_map/ppermute | solution.py:812
  60.2 12.0 %copy-start.21 = (bf16[608,384]{1,0:T(8,128)(2,1)}, bf16[608,384]{1,0:T(8,128)(2,1)S(1)}, u32[]{:S(2)}) copy-start(bf16[608,384]{1,0:T(8,128)(2,1)S(1)} %collective-permute-done.6.rest_3_) | copy-start | bytes 1400836
  60.2 11.9 %collective-permute-start.10 = (bf16[608,384]{1,0:T(8,128)(2,1)S(1)}, bf16[608,384]{1,0:T(8,128)(2,1)S(1)}, u32[]{:S(2)}, u32[]{:S(2)}) collective-permute-start(bf16[608,384]{1,0:T(8,128)(2,1)S(1)} %collective-permute-done.6.rest_3_), channel_id=1, source_target_pairs={{0,1},{1,0},{2,3},{3,2},{4,5},{5,4},{6,7},{7,6},{8,9},{9,8},{10,11... | collective-permute-start | bytes 1400840 | tf_op jit(solution)/shard_map/ppermute | solution.py:812
  64.6 7.6 %copy-start.22 = (bf16[608,384]{1,0:T(8,128)(2,1)}, bf16[608,384]{1,0:T(8,128)(2,1)S(1)}, u32[]{:S(2)}) copy-start(bf16[608,384]{1,0:T(8,128)(2,1)S(1)} %collective-permute-done.5.rest_2_) | copy-start | bytes 1400836
  64.6 7.5 %collective-permute-start.9 = (bf16[608,384]{1,0:T(8,128)(2,1)S(1)}, bf16[608,384]{1,0:T(8,128)(2,1)}, u32[]{:S(2)}, u32[]{:S(2)}) collective-permute-start(bf16[608,384]{1,0:T(8,128)(2,1)S(1)} %collective-permute-done.5.rest_2_), channel_id=1, source_target_pairs={{0,1},{1,0},{2,3},{3,2},{4,5},{5,4},{6,7},{7,6},{8,9},{9,8},{10,11... | collective-permute-start | bytes 1400840 | tf_op jit(solution)/shard_map/ppermute | solution.py:812
  69.6 2.5 copy-start.23
  69.6 2.5 collective-permute-start.8
  221.3 6.8 %copy-start = (bf16[16,24,4608]{2,1,0:T(8,128)(2,1)S(1)}, bf16[16,24,4608]{2,1,0:T(8,128)(2,1)}, u32[]{:S(2)}) copy-start(bf16[16,24,4608]{2,1,0:T(8,128)(2,1)} %get-tuple-element.121.refs_0_) | copy-start | bytes 10616836
  221.4 2.8 collective-permute-start.12
  221.7 5.0 %collective-permute-start.14 = (bf16[4,24,4608]{2,1,0:T(8,128)(2,1)}, bf16[4,24,4608]{2,1,0:T(8,128)(2,1)}, u32[]{:S(2)}, u32[]{:S(2)}) collective-permute-start(bf16[4,24,4608]{2,1,0:T(8,128)(2,1)} %get-tuple-element.126), channel_id=1, source_target_pairs={{0,1},{1,0},{2,3},{3,2},{4,5},{5,4},{6,7},{7,6},{8,9},{9,8},{10,11... | collective-permute-start | bytes 2654216 | tf_op jit(solution)/shard_map/ppermute | solution.py:812
  221.9 6.2 %collective-permute-start.15 = (bf16[4,24,4608]{2,1,0:T(8,128)(2,1)}, bf16[4,24,4608]{2,1,0:T(8,128)(2,1)}, u32[]{:S(2)}, u32[]{:S(2)}) collective-permute-start(bf16[4,24,4608]{2,1,0:T(8,128)(2,1)} %get-tuple-element.127), channel_id=1, source_target_pairs={{0,1},{1,0},{2,3},{3,2},{4,5},{5,4},{6,7},{7,6},{8,9},{9,8},{10,11... | collective-permute-start | bytes 2654216 | tf_op jit(solution)/shard_map/ppermute | solution.py:812
  222.2 12.8 %collective-permute-start.11 = (bf16[4,24,4608]{2,1,0:T(8,128)(2,1)}, bf16[4,24,4608]{2,1,0:T(8,128)(2,1)S(1)}, u32[]{:S(2)}, u32[]{:S(2)}) collective-permute-start(bf16[4,24,4608]{2,1,0:T(8,128)(2,1)} %get-tuple-element.122), channel_id=1, source_target_pairs={{0,1},{1,0},{2,3},{3,2},{4,5},{5,4},{6,7},{7,6},{8,9},{9,8},{10,11... | collective-permute-start | bytes 2654216 | tf_op jit(solution)/shard_map/ppermute | solution.py:812
  231.5 52.4 %collective-permute-start.17 = (bf16[4,24,4608]{2,1,0:T(8,128)(2,1)}, bf16[4,24,4608]{2,1,0:T(8,128)(2,1)S(1)}, u32[]{:S(2)}, u32[]{:S(2)}) collective-permute-start(bf16[4,24,4608]{2,1,0:T(8,128)(2,1)} %get-tuple-element.204), channel_id=1, source_target_pairs={{0,6},{1,7},{2,4},{3,5},{4,2},{5,3},{6,0},{7,1},{8,14},{9,15},{10,... | collective-permute-start | bytes 2654216 | tf_op jit(solution)/shard_map/ppermute | solution.py:812
  232.8 51.1 %collective-permute-start.16 = (bf16[4,24,4608]{2,1,0:T(8,128)(2,1)S(1)}, bf16[4,24,4608]{2,1,0:T(8,128)(2,1)S(1)}, u32[]{:S(2)}, u32[]{:S(2)}) collective-permute-start(bf16[4,24,4608]{2,1,0:T(8,128)(2,1)S(1)} %get-tuple-element.205), channel_id=1, source_target_pairs={{0,4},{1,5},{2,6},{3,7},{4,0},{5,1},{6,2},{7,3},{8,12},{9,13},{10,... | collective-permute-start | bytes 2654216 | tf_op jit(solution)/shard_map/ppermute | solution.py:812
  234.2 49.7 %collective-permute-start.13 = (bf16[4,24,4608]{2,1,0:T(8,128)(2,1)S(1)}, bf16[4,24,4608]{2,1,0:T(8,128)(2,1)S(1)}, u32[]{:S(2)}, u32[]{:S(2)}) collective-permute-start(bf16[4,24,4608]{2,1,0:T(8,128)(2,1)S(1)} %get-tuple-element.206), channel_id=1, source_target_pairs={{0,2},{1,3},{2,0},{3,1},{4,6},{5,7},{6,4},{7,5},{8,10},{9,11},{10,... | collective-permute-start | bytes 2654216 | tf_op jit(solution)/shard_map/ppermute | solution.py:812
  235.0 48.9 %copy-start.3 = (bf16[4,24,4608]{2,1,0:T(8,128)(2,1)}, bf16[4,24,4608]{2,1,0:T(8,128)(2,1)S(1)}, u32[]{:S(2)}) copy-start(bf16[4,24,4608]{2,1,0:T(8,128)(2,1)S(1)} %collective-permute-done.11.refs_1_) | copy-start | bytes 2654212
  235.0 49.0 %copy-start.16 = (f32[16,768]{1,0:T(8,128)S(1)}, f32[16,768]{1,0:T(8,128)}, u32[]{:S(2)}) copy-start(f32[16,768]{1,0:T(8,128)} %get-tuple-element.136) | copy-start | bytes 147460
  283.9 12.0 %copy-start.4 = (bf16[4,24,4608]{2,1,0:T(8,128)(2,1)}, bf16[4,24,4608]{2,1,0:T(8,128)(2,1)S(1)}, u32[]{:S(2)}) copy-start(bf16[4,24,4608]{2,1,0:T(8,128)(2,1)S(1)} %collective-permute-done.17.refs_4_) | copy-start | bytes 2654212
  283.9 12.0 %copy-start.5 = (bf16[4,24,4608]{2,1,0:T(8,128)(2,1)}, bf16[4,24,4608]{2,1,0:T(8,128)(2,1)S(1)}, u32[]{:S(2)}) copy-start(bf16[4,24,4608]{2,1,0:T(8,128)(2,1)S(1)} %collective-permute-done.16.refs_3_) | copy-start | bytes 2654212
  283.9 11.9 %copy-start.6 = (bf16[4,24,4608]{2,1,0:T(8,128)(2,1)}, bf16[4,24,4608]{2,1,0:T(8,128)(2,1)S(1)}, u32[]{:S(2)}) copy-start(bf16[4,24,4608]{2,1,0:T(8,128)(2,1)S(1)} %collective-permute-done.13.refs_2_) | copy-start | bytes 2654212
  283.9 4.0 %collective-permute-start.18 = (bf16[16,24,2304]{2,1,0:T(8,128)(2,1)}, bf16[16,24,2304]{2,1,0:T(8,128)(2,1)S(1)}, u32[]{:S(2)}, u32[]{:S(2)}) collective-permute-start(bf16[16,24,2304]{2,1,0:T(8,128)(2,1)} %get-tuple-element.133), channel_id=1, source_target_pairs={{0,1},{1,0},{2,3},{3,2},{4,5},{5,4},{6,7},{7,6},{8,9},{9,8},{10,11... | collective-permute-start | bytes 5308424 | tf_op jit(solution)/shard_map/ppermute | solution.py:812
  284.9 3.0 copy-start.10
  284.9 2.8 collective-permute-start.19
  292.3 24.8 %collective-permute-start.20 = (bf16[4,24,2432]{2,1,0:T(8,128)(2,1)}, bf16[4,24,2432]{2,1,0:T(8,128)(2,1)S(1)}, u32[]{:S(2)}, u32[]{:S(2)}) collective-permute-start(bf16[4,24,2432]{2,1,0:T(8,128)(2,1)} %get-tuple-element.137), channel_id=1, source_target_pairs={{0,2},{1,3},{2,0},{3,1},{4,6},{5,7},{6,4},{7,5},{8,10},{9,11},{10,... | collective-permute-start | bytes 1400840 | tf_op jit(solution)/shard_map/ppermute | solution.py:812
  293.6 24.3 %collective-permute-start.23 = (bf16[4,24,2432]{2,1,0:T(8,128)(2,1)}, bf16[4,24,2432]{2,1,0:T(8,128)(2,1)S(1)}, u32[]{:S(2)}, u32[]{:S(2)}) collective-permute-start(bf16[4,24,2432]{2,1,0:T(8,128)(2,1)} %get-tuple-element.138), channel_id=1, source_target_pairs={{0,4},{1,5},{2,6},{3,7},{4,0},{5,1},{6,2},{7,3},{8,12},{9,13},{10,... | collective-permute-start | bytes 1400840 | tf_op jit(solution)/shard_map/ppermute | solution.py:812
  294.2 23.8 %collective-permute-start.24 = (bf16[4,24,2432]{2,1,0:T(8,128)(2,1)}, bf16[4,24,2432]{2,1,0:T(8,128)(2,1)S(1)}, u32[]{:S(2)}, u32[]{:S(2)}) collective-permute-start(bf16[4,24,2432]{2,1,0:T(8,128)(2,1)} %get-tuple-element.139), channel_id=1, source_target_pairs={{0,6},{1,7},{2,4},{3,5},{4,2},{5,3},{6,0},{7,1},{8,14},{9,15},{10,... | collective-permute-start | bytes 1400840 | tf_op jit(solution)/shard_map/ppermute | solution.py:812
  299.3 15.4 %collective-permute-start.21 = (bf16[24,4608]{1,0:T(8,128)(2,1)}, bf16[24,4608]{1,0:T(8,128)(2,1)S(1)}, u32[]{:S(2)}, u32[]{:S(2)}) collective-permute-start(bf16[24,4608]{1,0:T(8,128)(2,1)} %get-tuple-element.141), channel_id=1, source_target_pairs={{0,8},{1,9},{2,10},{3,11},{4,12},{5,13},{6,14},{7,15},{8,0},{9,1},... | collective-permute-start | bytes 663560 | tf_op jit(solution)/shard_map/ppermute | solution.py:812
  300.4 16.7 %collective-permute-start.22 = (bf16[24,4608]{1,0:T(8,128)(2,1)}, bf16[24,4608]{1,0:T(8,128)(2,1)S(1)}, u32[]{:S(2)}, u32[]{:S(2)}) collective-permute-start(bf16[24,4608]{1,0:T(8,128)(2,1)} %get-tuple-element.142), channel_id=1, source_target_pairs={{0,16},{1,17},{2,18},{3,19},{4,20},{5,21},{6,22},{7,23},{8,24},{9,... | collective-permute-start | bytes 663560 | tf_op jit(solution)/shard_map/ppermute | solution.py:812
  301.4 13.3 %copy-start.26 = (bf16[24,4608]{1,0:T(8,128)(2,1)S(1)}, bf16[24,4608]{1,0:T(8,128)(2,1)}, u32[]{:S(2)}) copy-start(bf16[24,4608]{1,0:T(8,128)(2,1)} %get-tuple-element.153) | copy-start | bytes 663556
  314.7 11.7 %copy-start.11 = (f32[24,4608]{1,0:T(8,128)S(1)}, f32[24,4608]{1,0:T(8,128)}, u32[]{:S(2)}) copy-start(f32[24,4608]{1,0:T(8,128)} %get-tuple-element.152) | copy-start | bytes 1327108
  314.7 11.7 %collective-permute-start.25 = (bf16[24,4608]{1,0:T(8,128)(2,1)S(1)}, bf16[24,4608]{1,0:T(8,128)(2,1)S(1)}, u32[]{:S(2)}, u32[]{:S(2)}) collective-permute-start(bf16[24,4608]{1,0:T(8,128)(2,1)S(1)} %copy-done.26), channel_id=1, source_target_pairs={{0,24},{1,25},{2,26},{3,27},{4,28},{5,29},{6,30},{7,31},{8,16},{9,... | collective-permute-start | bytes 663560 | tf_op jit(solution)/shard_map/ppermute | solution.py:812
  322.1 20.8 %collective-permute-start.26 = (bf16[24,2816]{1,0:T(8,128)(2,1)}, bf16[24,2816]{1,0:T(8,128)(2,1)S(1)}, u32[]{:S(2)}, u32[]{:S(2)}) collective-permute-start(bf16[24,2816]{1,0:T(8,128)(2,1)} %get-tuple-element.149), channel_id=1, source_target_pairs={{0,8},{1,9},{2,10},{3,11},{4,12},{5,13},{6,14},{7,15},{8,0},{9,1},... | collective-permute-start | bytes 405512 | tf_op jit(solution)/shard_map/ppermute | solution.py:812
  323.5 19.3 %collective-permute-start.27 = (bf16[24,2816]{1,0:T(8,128)(2,1)}, bf16[24,2816]{1,0:T(8,128)(2,1)S(1)}, u32[]{:S(2)}, u32[]{:S(2)}) collective-permute-start(bf16[24,2816]{1,0:T(8,128)(2,1)} %get-tuple-element.150), channel_id=1, source_target_pairs={{0,16},{1,17},{2,18},{3,19},{4,20},{5,21},{6,22},{7,23},{8,24},{9,... | collective-permute-start | bytes 405512 | tf_op jit(solution)/shard_map/ppermute | solution.py:812
  325.8 17.1 %collective-permute-start.28 = (bf16[24,2816]{1,0:T(8,128)(2,1)}, bf16[24,2816]{1,0:T(8,128)(2,1)S(1)}, u32[]{:S(2)}, u32[]{:S(2)}) collective-permute-start(bf16[24,2816]{1,0:T(8,128)(2,1)} %get-tuple-element.151), channel_id=1, source_target_pairs={{0,24},{1,25},{2,26},{3,27},{4,28},{5,29},{6,30},{7,31},{8,16},{9,... | collective-permute-start | bytes 405512 | tf_op jit(solution)/shard_map/ppermute | solution.py:812
  (10 other events, 8.1 us)
Sparse Core Ops, SparseCore 0:
  12.2 102.5 all-gather.1
  222.3 115.3 reduce-scatter.1

commit v3 on v2

--- a/solution.py
+++ b/solution.py
@@ -587,6 +587,38 @@
     return jnp.sum(jnp.sum(v, axis=0, keepdims=True), axis=1, keepdims=True)
 
 
+def pack_kernel(up_ref, down_ref, out_w_ref, packed_ref):
+    part, width = out_w_ref.shape
+    chunks = up_ref.shape[1] // width
+    span = 128 * chunks
+    place = lax.broadcasted_iota(jnp.int32, (span, span), 0)
+    to = lax.broadcasted_iota(jnp.int32, (span, span), 1)
+    pick = jnp.where((place % chunks) * 128 + place // chunks == to, 1.0, 0.0).astype(bf16)
+    for c in range(width // 128):
+        moved = dot(up_ref[:, c * span : (c + 1) * span].astype(bf16), pick).astype(bf16)
+        for j in range(chunks):
+            packed_ref[:, j * width + c * 128 : j * width + (c + 1) * 128] = moved[:, j * 128 : (j + 1) * 128]
+    down = down_ref[...].astype(bf16)
+    row = lax.broadcasted_iota(jnp.int32, (part, chunks * part), 0)
+    source = lax.broadcasted_iota(jnp.int32, (part, chunks * part), 1)
+    for j in range(chunks):
+        at = (chunks + j) * width
+        pick = jnp.where(source == chunks * row + j, 1.0, 0.0).astype(bf16)
+        packed_ref[:, at : at + width] = dot(pick, down).astype(bf16)
+    packed_ref[:, 2 * chunks * width :] = out_w_ref[...].astype(bf16)
+
+
+def pack(w_out, w_up, w_down):
+    part, width = w_out.shape
+    return pl.pallas_call(
+        pack_kernel,
+        out_shape=jax.ShapeDtypeStruct((part, 2 * w_up.shape[1] + width), bf16),
+        compiler_params=pltpu.CompilerParams(vmem_limit_bytes=56 * MIB),
+        cost_estimate=cost(2),
+        name="pack",
+    )(w_up, w_down, w_out)
+
+
 def spread_vec(vec, part):
     return jnp.concatenate([vec[:, c * 128 : (c + 1) * 128] for c in range(vec.shape[1] // 128)], axis=0)
 
@@ -868,11 +900,7 @@
 
 
 def gather_rest(w_out, w_up, w_down):
-    part, width = w_out.shape
-    chunks = w_up.shape[1] // width
-    up = w_up.astype(bf16).reshape(part, width, chunks).transpose(0, 2, 1).reshape(part, chunks * width)
-    down = w_down.astype(bf16).reshape(part, chunks * width)
-    packed = jnp.concatenate([up, down, w_out.astype(bf16)], axis=1)
+    packed = pack(w_out, w_up, w_down)
     return lax.all_gather(packed, ALL, axis=0, tiled=True)
 
 
@@ -928,9 +956,10 @@
         came = [None] * 4
         for k in (1, 2, 3, 0):
             came[k] = ring.core(theirs[k])
-        sent = [
-            (mine[4 * k : 4 * k + 4].astype(f32) + came[k].astype(f32)).astype(bf16) for k in (1, 2, 3)
-        ]
+        sent = []
+        for k in (1, 2, 3):
+            other = after(came[k], *sent)
+            sent.append((mine[4 * k : 4 * k + 4].astype(f32) + other.astype(f32)).astype(bf16))
         parts = [ring.plane(v, k + 1) for k, v in enumerate(sent)]
         gate = after(gmixed, came[0], *sent)
         gqkv, gbias, mine_q, theirs_q = attend_backward(where, tokens, qkv, mixed, gate, probs, share_rows, 0, 1)

time: 379 us -> 373 us (0.984)
  other arithmetic: 10.6 us -> 6.25 us
  transfers between devices with their start and end apart: 31 -> 31, of which waited for: 14 -> 12; matrix products, arithmetic and copies ran while one was open for 3% -> 3% of each run, Pallas kernels for 29% -> 30%
where the time goes in v3:
time: 373 us; the launch traced here: 366 us
  Pallas kernels  227 us (61%)
  waiting for transfers between devices  67.8 us (18%)
  starting transfers between devices  28.3 us (8%)
  between operations  15.1 us (4%)
  blocking collectives  11.4 us (3%)
  local copies, waits for them, and re-layouts  10.6 us (3%)
  other arithmetic  6.25 us (2%)
    pallas_call x1, Pallas kernels, middle(): pl.pallas_call(middle_kernel, grid_spec=pltpu.PrefetchScalarGridSpec(num_...  107 us
    ppermute x29, waiting for transfers between devices, swap(): return lax.ppermute(value, ALL, [(i, i ^ bits) for i in range(self.amount)])  52.5 us
    pallas_call x1, Pallas kernels, attend_backward(): pl.pallas_call(attend_backward_kernel, grid_spec=pltpu.PrefetchScalarGrid...  48.7 us
    pallas_call x1, Pallas kernels, attend_forward(): pl.pallas_call(attend_forward_kernel, grid_spec=pltpu.PrefetchScalarGridS...  34.5 us
    ppermute x29, starting transfers between devices, swap(): return lax.ppermute(value, ALL, [(i, i ^ bits) for i in range(self.amount)])  28.2 us
    pallas_call x1, Pallas kernels, input_grad(): pl.pallas_call(input_grad_kernel, grid=(tok // block,), in_specs=[pl.Bloc...  13.5 us
    all_to_all x1, blocking collectives, share(): lax.all_to_all(jnp.broadcast_to(squares[None], (ring.amount,) + squares.s...  11.4 us
    reduce_scatter x1, waiting for transfers between devices, on_device(): down = lax.psum_scatter(down, ALL, scatter_dimension=0, tiled=True)  7.76 us
  transfers between devices with their start and end apart: 31, of which 12 were waited for; matrix products, arithmetic and copies ran while one was open for 3% of the time, Pallas kernels for 30%

profile of v3, /device:TPU:0, one launch (start us, length us, event | category | flops | bytes accessed | tf_op | source)
XLA Modules:
  0.0 366.1 jit_solution(14197053403344686284)
XLA Ops:
  7.3 2.6 pack.1
  10.8 0.8 collective-permute-start
  11.6 0.9 collective-permute-done
  12.6 3.0 collective-permute-start.1
  15.6 2.2 collective-permute-start.3
  18.2 1.3 collective-permute-done.1
  19.5 17.9 %collective-permute-done.2 = bf16[176,384]{1,0:T(8,128)(2,1)S(1)} collective-permute-done((bf16[176,384]{1,0:T(8,128)(2,1)S(1)}, bf16[176,384]{1,0:T(8,128)(2,1)S(1)}, u32[]{:S(2)}, u32[]{:S(2)}) %collective-permute-start.2) | collective-permute-done | bytes 135200 | tf_op jit(solution)/shard_map/ppermute | solution.py:844
  37.6 2.0 collective-permute-start.6
  40.2 1.0 collective-permute-start.4
  41.3 16.5 %collective-permute-done.6.rest_3_ = bf16[608,384]{1,0:T(8,128)(2,1)S(1)} collective-permute-done((bf16[608,384]{1,0:T(8,128)(2,1)S(1)}, bf16[608,384]{1,0:T(8,128)(2,1)S(1)}, u32[]{:S(2)}, u32[]{:S(2)}) %collective-permute-start.6) | collective-permute-done | bytes 466976 | tf_op jit(solution)/shard_map/ppermute | solution.py:844
  57.8 4.9 %collective-permute-done.5.rest_2_ = bf16[608,384]{1,0:T(8,128)(2,1)S(1)} collective-permute-done((bf16[608,384]{1,0:T(8,128)(2,1)S(1)}, bf16[608,384]{1,0:T(8,128)(2,1)S(1)}, u32[]{:S(2)}, u32[]{:S(2)}) %collective-permute-start.5) | collective-permute-done | bytes 466976 | tf_op jit(solution)/shard_map/ppermute | solution.py:844
  62.8 4.7 %collective-permute-done.4.rest_1_ = bf16[608,384]{1,0:T(8,128)(2,1)S(1)} collective-permute-done((bf16[608,384]{1,0:T(8,128)(2,1)S(1)}, bf16[608,384]{1,0:T(8,128)(2,1)S(1)}, u32[]{:S(2)}, u32[]{:S(2)}) %collective-permute-start.4) | collective-permute-done | bytes 466976 | tf_op jit(solution)/shard_map/ppermute | solution.py:844
  71.1 34.5 %attend_forward.1 = (bf16[2048,2304]{1,0:T(8,128)(2,1)}, bf16[2048,768]{1,0:T(8,128)(2,1)}, bf16[4,6,512,1024]{3,2,1,0:T(8,128)(2,1)}, f32[4,6,2,512]{3,2,1,0:T(2,128)}, bf16[3,768,768]{2,1,0:T(8,128)(2,1)}) custom-call(s32[18]{0:T(128)} %stack.85.where_ref, s32[4,4]{1,0:T(4,128)} %pad_add_fusion.bounds_ref, bf16[2048,768]{1,0:T(8,128)(2,1)} %x_ref.5, ...), custom_call_target="tpu_custom_call" | custom-call | flops 32999999488 | bytes 30000000 | tf_op jit(solution)/shard_map/attend_forward/pallas_call | solution.py:163
  105.6 7.5 %all-gather.2.cloned.1.call-done.packed_ref = bf16[768,6912]{1,0:T(8,128)(2,1)} async-done(((bf16[24,6912]{1,0:T(8,128)(2,1)}), bf16[768,6912]{1,0:T(8,128)(2,1)}) %all-gather.2.cloned.1.call-update) | async-done | bytes 10616848 | tf_op jit(solution)/shard_map/all_gather | solution.py:904
  113.1 106.6 %middle.1 = (bf16[2048,768]{1,0:T(8,128)(2,1)}, bf16[2048,768]{1,0:T(8,128)(2,1)}, f32[2048,768]{1,0:T(8,128)}, f32[16,768]{1,0:T(8,128)}, bf16[768,2304]{1,0:T(...) custom-call(s32[18]{0:T(128)} %stack.85.where_ref, ...), custom_call_target="tpu_custom_call" | custom-call | flops 114400002048 | bytes 104000000 | tf_op jit(solution)/shard_map/middle/pallas_call | solution.py:373
  220.9 1.7 collective-permute-done.12
  222.5 1.4 add_convert_fusion.2
  223.9 1.5 collective-permute-start.13
  225.6 1.1 collective-permute-start.16
  226.7 1.1 add_convert_fusion
  227.8 1.4 collective-permute-start.17
  229.2 48.7 %attend_backward.1 = (bf16[2048,2304]{1,0:T(8,128)(2,1)}, f32[8,2304]{1,0:T(8,128)}, bf16[16,24,2304]{2,1,0:T(8,128)(2,1)}, bf16[16,24,2304]{2,1,0:T(8,128)(2,1)}) custom-call(s32[18]{0:T(128)} %stack.85.where_ref, bf16[2048,768]{1,0:T(8,128)(2,1)} %x_ref.5, bf16[2048,2304]{1,0:T(8,128)(2,1)} %get-tuple-element.126.q_ref.k_ref.v_ref, ...), custom_call_target="tpu_custom_call" | custom-call | flops 62699999232 | bytes 57000000 | tf_op jit(solution)/shard_map/attend_backward/pallas_call | solution.py:510
  278.1 0.8 fusion.1
  279.6 2.3 collective-permute-done.19.vec_came_ref.refs_6_
  282.5 0.8 copy-done.1
  283.3 3.3 near.1
  286.6 1.2 collective-permute-start.20
  287.8 0.9 collective-permute-start.23
  288.6 1.4 collective-permute-start.24
  290.1 3.5 line.2
  293.5 1.3 collective-permute-start.21
  294.8 1.3 collective-permute-start.22
  296.1 13.5 %input_grad.1 = bf16[2048,768]{1,0:T(8,128)(2,1)} custom-call(f32[2048,768]{1,0:T(8,128)} %get-tuple-element.148.gres_ref, bf16[3,768,768]{2,1,0:T(8,128)(2,1)} %get-tuple-element.149.w_ref, bf16[2048,2304]{1,0:T(8,128)(2,1)} %get-tuple-element.150.rest_0_), custom_call_target="tpu_custom_call" | custom-call | flops 110000000 | bytes 100000 | tf_op jit(solution)/shard_map/input_grad/pallas_call | solution.py:560
  309.6 1.9 collective-permute-start.25
  311.5 2.1 collective-permute-done.23.refs_3_
  315.2 2.5 line.3
  317.7 1.3 collective-permute-start.26
  319.0 0.9 collective-permute-start.27
  319.9 2.1 collective-permute-start.28
  323.1 1.2 copy.71.refs_1_
  324.9 7.8 %reduce-scatter.2.cloned.1.call-done = bf16[24,2304]{1,0:T(8,128)(2,1)} async-done(((bf16[768,2304]{1,0:T(8,128)(2,1)}), bf16[24,2304]{1,0:T(8,128)(2,1)}) %reduce-scatter.2.cloned.1.call-update) | async-done | bytes 110608 | tf_op jit(solution)/shard_map/reduce_scatter | solution.py:947
  332.7 0.9 convert_element_type.61
  333.6 0.8 reshape.144.refs_2_
  334.4 3.3 moments.2
  338.5 2.4 own_grads.1
  340.9 2.4 moments.3
  344.0 11.4 %all_to_all.5.came_ref = f32[32,8,128]{2,1,0:T(8,128)} all-to-all(f32[32,8,128]{2,1,0:T(8,128)S(1)} %broadcast_in_dim.5), channel_id=1, replica_groups=mesh['gx'=8,'gy'=4] {'gx','gy'}, dimensions={0} | all-to-all | bytes 262144 | tf_op jit(solution)/shard_map/all_to_all | solution.py:920
  355.4 3.3 renew.1
  (136 shorter events, 13.0 us)
Async XLA Ops:
  7.2 2.8 copy-start.20
  7.2 2.8 copy-start.17
  7.2 3.5 copy-start.2
  7.2 33.9 %copy-start.18 = (s32[4,4]{1,0:T(4,128)S(1)}, s32[4,4]{1,0:T(4,128)}, u32[]{:S(2)}) copy-start(s32[4,4]{1,0:T(4,128)} %param.28) | copy-start | bytes 196
  7.3 105.8 %all-gather.2.cloned.1.call-start = ((), (), s32[]{:S(2)}) async-start(), calls=%async_computation.2 | async-start | bytes 10948608 | tf_op jit(solution)/shard_map/all_gather | solution.py:904
  10.0 322.7 %reduce-scatter.2.cloned.1.call-start = ((), (), s32[]{:S(2)}) async-start(), calls=%async_computation.3 | async-start | bytes 3649536 | tf_op jit(solution)/shard_map/reduce_scatter | solution.py:947
  10.8 1.7 collective-permute-start
  12.6 6.9 %collective-permute-start.1 = (bf16[176,384]{1,0:T(8,128)(2,1)S(1)}, bf16[176,384]{1,0:T(8,128)(2,1)S(1)}, u32[]{:S(2)}, u32[]{:S(2)}) collective-permute-start(bf16[176,384]{1,0:T(8,128)(2,1)S(1)} %pad_maximum_fusion.1), channel_id=1, source_target_pairs={{0,8},{1,9},{2,10},{3,11},{4,12},{5,13},{6,14},{7,15},{8,0},{9,1},... | collective-permute-start | bytes 405512 | tf_op jit(solution)/shard_map/ppermute | solution.py:844
  15.6 21.9 %collective-permute-start.3 = (bf16[176,384]{1,0:T(8,128)(2,1)S(1)}, bf16[176,384]{1,0:T(8,128)(2,1)S(1)}, u32[]{:S(2)}, u32[]{:S(2)}) collective-permute-start(bf16[176,384]{1,0:T(8,128)(2,1)S(1)} %pad_maximum_fusion.1), channel_id=1, source_target_pairs={{0,24},{1,25},{2,26},{3,27},{4,28},{5,29},{6,30},{7,31},{8,16},{9,... | collective-permute-start | bytes 405512 | tf_op jit(solution)/shard_map/ppermute | solution.py:844
  17.8 19.7 %collective-permute-start.2 = (bf16[176,384]{1,0:T(8,128)(2,1)S(1)}, bf16[176,384]{1,0:T(8,128)(2,1)S(1)}, u32[]{:S(2)}, u32[]{:S(2)}) collective-permute-start(bf16[176,384]{1,0:T(8,128)(2,1)S(1)} %pad_maximum_fusion.1), channel_id=1, source_target_pairs={{0,16},{1,17},{2,18},{3,19},{4,20},{5,21},{6,22},{7,23},{8,24},{9,... | collective-permute-start | bytes 405512 | tf_op jit(solution)/shard_map/ppermute | solution.py:844
  37.6 32.5 %copy-start.19 = (bf16[608,384]{1,0:T(8,128)(2,1)}, bf16[608,384]{1,0:T(8,128)(2,1)S(1)}, u32[]{:S(2)}) copy-start(bf16[608,384]{1,0:T(8,128)(2,1)S(1)} %get-tuple-element.206.rest_0_) | copy-start | bytes 1400836
  37.6 20.2 %collective-permute-start.6 = (bf16[608,384]{1,0:T(8,128)(2,1)S(1)}, bf16[608,384]{1,0:T(8,128)(2,1)S(1)}, u32[]{:S(2)}, u32[]{:S(2)}) collective-permute-start(bf16[608,384]{1,0:T(8,128)(2,1)S(1)} %get-tuple-element.206.rest_0_), channel_id=1, source_target_pairs={{0,6},{1,7},{2,4},{3,5},{4,2},{5,3},{6,0},{7,1},{8,14},{9,15},{10,... | collective-permute-start | bytes 1400840 | tf_op jit(solution)/shard_map/ppermute | solution.py:844
  39.6 23.1 %collective-permute-start.5 = (bf16[608,384]{1,0:T(8,128)(2,1)S(1)}, bf16[608,384]{1,0:T(8,128)(2,1)S(1)}, u32[]{:S(2)}, u32[]{:S(2)}) collective-permute-start(bf16[608,384]{1,0:T(8,128)(2,1)S(1)} %get-tuple-element.206.rest_0_), channel_id=1, source_target_pairs={{0,4},{1,5},{2,6},{3,7},{4,0},{5,1},{6,2},{7,3},{8,12},{9,13},{10,... | collective-permute-start | bytes 1400840 | tf_op jit(solution)/shard_map/ppermute | solution.py:844
  40.2 27.4 %collective-permute-start.4 = (bf16[608,384]{1,0:T(8,128)(2,1)S(1)}, bf16[608,384]{1,0:T(8,128)(2,1)S(1)}, u32[]{:S(2)}, u32[]{:S(2)}) collective-permute-start(bf16[608,384]{1,0:T(8,128)(2,1)S(1)} %get-tuple-element.206.rest_0_), channel_id=1, source_target_pairs={{0,2},{1,3},{2,0},{3,1},{4,6},{5,7},{6,4},{7,5},{8,10},{9,11},{10,... | collective-permute-start | bytes 1400840 | tf_op jit(solution)/shard_map/ppermute | solution.py:844
  41.3 28.7 %collective-permute-start.7 = (bf16[608,384]{1,0:T(8,128)(2,1)S(1)}, bf16[608,384]{1,0:T(8,128)(2,1)S(1)}, u32[]{:S(2)}, u32[]{:S(2)}) collective-permute-start(bf16[608,384]{1,0:T(8,128)(2,1)S(1)} %get-tuple-element.206.rest_0_), channel_id=1, source_target_pairs={{0,1},{1,0},{2,3},{3,2},{4,5},{5,4},{6,7},{7,6},{8,9},{9,8},{10,11... | collective-permute-start | bytes 1400840 | tf_op jit(solution)/shard_map/ppermute | solution.py:844
  57.8 12.2 %copy-start.21 = (bf16[608,384]{1,0:T(8,128)(2,1)}, bf16[608,384]{1,0:T(8,128)(2,1)S(1)}, u32[]{:S(2)}) copy-start(bf16[608,384]{1,0:T(8,128)(2,1)S(1)} %collective-permute-done.6.rest_3_) | copy-start | bytes 1400836
  57.8 12.2 %collective-permute-start.10 = (bf16[608,384]{1,0:T(8,128)(2,1)S(1)}, bf16[608,384]{1,0:T(8,128)(2,1)S(1)}, u32[]{:S(2)}, u32[]{:S(2)}) collective-permute-start(bf16[608,384]{1,0:T(8,128)(2,1)S(1)} %collective-permute-done.6.rest_3_), channel_id=1, source_target_pairs={{0,1},{1,0},{2,3},{3,2},{4,5},{5,4},{6,7},{7,6},{8,9},{9,8},{10,11... | collective-permute-start | bytes 1400840 | tf_op jit(solution)/shard_map/ppermute | solution.py:844
  62.7 7.4 %copy-start.22 = (bf16[608,384]{1,0:T(8,128)(2,1)}, bf16[608,384]{1,0:T(8,128)(2,1)S(1)}, u32[]{:S(2)}) copy-start(bf16[608,384]{1,0:T(8,128)(2,1)S(1)} %collective-permute-done.5.rest_2_) | copy-start | bytes 1400836
  62.7 7.3 %collective-permute-start.9 = (bf16[608,384]{1,0:T(8,128)(2,1)S(1)}, bf16[608,384]{1,0:T(8,128)(2,1)S(1)}, u32[]{:S(2)}, u32[]{:S(2)}) collective-permute-start(bf16[608,384]{1,0:T(8,128)(2,1)S(1)} %collective-permute-done.5.rest_2_), channel_id=1, source_target_pairs={{0,1},{1,0},{2,3},{3,2},{4,5},{5,4},{6,7},{7,6},{8,9},{9,8},{10,11... | collective-permute-start | bytes 1400840 | tf_op jit(solution)/shard_map/ppermute | solution.py:844
  67.5 2.6 copy-start.23
  67.5 2.5 collective-permute-start.8
  219.7 2.8 copy-start
  219.7 2.8 collective-permute-start.12
  220.0 9.2 %collective-permute-start.11 = (bf16[4,24,4608]{2,1,0:T(8,128)(2,1)}, bf16[4,24,4608]{2,1,0:T(8,128)(2,1)S(1)}, u32[]{:S(2)}, u32[]{:S(2)}) collective-permute-start(bf16[4,24,4608]{2,1,0:T(8,128)(2,1)} %get-tuple-element.124), channel_id=1, source_target_pairs={{0,1},{1,0},{2,3},{3,2},{4,5},{5,4},{6,7},{7,6},{8,9},{9,8},{10,11... | collective-permute-start | bytes 2654216 | tf_op jit(solution)/shard_map/ppermute | solution.py:844
  220.4 5.0 %collective-permute-start.14 = (bf16[4,24,4608]{2,1,0:T(8,128)(2,1)}, bf16[4,24,4608]{2,1,0:T(8,128)(2,1)S(1)}, u32[]{:S(2)}, u32[]{:S(2)}) collective-permute-start(bf16[4,24,4608]{2,1,0:T(8,128)(2,1)} %get-tuple-element.128), channel_id=1, source_target_pairs={{0,1},{1,0},{2,3},{3,2},{4,5},{5,4},{6,7},{7,6},{8,9},{9,8},{10,11... | collective-permute-start | bytes 2654216 | tf_op jit(solution)/shard_map/ppermute | solution.py:844
  220.6 6.0 %collective-permute-start.15 = (bf16[4,24,4608]{2,1,0:T(8,128)(2,1)}, bf16[4,24,4608]{2,1,0:T(8,128)(2,1)S(1)}, u32[]{:S(2)}, u32[]{:S(2)}) collective-permute-start(bf16[4,24,4608]{2,1,0:T(8,128)(2,1)} %get-tuple-element.130), channel_id=1, source_target_pairs={{0,1},{1,0},{2,3},{3,2},{4,5},{5,4},{6,7},{7,6},{8,9},{9,8},{10,11... | collective-permute-start | bytes 2654216 | tf_op jit(solution)/shard_map/ppermute | solution.py:844
  223.9 54.1 %collective-permute-start.13 = (bf16[4,24,4608]{2,1,0:T(8,128)(2,1)S(1)}, bf16[4,24,4608]{2,1,0:T(8,128)(2,1)S(1)}, u32[]{:S(2)}, u32[]{:S(2)}) collective-permute-start(bf16[4,24,4608]{2,1,0:T(8,128)(2,1)S(1)} %add_convert_fusion.2), channel_id=1, source_target_pairs={{0,2},{1,3},{2,0},{3,1},{4,6},{5,7},{6,4},{7,5},{8,10},{9,11},{10,... | collective-permute-start | bytes 2654216 | tf_op jit(solution)/shard_map/ppermute | solution.py:844
  225.6 52.4 %collective-permute-start.16 = (bf16[4,24,4608]{2,1,0:T(8,128)(2,1)S(1)}, bf16[4,24,4608]{2,1,0:T(8,128)(2,1)S(1)}, u32[]{:S(2)}, u32[]{:S(2)}) collective-permute-start(bf16[4,24,4608]{2,1,0:T(8,128)(2,1)S(1)} %add_convert_fusion.1), channel_id=1, source_target_pairs={{0,4},{1,5},{2,6},{3,7},{4,0},{5,1},{6,2},{7,3},{8,12},{9,13},{10,... | collective-permute-start | bytes 2654216 | tf_op jit(solution)/shard_map/ppermute | solution.py:844
  227.8 50.2 %collective-permute-start.17 = (bf16[4,24,4608]{2,1,0:T(8,128)(2,1)}, bf16[4,24,4608]{2,1,0:T(8,128)(2,1)S(1)}, u32[]{:S(2)}, u32[]{:S(2)}) collective-permute-start(bf16[4,24,4608]{2,1,0:T(8,128)(2,1)} %add_convert_fusion), channel_id=1, source_target_pairs={{0,6},{1,7},{2,4},{3,5},{4,2},{5,3},{6,0},{7,1},{8,14},{9,15},{10,... | collective-permute-start | bytes 2654216 | tf_op jit(solution)/shard_map/ppermute | solution.py:844
  229.2 48.7 %copy-start.3 = (bf16[4,24,4608]{2,1,0:T(8,128)(2,1)}, bf16[4,24,4608]{2,1,0:T(8,128)(2,1)S(1)}, u32[]{:S(2)}) copy-start(bf16[4,24,4608]{2,1,0:T(8,128)(2,1)S(1)} %collective-permute-done.11.refs_1_) | copy-start | bytes 2654212
  229.2 48.9 %copy-start.16 = (f32[16,768]{1,0:T(8,128)S(1)}, f32[16,768]{1,0:T(8,128)}, u32[]{:S(2)}) copy-start(f32[16,768]{1,0:T(8,128)} %get-tuple-element.140) | copy-start | bytes 147460
  278.0 12.1 %copy-start.4 = (bf16[4,24,4608]{2,1,0:T(8,128)(2,1)}, bf16[4,24,4608]{2,1,0:T(8,128)(2,1)S(1)}, u32[]{:S(2)}) copy-start(bf16[4,24,4608]{2,1,0:T(8,128)(2,1)S(1)} %collective-permute-done.13.refs_2_) | copy-start | bytes 2654212
  278.0 12.1 %copy-start.5 = (bf16[4,24,4608]{2,1,0:T(8,128)(2,1)}, bf16[4,24,4608]{2,1,0:T(8,128)(2,1)S(1)}, u32[]{:S(2)}) copy-start(bf16[4,24,4608]{2,1,0:T(8,128)(2,1)S(1)} %collective-permute-done.16.refs_3_) | copy-start | bytes 2654212
  278.0 12.0 %copy-start.6 = (bf16[4,24,4608]{2,1,0:T(8,128)(2,1)}, bf16[4,24,4608]{2,1,0:T(8,128)(2,1)S(1)}, u32[]{:S(2)}) copy-start(bf16[4,24,4608]{2,1,0:T(8,128)(2,1)S(1)} %collective-permute-done.17.refs_4_) | copy-start | bytes 2654212
  278.0 4.0 %collective-permute-start.18 = (bf16[16,24,2304]{2,1,0:T(8,128)(2,1)}, bf16[16,24,2304]{2,1,0:T(8,128)(2,1)S(1)}, u32[]{:S(2)}, u32[]{:S(2)}) collective-permute-start(bf16[16,24,2304]{2,1,0:T(8,128)(2,1)} %get-tuple-element.137), channel_id=1, source_target_pairs={{0,1},{1,0},{2,3},{3,2},{4,5},{5,4},{6,7},{7,6},{8,9},{9,8},{10,11... | collective-permute-start | bytes 5308424 | tf_op jit(solution)/shard_map/ppermute | solution.py:844
  279.0 3.0 copy-start.10
  279.0 2.8 collective-permute-start.19
  286.6 24.9 %collective-permute-start.20 = (bf16[4,24,2432]{2,1,0:T(8,128)(2,1)}, bf16[4,24,2432]{2,1,0:T(8,128)(2,1)S(1)}, u32[]{:S(2)}, u32[]{:S(2)}) collective-permute-start(bf16[4,24,2432]{2,1,0:T(8,128)(2,1)} %get-tuple-element.141), channel_id=1, source_target_pairs={{0,2},{1,3},{2,0},{3,1},{4,6},{5,7},{6,4},{7,5},{8,10},{9,11},{10,... | collective-permute-start | bytes 1400840 | tf_op jit(solution)/shard_map/ppermute | solution.py:844
  287.8 25.8 %collective-permute-start.23 = (bf16[4,24,2432]{2,1,0:T(8,128)(2,1)}, bf16[4,24,2432]{2,1,0:T(8,128)(2,1)S(1)}, u32[]{:S(2)}, u32[]{:S(2)}) collective-permute-start(bf16[4,24,2432]{2,1,0:T(8,128)(2,1)} %get-tuple-element.142), channel_id=1, source_target_pairs={{0,4},{1,5},{2,6},{3,7},{4,0},{5,1},{6,2},{7,3},{8,12},{9,13},{10,... | collective-permute-start | bytes 1400840 | tf_op jit(solution)/shard_map/ppermute | solution.py:844
  288.6 25.0 %collective-permute-start.24 = (bf16[4,24,2432]{2,1,0:T(8,128)(2,1)}, bf16[4,24,2432]{2,1,0:T(8,128)(2,1)S(1)}, u32[]{:S(2)}, u32[]{:S(2)}) collective-permute-start(bf16[4,24,2432]{2,1,0:T(8,128)(2,1)} %get-tuple-element.143), channel_id=1, source_target_pairs={{0,6},{1,7},{2,4},{3,5},{4,2},{5,3},{6,0},{7,1},{8,14},{9,15},{10,... | collective-permute-start | bytes 1400840 | tf_op jit(solution)/shard_map/ppermute | solution.py:844
  293.5 16.0 %collective-permute-start.21 = (bf16[24,4608]{1,0:T(8,128)(2,1)}, bf16[24,4608]{1,0:T(8,128)(2,1)S(1)}, u32[]{:S(2)}, u32[]{:S(2)}) collective-permute-start(bf16[24,4608]{1,0:T(8,128)(2,1)} %get-tuple-element.145), channel_id=1, source_target_pairs={{0,8},{1,9},{2,10},{3,11},{4,12},{5,13},{6,14},{7,15},{8,0},{9,1},... | collective-permute-start | bytes 663560 | tf_op jit(solution)/shard_map/ppermute | solution.py:844
  294.8 16.7 %collective-permute-start.22 = (bf16[24,4608]{1,0:T(8,128)(2,1)}, bf16[24,4608]{1,0:T(8,128)(2,1)S(1)}, u32[]{:S(2)}, u32[]{:S(2)}) collective-permute-start(bf16[24,4608]{1,0:T(8,128)(2,1)} %get-tuple-element.146), channel_id=1, source_target_pairs={{0,16},{1,17},{2,18},{3,19},{4,20},{5,21},{6,22},{7,23},{8,24},{9,... | collective-permute-start | bytes 663560 | tf_op jit(solution)/shard_map/ppermute | solution.py:844
  296.1 13.5 %copy-start.27 = (bf16[24,4608]{1,0:T(8,128)(2,1)S(1)}, bf16[24,4608]{1,0:T(8,128)(2,1)}, u32[]{:S(2)}) copy-start(bf16[24,4608]{1,0:T(8,128)(2,1)} %get-tuple-element.157) | copy-start | bytes 663556
  309.6 12.5 %copy-start.11 = (f32[24,4608]{1,0:T(8,128)S(1)}, f32[24,4608]{1,0:T(8,128)}, u32[]{:S(2)}) copy-start(f32[24,4608]{1,0:T(8,128)} %get-tuple-element.156) | copy-start | bytes 1327108
  309.6 12.5 %collective-permute-start.25 = (bf16[24,4608]{1,0:T(8,128)(2,1)S(1)}, bf16[24,4608]{1,0:T(8,128)(2,1)S(1)}, u32[]{:S(2)}, u32[]{:S(2)}) collective-permute-start(bf16[24,4608]{1,0:T(8,128)(2,1)S(1)} %copy-done.27), channel_id=1, source_target_pairs={{0,24},{1,25},{2,26},{3,27},{4,28},{5,29},{6,30},{7,31},{8,16},{9,... | collective-permute-start | bytes 663560 | tf_op jit(solution)/shard_map/ppermute | solution.py:844
  317.7 20.1 %collective-permute-start.26 = (bf16[24,2816]{1,0:T(8,128)(2,1)}, bf16[24,2816]{1,0:T(8,128)(2,1)S(1)}, u32[]{:S(2)}, u32[]{:S(2)}) collective-permute-start(bf16[24,2816]{1,0:T(8,128)(2,1)} %get-tuple-element.153), channel_id=1, source_target_pairs={{0,8},{1,9},{2,10},{3,11},{4,12},{5,13},{6,14},{7,15},{8,0},{9,1},... | collective-permute-start | bytes 405512 | tf_op jit(solution)/shard_map/ppermute | solution.py:844
  319.0 18.8 %collective-permute-start.27 = (bf16[24,2816]{1,0:T(8,128)(2,1)}, bf16[24,2816]{1,0:T(8,128)(2,1)S(1)}, u32[]{:S(2)}, u32[]{:S(2)}) collective-permute-start(bf16[24,2816]{1,0:T(8,128)(2,1)} %get-tuple-element.154), channel_id=1, source_target_pairs={{0,16},{1,17},{2,18},{3,19},{4,20},{5,21},{6,22},{7,23},{8,24},{9,... | collective-permute-start | bytes 405512 | tf_op jit(solution)/shard_map/ppermute | solution.py:844
  319.9 17.8 %collective-permute-start.28 = (bf16[24,2816]{1,0:T(8,128)(2,1)}, bf16[24,2816]{1,0:T(8,128)(2,1)S(1)}, u32[]{:S(2)}, u32[]{:S(2)}) collective-permute-start(bf16[24,2816]{1,0:T(8,128)(2,1)} %get-tuple-element.155), channel_id=1, source_target_pairs={{0,24},{1,25},{2,26},{3,27},{4,28},{5,29},{6,30},{7,31},{8,16},{9,... | collective-permute-start | bytes 405512 | tf_op jit(solution)/shard_map/ppermute | solution.py:844
  (11 other events, 10.4 us)
Sparse Core Ops, SparseCore 0:
  11.0 102.0 all-gather.1
  220.2 112.4 reduce-scatter.1
